TPU v7x, 32 devices: a whole 2x2x4 slice. The times are simulated.
32 devices in a mesh: gx: 8 (over z, y), gy: 4 (over x, core).
Axes of the slice: x: 2, y: 2, z: 4, core: 2. Of those that a mesh axis runs over, the one named last changes fastest.
Arguments:
- wavefield: bfloat16 [2, 1, 3584, 1792], P(None, None, 'gx', 'gy'), may hold values from -6 to 6
- slowness: float32 [3584, 1792], P('gx', 'gy'), may hold values from -4 to 4
- frequencies: float32 [1], replicated, may hold values from 1 to 4
- propagator: bfloat16 [3, 1, 2, 256, 256], replicated, may hold values from -0.25 to 0.25
- window_velocity_group: int32 [16, 8], replicated, may hold values from 0 to 2
- reach_list: int32 [16, 8, 5], replicated, may hold values from -1 to 127, as said below
- coupling: float32 [16, 8, 5, 2], replicated, may hold values from -3 to 3
Outputs:
- migrated: bfloat16 [2, 1, 3584, 1792], P(None, None, 'gx', 'gy')
Inputs may be any that keep to these rules, and one draw needn't show every extreme that they name: `reach_list`: slot 0 of window (x, y) holds the window itself, x * 8 + y. Every other slot holds -1 or one of the eight windows that touch (x, y) along x, y or a diagonal; the entries of one list are distinct apart from -1. Some windows have one live entry, some have 5.
All inputs are finite; a program needn't handle non-finite values.
Results may differ from a plain program's by a relative error of at most 0.01.
Values may be sent and summed in bfloat16 or wider, within the bound.
No kernel may reach another device: no remote copies, remote signals or barrier semaphores. Data moves between devices by JAX's collectives and lax.ppermute only.
A program may use at most 64 MiB of HBM per device.

v0:
```python
import math

import jax
import jax.numpy as jnp
from jax import lax
from jax.sharding import PartitionSpec as P

OVER = 32


def extended(shard, sides, width):
    for axis, dim in sides:
        size, length = (lax.axis_size(axis), shard.shape[dim])
        up = [(i, (i + 1) % size) for i in range(size - 1)]
        down = [(j, i) for i, j in up]
        last = lax.slice_in_dim(shard, length - width, length, axis=dim)
        first = lax.slice_in_dim(shard, 0, width, axis=dim)
        before = lax.ppermute(last, axis, up)
        after = lax.ppermute(first, axis, down)
        shard = jnp.concatenate([before, shard, after], axis=dim)
    return shard


def cosine_table(length):
    points = jnp.arange(length, dtype=jnp.float32) + 0.5
    return jnp.sqrt(2.0 / length) * jnp.cos(math.pi / length * points[:, None] * points[None, :])


def bell_curve(length, margin):
    points = jnp.arange(length, dtype=jnp.float32)
    rising = jnp.sin(0.5 * math.pi * (points + 0.5) / margin)
    falling = jnp.cos(0.5 * math.pi * (points - (length - margin) + 0.5) / margin)
    return jnp.where(points < margin, rising, jnp.where(points >= length - margin, falling, 1.0))


def apply_complex(spec, matrices, block):
    matrix_real = jnp.take(matrices, 0, axis=3)
    matrix_imag = jnp.take(matrices, 1, axis=3)

    def contract(left, right):
        return jnp.einsum(spec, left, right, preferred_element_type=jnp.float32)

    real_part = contract(matrix_real, block[0]) - contract(matrix_imag, block[1])
    imag_part = contract(matrix_real, block[1]) + contract(matrix_imag, block[0])
    return jnp.stack([real_part, imag_part]).astype(jnp.bfloat16)


def rebuild(propagated, cosines, bell_values, stride, length):
    second = jnp.einsum(
        "pfxkyl,lb->pfxkyb", propagated, cosines, preferred_element_type=jnp.float32
    ).astype(jnp.bfloat16)
    pieces = jnp.einsum("pfxkyb,ka->pfxayb", second, cosines, preferred_element_type=jnp.float32)
    pieces = pieces * bell_values[:, None, None] * bell_values
    count_x = propagated.shape[2]
    count_y = propagated.shape[4]
    margin = length - stride
    canvas = jnp.zeros(
        pieces.shape[:2] + (count_x * stride + margin, count_y * stride + margin), jnp.float32
    )
    for tile_x in range(count_x):
        for tile_y in range(count_y):
            canvas = canvas.at[
                :,
                :,
                tile_x * stride : tile_x * stride + length,
                tile_y * stride : tile_y * stride + length,
            ].add(pieces[:, :, tile_x, :, tile_y, :])
    return canvas


def per_device(
    wavefield, slowness, frequencies, propagator, window_velocity_group, reach_list, coupling
):
    length = propagator.shape[-1]
    stride = length - OVER
    half_rim = OVER // 2
    tile_rows = wavefield.shape[2]
    tile_cols = wavefield.shape[3]
    count_x = tile_rows // stride
    count_y = tile_cols // stride
    total_x = window_velocity_group.shape[0]
    total_y = window_velocity_group.shape[1]
    slot_count = reach_list.shape[2]
    cosines = cosine_table(length).astype(jnp.bfloat16)
    bell_values = bell_curve(length, OVER)
    padded = extended(wavefield, (("gx", 2), ("gy", 3)), half_rim)
    row_strips = jnp.stack(
        [padded[:, :, tile_x * stride : tile_x * stride + length, :] for tile_x in range(count_x)],
        2,
    )
    patches = jnp.stack(
        [row_strips[..., tile_y * stride : tile_y * stride + length] for tile_y in range(count_y)],
        4,
    )
    tapered = (patches.astype(jnp.float32) * bell_values[:, None, None] * bell_values).astype(
        jnp.bfloat16
    )
    first_pass = jnp.einsum(
        "pfxayb,lb->pfxayl", tapered, cosines, preferred_element_type=jnp.float32
    ).astype(jnp.bfloat16)
    coefficients = jnp.einsum(
        "pfxayl,ka->pfxkyl", first_pass, cosines, preferred_element_type=jnp.float32
    ).astype(jnp.bfloat16)
    base_x = lax.axis_index("gx") * count_x
    starting_y = lax.axis_index("gy") * count_y
    own_x = base_x + jnp.arange(count_x)
    own_y = starting_y + jnp.arange(count_y)
    own_props = propagator[window_velocity_group[own_x[:, None], own_y[None, :]]]
    arrived = extended(coefficients, (("gx", 2), ("gy", 4)), 1)
    near_x = jnp.clip(base_x - 1 + jnp.arange(count_x + 2), 0, total_x - 1)
    near_y = jnp.clip(starting_y - 1 + jnp.arange(count_y + 2), 0, total_y - 1)
    near_props = propagator[window_velocity_group[near_x[:, None], near_y[None, :]]]
    swept_coefs = apply_complex("xyfmk,fxkyl->fxmyl", near_props, arrived)
    own_reach = reach_list[own_x[:, None], own_y[None, :]]
    self_coupling = coupling[own_x[:, None], own_y[None, :]]
    is_live = own_reach >= 0
    safe_index = jnp.where(is_live, own_reach, 0)
    self_x = jnp.arange(count_x)[:, None, None] + 1
    self_y = jnp.arange(count_y)[None, :, None] + 1
    near_row = jnp.where(is_live, safe_index // total_y - base_x + 1, self_x)
    near_col = jnp.where(is_live, safe_index % total_y - starting_y + 1, self_y)
    weight_real = jnp.where(is_live, self_coupling[..., 0], 0.0)
    weight_imag = jnp.where(is_live, self_coupling[..., 1], 0.0)
    mixed_rows = []
    for tile_x in range(count_x):
        mixed_cols = []
        for tile_y in range(count_y):
            acc_real = jnp.zeros(swept_coefs.shape[1:2] + (length, length), jnp.float32)
            acc_imag = jnp.zeros(swept_coefs.shape[1:2] + (length, length), jnp.float32)
            for slot_index in range(slot_count):
                piece = swept_coefs[
                    :,
                    :,
                    near_row[tile_x, tile_y, slot_index],
                    :,
                    near_col[tile_x, tile_y, slot_index],
                    :,
                ].astype(jnp.float32)
                w_real = weight_real[tile_x, tile_y, slot_index]
                w_imag = weight_imag[tile_x, tile_y, slot_index]
                acc_real = acc_real + w_real * piece[0] - w_imag * piece[1]
                acc_imag = acc_imag + w_real * piece[1] + w_imag * piece[0]
            mixed_cols.append(jnp.stack([acc_real, acc_imag]).astype(jnp.bfloat16))
        mixed_rows.append(jnp.stack(mixed_cols, 3))
    mixed_coefs = jnp.stack(mixed_rows, 2)
    propagated = apply_complex("xyfnl,fxkyl->fxkyn", own_props, mixed_coefs)
    canvas = rebuild(propagated, cosines, bell_values, stride, length)
    send_rows = jnp.concatenate([canvas[:, :, :half_rim], canvas[:, :, -half_rim:]], 2)
    got_rows = extended(send_rows.astype(jnp.bfloat16), (("gx", 2),), half_rim).astype(
        send_rows.dtype
    )
    inner = canvas[:, :, half_rim : half_rim + tile_rows]
    inner = inner.at[:, :, :half_rim].add(got_rows[:, :, :half_rim])
    inner = inner.at[:, :, tile_rows - half_rim :].add(got_rows[:, :, 3 * half_rim :])
    send_cols = jnp.swapaxes(
        jnp.concatenate([inner[..., :half_rim], inner[..., -half_rim:]], 3), 2, 3
    )
    got_cols = jnp.swapaxes(
        extended(send_cols.astype(jnp.bfloat16), (("gy", 2),), half_rim).astype(send_cols.dtype),
        2,
        3,
    )
    summed = inner[..., half_rim : half_rim + tile_cols]
    summed = summed.at[..., :half_rim].add(got_cols[..., :half_rim])
    summed = summed.at[..., tile_cols - half_rim :].add(got_cols[..., 3 * half_rim :])
    phases = frequencies[:, None, None] * slowness
    cos_phase = jnp.cos(phases)
    sin_phase = jnp.sin(phases)
    out_real = summed[0] * cos_phase - summed[1] * sin_phase
    out_imag = summed[0] * sin_phase + summed[1] * cos_phase
    return jnp.stack([out_real, out_imag]).astype(jnp.bfloat16)


def solution(mesh):
    return jax.shard_map(
        per_device,
        mesh=mesh,
        in_specs=(P(None, None, "gx", "gy"), P("gx", "gy"), P(), P(), P(), P(), P()),
        out_specs=P(None, None, "gx", "gy"),
        check_vma=False,
    )
```

profile of v0, /device:TPU:9, one launch (start us, length us, event | category | flops | bytes accessed | tf_op | source)
XLA Modules:
  0.0 260.3 jit_solution(929120129716306765)
XLA Ops:
  0.0 0.9 fusion.130
  0.9 3.1 %collective-permute-start = (bf16[2,1,16,448]{3,2,1,0:T(8,128)(2,1)S(1)}, bf16[2,1,16,448]{3,2,1,0:T(8,128)(2,1)S(1)}, u32[]{:S(2)}, u32[]{:S(2)}) collective-permute-start(bf16[2,1,16,448]{3,2,1,0:T(8,128)(2,1)S(1)} %get-tuple-element.184), channel_id=1, source_target_pairs={{0,4},{4,8},{8,12},{12,16},{16,20},{20,24},{24,28},{1,5},{5,9},{9,... | collective-permute-start | bytes 86024 | tf_op jit(solution)/shard_map/ppermute | solution.py:18
  4.0 3.0 %collective-permute-start.1 = (bf16[2,1,16,448]{3,2,1,0:T(8,128)(2,1)S(1)}, bf16[2,1,16,448]{3,2,1,0:T(8,128)(2,1)S(1)}, u32[]{:S(2)}, u32[]{:S(2)}) collective-permute-start(bf16[2,1,16,448]{3,2,1,0:T(8,128)(2,1)S(1)} %get-tuple-element.183), channel_id=1, source_target_pairs={{4,0},{8,4},{12,8},{16,12},{20,16},{24,20},{28,24},{5,1},{9,5},{13... | collective-permute-start | bytes 86024 | tf_op jit(solution)/shard_map/ppermute | solution.py:19
  10.3 1.2 constant_dynamic-update-slice_fusion.1
  11.7 4.2 %collective-permute-start.2 = (bf16[2,1,480,16]{3,2,1,0:T(8,128)(2,1)S(1)}, bf16[2,1,480,16]{3,2,1,0:T(8,128)(2,1)S(1)}, u32[]{:S(2)}, u32[]{:S(2)}) collective-permute-start(bf16[2,1,480,16]{3,2,1,0:T(8,128)(2,1)S(1)} %get-tuple-element.179), channel_id=1, source_target_pairs={{0,1},{1,2},{2,3},{4,5},{5,6},{6,7},{8,9},{9,10},{10,11},{12,13},{... | collective-permute-start | bytes 92168 | tf_op jit(solution)/shard_map/ppermute | solution.py:18
  16.0 1.9 collective-permute-start.3
  71.5 2.6 %fusion.6 = bf16[2,1,2,256,2,256]{5,3,4,2,0,1:T(8,128)(2,1)S(1)} fusion(f32[256]{0:T(256)S(1)} %get-tuple-element.271, f32[256]{0:T(256)S(1)} %get-tuple-element.272, bf16[2,2,256,1,256]{4,2,0,1,3:T(8,128)(2,1)S(1)} %get-tuple-element.178, bf16[2,2,256,1,256]{4,2,0,1,3:T(8,128)(2,1)S(1)} %get-tuple-element.177, f32[256]{0:T(256)S(1)} %fusion.102), kind=kOutput, calls=%fused_computation.65 | convolution fusion | flops 540934144 | bytes 2100224 | tf_op jit(solution)/shard_map/pfxayl,ka->pfxkyl/dot_general | solution.py:101
  74.2 0.9 fusion.127
  75.0 2.2 collective-permute-start.4
  77.3 3.9 %collective-permute-start.5 = (bf16[2,1,1,256,2,256]{5,3,4,2,0,1:T(8,128)(2,1)S(1)}, bf16[2,1,1,256,2,256]{5,3,4,2,0,1:T(8,128)(2,1)S(1)}, u32[]{:S(2)}, u32[]{:S(2)}) collective-permute-start(bf16[2,1,1,256,2,256]{5,3,4,2,0,1:T(8,128)(2,1)S(1)} %get-tuple-element.176), channel_id=1, source_target_pairs={{4,0},{8,4},{12,8},{16,12},{20,16},{24,20},{28,24},{5,1},{9,5},{13... | collective-permute-start | bytes 1572872 | tf_op jit(solution)/shard_map/ppermute | solution.py:19
  81.3 2.8 %gather_fusion.3 = bf16[16,2,256,256]{3,2,1,0:T(8,128)(2,1)} fusion(bf16[3,2,256,256]{3,2,1,0:T(8,128)(2,1)S(1)} %bitcast.279, s32[1024]{0:T(1024)S(1)} %pad_clamp_fusion.1), kind=kCustom, calls=%fused_computation.3 | custom fusion | bytes 8388672 | tf_op jit(solution)/shard_map/gather | solution.py:112
  84.2 4.6 %copy.80 = bf16[16,2,256,256]{3,2,0,1:T(8,128)(2,1)} copy(bf16[16,2,256,256]{3,2,1,0:T(8,128)(2,1)} %gather_fusion.3) | data formatting | bytes 8388608 | tf_op jit(solution)/shard_map/gather | solution.py:112
  88.8 1.0 copy.75
  90.3 8.4 %collective-permute-done.4 = bf16[2,1,1,256,2,256]{5,3,4,2,0,1:T(8,128)(2,1)S(1)} collective-permute-done((bf16[2,1,1,256,2,256]{5,3,4,2,0,1:T(8,128)(2,1)}, bf16[2,1,1,256,2,256]{5,3,4,2,0,1:T(8,128)(2,1)S(1)}, u32[]{:S(2)}, u32[]{:S(2)}) %collective-permute-start.4) | collective-permute-done | bytes 524320 | tf_op jit(solution)/shard_map/ppermute | solution.py:18
  98.7 2.6 collective-permute-done.5
  102.0 1.5 fusion.125
  103.5 4.3 %collective-permute-start.6 = (bf16[2,1,4,256,1,256]{5,3,4,2,0,1:T(8,128)(2,1)}, bf16[2,1,4,256,1,256]{5,3,4,2,0,1:T(8,128)(2,1)}, u32[]{:S(2)}, u32[]{:S(2)}) collective-permute-start(bf16[2,1,4,256,1,256]{5,3,4,2,0,1:T(8,128)(2,1)} %get-tuple-element.171), channel_id=1, source_target_pairs={{0,1},{1,2},{2,3},{4,5},{5,6},{6,7},{8,9},{9,10},{10,11},{12,13},{... | collective-permute-start | bytes 3145736 | tf_op jit(solution)/shard_map/ppermute | solution.py:18
  107.8 1.9 collective-permute-start.7
  111.1 1.6 gather_fusion.5
  112.7 1.4 copy.87
  141.5 2.2 pad_maximum_fusion
  146.7 0.9 fusion.5
  147.9 6.3 %fusion.89 = bf16[1,1,256,1,256]{2,4,3,0,1:T(8,128)(2,1)S(1)} fusion(f32[2,1,1,256,1,256]{3,5,4,2,1,0:T(8,128)S(1)} %get-tuple-element.155, f32[]{:T(128)} %bitcast.51, f32[]{:T(128)} %bitcast.48, f32[2,1,1,256,1,256]{3,5,4,2,1,0:T(8,128)S(1)} %get-tuple-element.154, f32[]{:T(128)} %bitcast.47, f32[]{:T(128)} %bitcast.44, ...), kind=kLoop, calls=%fused_computation.175 | loop fusion | flops 1310720 | bytes 2752552 | tf_op jit(solution)/shard_map/stack | solution.py:143
  154.1 6.3 %fusion.90 = bf16[1,1,256,1,256]{2,4,3,0,1:T(8,128)(2,1)S(1)} fusion(f32[2,1,1,256,1,256]{3,5,4,2,1,0:T(8,128)S(1)} %get-tuple-element.155, f32[]{:T(128)} %bitcast.51, f32[]{:T(128)} %bitcast.48, f32[2,1,1,256,1,256]{3,5,4,2,1,0:T(8,128)S(1)} %get-tuple-element.154, f32[]{:T(128)} %bitcast.47, f32[]{:T(128)} %bitcast.44, ...), kind=kLoop, calls=%fused_computation.176 | loop fusion | flops 1310720 | bytes 2752552 | tf_op jit(solution)/shard_map/stack | solution.py:143
  160.5 6.4 %fusion.91 = bf16[1,1,256,1,256]{2,4,3,0,1:T(8,128)(2,1)S(1)} fusion(f32[2,1,1,256,1,256]{3,5,4,2,1,0:T(8,128)S(1)} %get-tuple-element.160, f32[]{:T(128)} %bitcast.74, f32[]{:T(128)} %bitcast.71, f32[2,1,1,256,1,256]{3,5,4,2,1,0:T(8,128)S(1)} %get-tuple-element.159, f32[]{:T(128)} %bitcast.70, f32[]{:T(128)} %bitcast.67, ...), kind=kLoop, calls=%fused_computation.177 | loop fusion | flops 1310720 | bytes 2752552 | tf_op jit(solution)/shard_map/stack | solution.py:143
  167.0 6.4 %fusion.92 = bf16[1,1,256,1,256]{2,4,3,0,1:T(8,128)(2,1)S(1)} fusion(f32[2,1,1,256,1,256]{3,5,4,2,1,0:T(8,128)S(1)} %get-tuple-element.160, f32[]{:T(128)} %bitcast.74, f32[]{:T(128)} %bitcast.71, f32[2,1,1,256,1,256]{3,5,4,2,1,0:T(8,128)S(1)} %get-tuple-element.159, f32[]{:T(128)} %bitcast.70, f32[]{:T(128)} %bitcast.67, ...), kind=kLoop, calls=%fused_computation.178 | loop fusion | flops 1310720 | bytes 2752552 | tf_op jit(solution)/shard_map/stack | solution.py:143
  173.6 6.6 %fusion.93 = bf16[1,1,256,1,256]{2,4,3,1,0:T(8,128)(2,1)S(1)} fusion(f32[2,1,1,256,1,256]{3,5,4,2,1,0:T(8,128)S(1)} %get-tuple-element.165, f32[]{:T(128)} %bitcast.98, f32[]{:T(128)} %bitcast.95, f32[2,1,1,256,1,256]{3,5,4,2,1,0:T(8,128)S(1)} %get-tuple-element.164, f32[]{:T(128)} %bitcast.94, f32[]{:T(128)} %bitcast.91, ...), kind=kLoop, calls=%fused_computation.179 | loop fusion | flops 1310720 | bytes 2752552 | tf_op jit(solution)/shard_map/stack | solution.py:143
  180.2 6.6 %fusion.94 = bf16[1,1,256,1,256]{2,4,3,1,0:T(8,128)(2,1)S(1)} fusion(f32[2,1,1,256,1,256]{3,5,4,2,1,0:T(8,128)S(1)} %get-tuple-element.165, f32[]{:T(128)} %bitcast.98, f32[]{:T(128)} %bitcast.95, f32[2,1,1,256,1,256]{3,5,4,2,1,0:T(8,128)S(1)} %get-tuple-element.164, f32[]{:T(128)} %bitcast.94, f32[]{:T(128)} %bitcast.91, ...), kind=kLoop, calls=%fused_computation.180 | loop fusion | flops 1310720 | bytes 2752552 | tf_op jit(solution)/shard_map/stack | solution.py:143
  187.0 6.5 %fusion.95 = bf16[1,1,256,1,256]{2,4,3,1,0:T(8,128)(2,1)S(1)} fusion(f32[2,1,1,256,1,256]{3,5,4,2,1,0:T(8,128)S(1)} %get-tuple-element.170, f32[]{:T(128)} %bitcast.120, f32[]{:T(128)} %bitcast.117, f32[2,1,1,256,1,256]{3,5,4,2,1,0:T(8,128)S(1)} %get-tuple-element.169, f32[]{:T(128)} %bitcast.116, f32[]{:T(128)} %bitcast.113, ...), kind=kLoop, calls=%fused_computation.181 | loop fusion | flops 1310720 | bytes 2752552 | tf_op jit(solution)/shard_map/stack | solution.py:143
  193.5 6.5 %fusion.96 = bf16[1,1,256,1,256]{2,4,3,1,0:T(8,128)(2,1)S(1)} fusion(f32[2,1,1,256,1,256]{3,5,4,2,1,0:T(8,128)S(1)} %get-tuple-element.170, f32[]{:T(128)} %bitcast.120, f32[]{:T(128)} %bitcast.117, f32[2,1,1,256,1,256]{3,5,4,2,1,0:T(8,128)S(1)} %get-tuple-element.169, f32[]{:T(128)} %bitcast.116, f32[]{:T(128)} %bitcast.113, ...), kind=kLoop, calls=%fused_computation.182 | loop fusion | flops 1310720 | bytes 2752552 | tf_op jit(solution)/shard_map/stack | solution.py:143
  201.3 1.2 fusion.9
  202.4 3.6 %fusion.1 = f32[2,1,2,256,2,256]{5,3,4,2,0,1:T(8,128)S(1)} fusion(bf16[1,2,256,2,256]{4,2,3,1,0:T(8,128)(2,1)} %fusion.9, bf16[1,2,256,2,256]{4,2,3,1,0:T(8,128)(2,1)S(1)} %fusion.10, f32[256]{0:T(256)S(1)} %copy-done.13, f32[256]{0:T(256)S(1)} %copy-done.8, f32[256]{0:T(256)S(1)} %copy-done.10), kind=kOutput, calls=%fused_computation.56 | convolution fusion | flops 539361280 | bytes 3148800 | tf_op jit(solution)/shard_map/pfxkyb,ka->pfxayb/dot_general | solution.py:52
  206.0 1.3 copy-done.4
  207.6 3.1 %add_select_fusion = f32[2,1,256,256]{3,2,0,1:T(8,128)S(1)} fusion(s32[]{:T(128)} %bitcast.141, s32[]{:T(128)} %bitcast.142, f32[2,1,256,256]{3,2,0,1:T(8,128)S(1)} %slice_bitcast_fusion.25, f32[2,1,2,256,2,256]{5,3,4,2,0,1:T(8,128)} %copy-done.4, pred[]{:T(512)} %and_reduce_fusion), kind=kLoop, calls=%fused_computation.88 | loop fusion | flops 262144 | bytes 1572873 | tf_op jit(solution)/shard_map/select.9
  210.8 10.1 %scatter-add.29 = f32[2,1,480,480]{3,2,0,1:T(8,128)S(1)} dynamic-update-slice(f32[2,1,480,480]{3,2,0,1:T(8,128)S(1)} %scatter-add.26, f32[2,1,256,256]{3,2,0,1:T(8,128)S(1)} %add_select_fusion, s32[]{:T(128)} %constant.349.clone.1, s32[]{:T(128)} %constant.349.clone.1, s32[]{:T(128)} %bitcast.141, s32[]{:T(128)} %bitcast.142) | dynamic-update-slice | bytes 1048580 | tf_op jit(solution)/shard_map/scatter-add | solution.py:67
  220.9 1.2 fusion.25
  222.1 1.2 fusion.23
  223.3 6.7 %scatter-add.31 = f32[2,1,480,480]{3,2,0,1:T(8,128)S(1)} dynamic-update-slice(f32[2,1,480,480]{3,2,0,1:T(8,128)S(1)} %fusion.25, f32[2,1,256,256]{3,2,0,1:T(8,128)S(1)} %fusion.23, s32[]{:T(128)} %constant.349.clone.1, s32[]{:T(128)} %constant.349.clone.1, s32[]{:T(128)} %constant.366.clone.1, s32[]{:T(128)} %constant.366.clone.1) | dynamic-update-slice | bytes 1048580 | tf_op jit(solution)/shard_map/scatter-add | solution.py:67
  230.1 1.9 collective-permute-start.8
  232.0 4.3 %collective-permute-start.9 = (bf16[2,1,16,480]{3,2,0,1:T(8,128)(2,1)S(1)}, bf16[2,1,16,480]{3,2,0,1:T(8,128)(2,1)S(1)}, u32[]{:S(2)}, u32[]{:S(2)}) collective-permute-start(bf16[2,1,16,480]{3,2,0,1:T(8,128)(2,1)S(1)} %get-tuple-element.174), channel_id=1, source_target_pairs={{4,0},{8,4},{12,8},{16,12},{20,16},{24,20},{28,24},{5,1},{9,5},{13... | collective-permute-start | bytes 92168 | tf_op jit(solution)/shard_map/ppermute | solution.py:19
  236.5 1.2 collective-permute-done.9
  238.3 4.8 %collective-permute-start.10 = (bf16[2,1,16,448]{2,3,0,1:T(8,128)(2,1)S(1)}, bf16[2,1,16,448]{2,3,0,1:T(8,128)(2,1)S(1)}, u32[]{:S(2)}, u32[]{:S(2)}) collective-permute-start(bf16[2,1,16,448]{2,3,0,1:T(8,128)(2,1)S(1)} %get-tuple-element.185), channel_id=1, source_target_pairs={{0,1},{1,2},{2,3},{4,5},{5,6},{6,7},{8,9},{9,10},{10,11},{12,13},{... | collective-permute-start | bytes 86024 | tf_op jit(solution)/shard_map/ppermute | solution.py:18
  243.1 1.9 collective-permute-start.11
  246.2 4.2 %collective-permute-done.11 = bf16[2,1,16,448]{2,3,0,1:T(8,128)(2,1)S(1)} collective-permute-done((bf16[2,1,16,448]{2,3,0,1:T(8,128)(2,1)S(1)}, bf16[2,1,16,448]{2,3,0,1:T(8,128)(2,1)S(1)}, u32[]{:S(2)}, u32[]{:S(2)}) %collective-permute-start.11) | collective-permute-done | bytes 28704 | tf_op jit(solution)/shard_map/ppermute | solution.py:19
  250.8 1.8 scatter-add.36
  252.9 1.8 scatter-add.39
  254.7 4.6 %fusion.30 = (bf16[1,1,448,448]{3,2,1,0:T(8,128)(2,1)S(1)}, bf16[1,1,448,448]{3,2,1,0:T(8,128)(2,1)S(1)}) fusion(f32[2,1,448,448]{3,2,0,1:T(8,128)S(1)} %scatter-add.39, f32[448,448]{1,0:T(8,128)} %param.32, f32[]{:T(128)} %bitcast.278, f32[2,1,448,448]{3,2,1,0:T(8,128)S(1)} %bitcast.289), kind=kLoop, calls=%fused_computation.116 | loop fusion | flops 1806336 | bytes 3211268 | tf_op jit(solution)/shard_map/stack | solution.py:171
  259.3 1.0 pad_maximum_fusion.3
  (108 shorter events, 20.5 us)
Async XLA Ops:
  0.0 81.3 %copy-start = (bf16[3,1,2,256,256]{4,3,2,1,0:T(8,128)(2,1)S(1)}, bf16[3,1,2,256,256]{4,3,2,1,0:T(8,128)(2,1)}, u32[]{:S(2)}) copy-start(bf16[3,1,2,256,256]{4,3,2,1,0:T(8,128)(2,1)} %param.34) | copy-start | bytes 2359300
  0.0 68.4 %copy-start.2 = (s32[16,8]{0,1:T(8,128)S(1)}, s32[16,8]{0,1:T(8,128)}, u32[]{:S(2)}) copy-start(s32[16,8]{0,1:T(8,128)} %param.35) | copy-start | bytes 1540
  0.9 9.4 %collective-permute-start = (bf16[2,1,16,448]{3,2,1,0:T(8,128)(2,1)S(1)}, bf16[2,1,16,448]{3,2,1,0:T(8,128)(2,1)S(1)}, u32[]{:S(2)}, u32[]{:S(2)}) collective-permute-start(bf16[2,1,16,448]{3,2,1,0:T(8,128)(2,1)S(1)} %get-tuple-element.184), channel_id=1, source_target_pairs={{0,4},{4,8},{8,12},{12,16},{16,20},{20,24},{24,28},{1,5},{5,9},{9,... | collective-permute-start | bytes 86024 | tf_op jit(solution)/shard_map/ppermute | solution.py:18
  4.0 7.5 %collective-permute-start.1 = (bf16[2,1,16,448]{3,2,1,0:T(8,128)(2,1)S(1)}, bf16[2,1,16,448]{3,2,1,0:T(8,128)(2,1)S(1)}, u32[]{:S(2)}, u32[]{:S(2)}) collective-permute-start(bf16[2,1,16,448]{3,2,1,0:T(8,128)(2,1)S(1)} %get-tuple-element.183), channel_id=1, source_target_pairs={{4,0},{8,4},{12,8},{16,12},{20,16},{24,20},{28,24},{5,1},{9,5},{13... | collective-permute-start | bytes 86024 | tf_op jit(solution)/shard_map/ppermute | solution.py:19
  10.3 61.2 %copy-start.7 = (f32[256]{0:T(256)}, f32[256]{0:T(256)S(1)}, u32[]{:S(2)}) copy-start(f32[256]{0:T(256)S(1)} %get-tuple-element.271) | copy-start | bytes 3076
  10.3 61.2 %copy-start.9 = (f32[256]{0:T(256)}, f32[256]{0:T(256)S(1)}, u32[]{:S(2)}) copy-start(f32[256]{0:T(256)S(1)} %get-tuple-element.272) | copy-start | bytes 3076
  11.7 58.1 %collective-permute-start.2 = (bf16[2,1,480,16]{3,2,1,0:T(8,128)(2,1)S(1)}, bf16[2,1,480,16]{3,2,1,0:T(8,128)(2,1)S(1)}, u32[]{:S(2)}, u32[]{:S(2)}) collective-permute-start(bf16[2,1,480,16]{3,2,1,0:T(8,128)(2,1)S(1)} %get-tuple-element.179), channel_id=1, source_target_pairs={{0,1},{1,2},{2,3},{4,5},{5,6},{6,7},{8,9},{9,10},{10,11},{12,13},{... | collective-permute-start | bytes 92168 | tf_op jit(solution)/shard_map/ppermute | solution.py:18
  16.0 53.8 %collective-permute-start.3 = (bf16[2,1,480,16]{3,2,1,0:T(8,128)(2,1)S(1)}, bf16[2,1,480,16]{3,2,1,0:T(8,128)(2,1)S(1)}, u32[]{:S(2)}, u32[]{:S(2)}) collective-permute-start(bf16[2,1,480,16]{3,2,1,0:T(8,128)(2,1)S(1)} %get-tuple-element.180), channel_id=1, source_target_pairs={{1,0},{2,1},{3,2},{5,4},{6,5},{7,6},{9,8},{10,9},{11,10},{13,12},{... | collective-permute-start | bytes 92168 | tf_op jit(solution)/shard_map/ppermute | solution.py:19
  18.0 53.6 %copy-start.12 = (f32[256]{0:T(256)}, f32[256]{0:T(256)S(1)}, u32[]{:S(2)}) copy-start(f32[256]{0:T(256)S(1)} %fusion.102) | copy-start | bytes 3076
  75.0 23.6 %collective-permute-start.4 = (bf16[2,1,1,256,2,256]{5,3,4,2,0,1:T(8,128)(2,1)}, bf16[2,1,1,256,2,256]{5,3,4,2,0,1:T(8,128)(2,1)S(1)}, u32[]{:S(2)}, u32[]{:S(2)}) collective-permute-start(bf16[2,1,1,256,2,256]{5,3,4,2,0,1:T(8,128)(2,1)} %get-tuple-element.175), channel_id=1, source_target_pairs={{0,4},{4,8},{8,12},{12,16},{16,20},{20,24},{24,28},{1,5},{5,9},{9,... | collective-permute-start | bytes 1572872 | tf_op jit(solution)/shard_map/ppermute | solution.py:18
  77.3 24.0 %collective-permute-start.5 = (bf16[2,1,1,256,2,256]{5,3,4,2,0,1:T(8,128)(2,1)S(1)}, bf16[2,1,1,256,2,256]{5,3,4,2,0,1:T(8,128)(2,1)S(1)}, u32[]{:S(2)}, u32[]{:S(2)}) collective-permute-start(bf16[2,1,1,256,2,256]{5,3,4,2,0,1:T(8,128)(2,1)S(1)} %get-tuple-element.176), channel_id=1, source_target_pairs={{4,0},{8,4},{12,8},{16,12},{20,16},{24,20},{28,24},{5,1},{9,5},{13... | collective-permute-start | bytes 1572872 | tf_op jit(solution)/shard_map/ppermute | solution.py:19
  101.2 0.8 copy-start.5
  103.5 37.9 %collective-permute-start.6 = (bf16[2,1,4,256,1,256]{5,3,4,2,0,1:T(8,128)(2,1)}, bf16[2,1,4,256,1,256]{5,3,4,2,0,1:T(8,128)(2,1)}, u32[]{:S(2)}, u32[]{:S(2)}) collective-permute-start(bf16[2,1,4,256,1,256]{5,3,4,2,0,1:T(8,128)(2,1)} %get-tuple-element.171), channel_id=1, source_target_pairs={{0,1},{1,2},{2,3},{4,5},{5,6},{6,7},{8,9},{9,10},{10,11},{12,13},{... | collective-permute-start | bytes 3145736 | tf_op jit(solution)/shard_map/ppermute | solution.py:18
  107.8 33.7 %collective-permute-start.7 = (bf16[2,1,4,256,1,256]{5,3,4,2,0,1:T(8,128)(2,1)}, bf16[2,1,4,256,1,256]{5,3,4,2,0,1:T(8,128)(2,1)}, u32[]{:S(2)}, u32[]{:S(2)}) collective-permute-start(bf16[2,1,4,256,1,256]{5,3,4,2,0,1:T(8,128)(2,1)} %get-tuple-element.172), channel_id=1, source_target_pairs={{1,0},{2,1},{3,2},{5,4},{6,5},{7,6},{9,8},{10,9},{11,10},{13,12},{... | collective-permute-start | bytes 3145736 | tf_op jit(solution)/shard_map/ppermute | solution.py:19
  111.1 28.2 %copy-start.11 = (s32[4]{0:T(128)S(1)}, s32[4]{0:T(128)}, u32[]{:S(2)}) copy-start(s32[4]{0:T(128)} %constant.367.clone.1) | copy-start | bytes 52
  112.7 28.8 %copy-start.6 = (bf16[2,1,1,256,2,256]{5,3,4,2,0,1:T(8,128)(2,1)S(1)}, bf16[2,1,1,256,2,256]{5,3,4,2,0,1:T(8,128)(2,1)}, u32[]{:S(2)}) copy-start(bf16[2,1,1,256,2,256]{5,3,4,2,0,1:T(8,128)(2,1)} %copy-done.5) | copy-start | bytes 1572868
  141.4 2.8 %copy-start.3 = (bf16[16,2,256,256]{3,2,0,1:T(8,128)(2,1)S(1)}, bf16[16,2,256,256]{3,2,0,1:T(8,128)(2,1)}, u32[]{:S(2)}) copy-start(bf16[16,2,256,256]{3,2,0,1:T(8,128)(2,1)} %copy.80) | copy-start | bytes 12582916
  201.2 1.2 copy-start.8
  201.3 1.2 copy-start.10
  201.3 1.2 copy-start.13
  206.0 1.3 copy-start.4
  230.1 6.4 %collective-permute-start.8 = (bf16[2,1,16,480]{3,2,0,1:T(8,128)(2,1)S(1)}, bf16[2,1,16,480]{3,2,0,1:T(8,128)(2,1)S(1)}, u32[]{:S(2)}, u32[]{:S(2)}) collective-permute-start(bf16[2,1,16,480]{3,2,0,1:T(8,128)(2,1)S(1)} %get-tuple-element.173), channel_id=1, source_target_pairs={{0,4},{4,8},{8,12},{12,16},{16,20},{20,24},{24,28},{1,5},{5,9},{9,... | collective-permute-start | bytes 92168 | tf_op jit(solution)/shard_map/ppermute | solution.py:18
  232.0 5.7 %collective-permute-start.9 = (bf16[2,1,16,480]{3,2,0,1:T(8,128)(2,1)S(1)}, bf16[2,1,16,480]{3,2,0,1:T(8,128)(2,1)S(1)}, u32[]{:S(2)}, u32[]{:S(2)}) collective-permute-start(bf16[2,1,16,480]{3,2,0,1:T(8,128)(2,1)S(1)} %get-tuple-element.174), channel_id=1, source_target_pairs={{4,0},{8,4},{12,8},{16,12},{20,16},{24,20},{28,24},{5,1},{9,5},{13... | collective-permute-start | bytes 92168 | tf_op jit(solution)/shard_map/ppermute | solution.py:19
  238.3 7.9 %collective-permute-start.10 = (bf16[2,1,16,448]{2,3,0,1:T(8,128)(2,1)S(1)}, bf16[2,1,16,448]{2,3,0,1:T(8,128)(2,1)S(1)}, u32[]{:S(2)}, u32[]{:S(2)}) collective-permute-start(bf16[2,1,16,448]{2,3,0,1:T(8,128)(2,1)S(1)} %get-tuple-element.185), channel_id=1, source_target_pairs={{0,1},{1,2},{2,3},{4,5},{5,6},{6,7},{8,9},{9,10},{10,11},{12,13},{... | collective-permute-start | bytes 86024 | tf_op jit(solution)/shard_map/ppermute | solution.py:18
  243.1 7.3 %collective-permute-start.11 = (bf16[2,1,16,448]{2,3,0,1:T(8,128)(2,1)S(1)}, bf16[2,1,16,448]{2,3,0,1:T(8,128)(2,1)S(1)}, u32[]{:S(2)}, u32[]{:S(2)}) collective-permute-start(bf16[2,1,16,448]{2,3,0,1:T(8,128)(2,1)S(1)} %get-tuple-element.186), channel_id=1, source_target_pairs={{1,0},{2,1},{3,2},{5,4},{6,5},{7,6},{9,8},{10,9},{11,10},{13,12},{... | collective-permute-start | bytes 86024 | tf_op jit(solution)/shard_map/ppermute | solution.py:19
  254.7 5.6 %copy-start.1 = (bf16[3,1,2,256,256]{4,3,2,1,0:T(8,128)(2,1)S(1)}, bf16[3,1,2,256,256]{4,3,2,1,0:T(8,128)(2,1)}, u32[]{:S(2)}) copy-start(bf16[3,1,2,256,256]{4,3,2,1,0:T(8,128)(2,1)} %param.34) | copy-start | bytes 2359300
where the time goes:
time: 264 us; the launch traced here: 260 us
  between operations  75.2 us (28%)
  other arithmetic  69.8 us (26%)
  local copies, waits for them, and re-layouts  49.8 us (19%)
  starting transfers between devices  37.6 us (14%)
  waiting for transfers between devices  16.4 us (6%)
  matrix products  11.7 us (4%)
    another operation x8, other arithmetic, per_device(): mixed_cols.append(jnp.stack([acc_real, acc_imag]).astype(jnp.bfloat16))  51.6 us
    ppermute x6, starting transfers between devices, extended(): before = lax.ppermute(last, axis, up)  20.6 us
    scatter-add x3, local copies, waits for them, and re-layouts, rebuild(): canvas = canvas.at[:, :, tile_x * stride:tile_x * stride + length, tile_y...  17.1 us
    ppermute x6, starting transfers between devices, extended(): after = lax.ppermute(first, axis, down)  17 us
    ppermute x6, waiting for transfers between devices, extended(): before = lax.ppermute(last, axis, up)  8.37 us
    ppermute x6, waiting for transfers between devices, extended(): after = lax.ppermute(first, axis, down)  8 us
    gather x2, local copies, waits for them, and re-layouts, per_device(): propagator[window_velocity_group[near_x[:, None], near_y[None, :]]]  7.43 us
    unnamed x32, local copies, waits for them, and re-layouts  5.61 us
  transfers between devices with their start and end apart: 12, of which 4 were waited for; matrix products, arithmetic and copies ran while one was open for 9% of the time, Pallas kernels for 0%

commit v1 on v0

v1 whole, which is shorter than its diff:
```python
import math

import jax
import jax.numpy as jnp
import ml_dtypes
import numpy as np
from jax import lax
from jax.experimental import pallas as pl
from jax.experimental.pallas import tpu as pltpu
from jax.sharding import PartitionSpec as P

OVER = 32
HALF = OVER // 2
F32 = jnp.float32
BF16 = jnp.bfloat16
VMEM = pl.BlockSpec(memory_space=pltpu.VMEM)
SMEM = pl.BlockSpec(memory_space=pltpu.SMEM)
PARAMS = pltpu.CompilerParams(vmem_limit_bytes=48 * 2**20)


def cosine_table(length):
    points = np.arange(length, dtype=np.float32) + np.float32(0.5)
    angles = (np.float32(math.pi / length) * points[:, None]) * points[None, :]
    waves = np.cos(angles.astype(np.float64)).astype(np.float32)
    return (np.sqrt(np.float32(2.0 / length)) * waves).astype(ml_dtypes.bfloat16)


def bell_curve(length, margin):
    points = np.arange(length, dtype=np.float64)
    rising = np.sin(0.5 * math.pi * (points + 0.5) / margin)
    falling = np.cos(0.5 * math.pi * (points - (length - margin) + 0.5) / margin)
    bell = np.where(points < margin, rising, np.where(points >= length - margin, falling, 1.0))
    return bell.astype(np.float32)


def dot(left, right):
    return jnp.dot(left, right, preferred_element_type=F32)


def swap(block, axis, odd):
    size = lax.axis_size(axis)
    pairs = []
    for i in range(1 if odd else 0, size - 1, 2):
        pairs += [(i, i + 1), (i + 1, i)]
    return lax.ppermute(block, axis, pairs)


def parity(axis):
    return lax.rem(lax.axis_index(axis), 2)


def folded_kernel(prop_ref, cos_ref, cos_t_ref, row_ref, col_ref, left_ref, right_ref):
    groups, _, _, length, _ = prop_ref.shape
    wide = right_ref.shape[-1]
    bell = col_ref[...] * row_ref[...]
    inner = wide - 2 * OVER
    for g in range(groups):
        for part in range(2):
            half = dot(prop_ref[g, 0, part], cos_ref[...])
            high = half.astype(BF16)
            low = (half - high.astype(F32)).astype(BF16)
            full = (dot(cos_t_ref[...], high) + dot(cos_t_ref[...], low)) * bell
            left_ref[g, part] = full
            flipped = full.T
            zeros = jnp.zeros((length, wide), F32)
            edge = length - HALF
            right_ref[g, 0, part] = jnp.concatenate(
                [
                    flipped[:, HALF:],
                    zeros[:, : inner - edge],
                    flipped[:, :HALF],
                    zeros[:, : wide - inner - HALF],
                ],
                axis=1,
            ).astype(BF16)
            right_ref[g, 1, part] = jnp.concatenate(
                [
                    zeros[:, : inner - edge],
                    flipped[:, :edge],
                    zeros[:, :HALF],
                    flipped[:, edge:],
                    zeros[:, : wide - inner - OVER],
                ],
                axis=1,
            ).astype(BF16)


def fold(propagator, cosines, bell):
    groups, _, _, length, _ = propagator.shape
    wide = 2 * length
    return pl.pallas_call(
        folded_kernel,
        out_shape=(
            jax.ShapeDtypeStruct((groups, 2, length, length), F32),
            jax.ShapeDtypeStruct((groups, 2, 2, length, wide), BF16),
        ),
        in_specs=[VMEM] * 5,
        out_specs=(VMEM, VMEM),
        compiler_params=PARAMS,
        name="fold",
    )(propagator, cosines, cosines.T, bell[None, :], bell[:, None])


def spread(frame_ref, start, left, middle, right):
    count = middle.shape[1]
    span = left.shape[2]
    rows = pl.ds(start, count)
    wide = middle.shape[2]
    for part in range(2):
        west, centre, east = left[part], middle[part], right[part]
        frame_ref[0, part, rows] = jnp.concatenate([west, centre[:, :HALF]], axis=1)
        frame_ref[1, part, rows] = jnp.concatenate([west[:, span - HALF :], centre[:, :span]], axis=1)
        frame_ref[2, part, rows] = jnp.concatenate([centre[:, wide - span :], east[:, :HALF]], axis=1)
        frame_ref[3, part, rows] = jnp.concatenate([centre[:, wide - HALF :], east], axis=1)


def main_kernel(
    reach_ref,
    coup_ref,
    group_ref,
    own_ref,
    ye_ref,
    yo_ref,
    xe_ref,
    xo_ref,
    ze_ref,
    zo_ref,
    left_ref,
    right_ref,
    mid_ref,
    send_e_ref,
    send_o_ref,
    frame_ref,
    acc_ref,
    total_y,
    slots,
):
    length = left_ref.shape[-1]
    tile = own_ref.shape[1]
    span = length - HALF
    stride = length - OVER
    odd_x, odd_y = parity("gx"), parity("gy")
    base_x = lax.axis_index("gx") * 2
    base_y = lax.axis_index("gy") * 2
    row_e = pl.multiple_of(jnp.where(odd_x == 0, span + tile, 0), HALF)
    row_o = pl.multiple_of(jnp.where(odd_x == 0, 0, span + tile), HALF)

    def place(west, east, west_z, east_z):
        spread(frame_ref, span, west, own_ref, east)
        spread(frame_ref, row_e, west_z.at[:, :span], xe_ref, east_z.at[:, :span])
        spread(frame_ref, row_o, west_z.at[:, span:], xo_ref, east_z.at[:, span:])

    @pl.when(odd_y == 0)
    def _():
        place(yo_ref, ye_ref, zo_ref, ze_ref)

    @pl.when(odd_y == 1)
    def _():
        place(ye_ref, yo_ref, ze_ref, zo_ref)

    acc_ref[...] = jnp.zeros_like(acc_ref)

    def step(index, carry):
        target = index // slots
        slot = index % slots
        window = (base_x + target // 2) * total_y + base_y + target % 2
        source = reach_ref[window * slots + slot]

        @pl.when(source >= 0)
        def _():
            at_x = source // total_y - base_x + 1
            at_y = source % total_y - base_y + 1
            rows = pl.ds(pl.multiple_of(at_x * stride, HALF), length)
            group = group_ref[source]
            w_real = coup_ref[(window * slots + slot) * 2]
            w_imag = coup_ref[(window * slots + slot) * 2 + 1]
            t_real, t_imag = left_ref[group, 0], left_ref[group, 1]
            m_real = (w_real * t_real - w_imag * t_imag).astype(BF16)
            m_imag = (w_real * t_imag + w_imag * t_real).astype(BF16)
            x_real = frame_ref[at_y, 0, rows]
            x_imag = frame_ref[at_y, 1, rows]
            acc_ref[target, 0] += dot(m_real, x_real) - dot(m_imag, x_imag)
            acc_ref[target, 1] += dot(m_real, x_imag) + dot(m_imag, x_real)

        return carry

    lax.fori_loop(0, 4 * slots, step, 0)

    inner = tile
    edge = span
    for row in range(2):
        real = jnp.zeros((length, right_ref.shape[-1]), F32)
        imag = real
        for col in range(2):
            group = group_ref[(base_x + row) * total_y + base_y + col]
            m_real = acc_ref[row * 2 + col, 0].astype(BF16)
            m_imag = acc_ref[row * 2 + col, 1].astype(BF16)
            r_real, r_imag = right_ref[group, col, 0], right_ref[group, col, 1]
            real += dot(m_real, r_real) - dot(m_imag, r_imag)
            imag += dot(m_real, r_imag) + dot(m_imag, r_real)
        for part, out in ((0, real), (1, imag)):
            if row == 0:
                mid_ref[part, :edge] = out[HALF:]
                border = out[:HALF].astype(BF16)
            else:
                both = edge - (inner - edge)
                mid_ref[part, inner - edge : edge] += out[:both]
                mid_ref[part, edge:] = out[both:edge]
                border = out[edge:].astype(BF16)

            @pl.when(odd_x == row)
            def _():
                send_o_ref[part] = border

            @pl.when(odd_x != row)
            def _():
                send_e_ref[part] = border


def border_kernel(mid_ref, got_e_ref, got_o_ref, send_e_ref, send_o_ref, work_ref):
    tile = mid_ref.shape[1]
    odd_x, odd_y = parity("gx"), parity("gy")
    row_e = pl.multiple_of(jnp.where(odd_x == 0, tile - HALF, 0), HALF)
    row_o = pl.multiple_of(jnp.where(odd_x == 0, 0, tile - HALF), HALF)
    work_ref[...] = mid_ref[...]
    at = tile % 128
    for part in range(2):
        work_ref[part, pl.ds(row_e, HALF)] += got_e_ref[part].astype(F32)
        work_ref[part, pl.ds(row_o, HALF)] += got_o_ref[part].astype(F32)
        turned = work_ref[part].T
        west = turned[at : at + HALF].astype(BF16)
        east = turned[at + HALF : at + OVER].astype(BF16)

        @pl.when(odd_y == 0)
        def _():
            send_e_ref[part] = east
            send_o_ref[part] = west

        @pl.when(odd_y == 1)
        def _():
            send_e_ref[part] = west
            send_o_ref[part] = east


def final_kernel(
    mid_ref, xe_ref, xo_ref, ye_ref, yo_ref, cos_ref, sin_ref, out_ref, work_ref
):
    tile = mid_ref.shape[1]
    odd_x, odd_y = parity("gx"), parity("gy")
    row_e = pl.multiple_of(jnp.where(odd_x == 0, tile - HALF, 0), HALF)
    row_o = pl.multiple_of(jnp.where(odd_x == 0, 0, tile - HALF), HALF)
    far = tile - HALF
    lane = lax.broadcasted_iota(jnp.int32, (HALF, tile), 1)
    line = lax.broadcasted_iota(jnp.int32, (HALF, tile), 0)
    pick_e = (lane == line + jnp.where(odd_y == 0, far, 0)).astype(F32).astype(BF16)
    pick_o = (lane == line + jnp.where(odd_y == 0, 0, far)).astype(F32).astype(BF16)

    def outer(values, pick):
        return lax.dot_general(values, pick, (((0,), (0,)), ((), ())), preferred_element_type=F32)

    for part in range(2):
        work_ref[part] = (
            mid_ref[part, :, :tile] + outer(ye_ref[part], pick_e) + outer(yo_ref[part], pick_o)
        )
        work_ref[part, pl.ds(row_e, HALF)] += xe_ref[part, :, :tile].astype(F32)
        work_ref[part, pl.ds(row_o, HALF)] += xo_ref[part, :, :tile].astype(F32)
    real, imag = work_ref[0], work_ref[1]
    out_ref[0, 0] = (real * cos_ref[...] - imag * sin_ref[...]).astype(BF16)
    out_ref[1, 0] = (real * sin_ref[...] + imag * cos_ref[...]).astype(BF16)


def pick_side(odd, first, last, partner_is_even):
    toward_last = odd == (0 if partner_is_even else 1)
    return jnp.where(toward_last, last, first)


def per_device(
    wavefield, slowness, frequencies, propagator, window_velocity_group, reach_list, coupling
):
    length = propagator.shape[-1]
    span = length - HALF
    wide = 2 * length
    tile_rows, tile_cols = wavefield.shape[2:]
    total_y = window_velocity_group.shape[1]
    slots = reach_list.shape[2]
    odd_x, odd_y = parity("gx"), parity("gy")
    own = wavefield[:, 0]
    first_x, last_x = own[:, :span], own[:, tile_rows - span :]
    first_y, last_y = own[:, :, :span], own[:, :, tile_cols - span :]
    x_even = swap(pick_side(odd_x, first_x, last_x, True), "gx", False)
    x_odd = swap(pick_side(odd_x, first_x, last_x, False), "gx", True)
    y_even = swap(pick_side(odd_y, first_y, last_y, True), "gy", False)
    y_odd = swap(pick_side(odd_y, first_y, last_y, False), "gy", True)
    arrived = jnp.concatenate([x_even, x_odd], axis=1)
    first_z, last_z = arrived[:, :, :span], arrived[:, :, tile_cols - span :]
    z_even = swap(pick_side(odd_y, first_z, last_z, True), "gy", False)
    z_odd = swap(pick_side(odd_y, first_z, last_z, False), "gy", True)

    cosines = cosine_table(length)
    bell = bell_curve(length, OVER)
    left, right = fold(propagator, cosines, bell)

    def main(*refs):
        main_kernel(*refs, total_y=total_y, slots=slots)

    mid, send_e, send_o = pl.pallas_call(
        main,
        out_shape=(
            jax.ShapeDtypeStruct((2, tile_rows, wide), F32),
            jax.ShapeDtypeStruct((2, HALF, wide), BF16),
            jax.ShapeDtypeStruct((2, HALF, wide), BF16),
        ),
        in_specs=[SMEM] * 3 + [VMEM] * 9,
        out_specs=(VMEM,) * 3,
        scratch_shapes=[
            pltpu.VMEM((4, 2, tile_rows + 2 * span, length), BF16),
            pltpu.VMEM((4, 2, length, length), F32),
        ],
        compiler_params=PARAMS,
        name="mix",
    )(
        reach_list.reshape(-1),
        coupling.reshape(-1),
        window_velocity_group.reshape(-1),
        own,
        y_even,
        y_odd,
        x_even,
        x_odd,
        z_even,
        z_odd,
        left,
        right,
    )
    rows_e = swap(send_e, "gx", False)
    rows_o = swap(send_o, "gx", True)

    last_block = tile_cols // 128
    side = pl.BlockSpec((2, HALF, 128), lambda i: (0, 0, last_block))
    cols_spec = pl.BlockSpec((2, HALF, tile_rows), lambda i: (0, 0, 0))
    send_e, send_o = pl.pallas_call(
        border_kernel,
        grid=(1,),
        out_shape=(jax.ShapeDtypeStruct((2, HALF, tile_rows), BF16),) * 2,
        in_specs=[pl.BlockSpec((2, tile_rows, 128), lambda i: (0, 0, last_block)), side, side],
        out_specs=(cols_spec, cols_spec),
        scratch_shapes=[pltpu.VMEM((2, tile_rows, 128), F32)],
        compiler_params=PARAMS,
        name="border",
    )(mid, rows_e, rows_o)
    cols_e = swap(send_e, "gy", False)
    cols_o = swap(send_o, "gy", True)

    phases = frequencies[0] * slowness
    return pl.pallas_call(
        final_kernel,
        out_shape=jax.ShapeDtypeStruct(wavefield.shape, BF16),
        in_specs=[VMEM] * 7,
        out_specs=VMEM,
        scratch_shapes=[pltpu.VMEM((2, tile_rows, tile_cols), F32)],
        compiler_params=PARAMS,
        name="turn",
    )(mid, rows_e, rows_o, cols_e, cols_o, jnp.cos(phases), jnp.sin(phases))


def solution(mesh):
    return jax.shard_map(
        per_device,
        mesh=mesh,
        in_specs=(P(None, None, "gx", "gy"), P("gx", "gy"), P(), P(), P(), P(), P()),
        out_specs=P(None, None, "gx", "gy"),
        check_vma=False,
    )
```

time: 264 us -> 72.5 us (0.27); the launches traced: 260 us -> 71.8 us
  between operations: 75.2 us -> 0.92 us
  other arithmetic: 69.8 us -> 6.79 us
  local copies, waits for them, and re-layouts: 49.8 us -> 7.15 us
  starting transfers between devices: 37.6 us -> 18.7 us
  Pallas kernels: 0 us -> 15.2 us
  matrix products: 11.7 us -> 0 us
  waiting for transfers between devices: 16.4 us -> 23 us
    another operation x17 -> x0, other arithmetic: 61.6 us -> none  [the longest x8 51.6 us: per_device(): mixed_cols.append(jnp.stack([acc_real, acc_imag]).astype(jnp.bfloat16))]
    scatter-add x5 -> x0, local copies, waits for them, and re-layouts: 20.6 us -> none  [the longest x3 17.1 us: rebuild(): canvas = canvas.at[:, :, tile_x * stride:tile_x * stride + length, tile_y...]
    ppermute x12 -> x10, starting transfers between devices: 37.6 us -> 18.7 us  [swap(): return lax.ppermute(block, axis, pairs)]
    pallas_call x0 -> x4, Pallas kernels: none -> 15.2 us  [the longest x1 11.5 us: per_device(): pl.pallas_call(main, out_shape=(jax.ShapeDtypeStruct((2, tile_rows, wide)...]
    gather x10 -> x0, local copies, waits for them, and re-layouts: 13 us -> none  [the longest x2 7.43 us: per_device(): propagator[window_velocity_group[near_x[:, None], near_y[None, :]]]]
    dot_general x10 -> x0, matrix products: 11.7 us -> none  [the longest x8 5.47 us: contract(): return jnp.einsum(spec, left, right, preferred_element_type=jnp.float32)]
    slice x18 -> x0, local copies, waits for them, and re-layouts: 9.54 us -> none  [the longest x4 2.63 us: extended(): last = lax.slice_in_dim(shard, length - width, length, axis=dim)]
    ppermute x12 -> x10, waiting for transfers between devices: 16.4 us -> 23 us  [swap(): return lax.ppermute(block, axis, pairs)]
  transfers between devices with their start and end apart: 12 -> 10, of which waited for: 4 -> 3; matrix products, arithmetic and copies ran while one was open for 9% -> 10% of each run, Pallas kernels for 0% -> 2%
where the time goes in v1:
time: 72.5 us; the launch traced here: 71.8 us
  waiting for transfers between devices  23 us (32%)
  starting transfers between devices  18.7 us (26%)
  Pallas kernels  15.2 us (21%)
  local copies, waits for them, and re-layouts  7.15 us (10%)
  other arithmetic  6.79 us (9%)
  between operations  0.92 us (1%)
    ppermute x10, waiting for transfers between devices, swap(): return lax.ppermute(block, axis, pairs)  23 us
    ppermute x10, starting transfers between devices, swap(): return lax.ppermute(block, axis, pairs)  18.7 us
    pallas_call x1, Pallas kernels, per_device(): pl.pallas_call(main, out_shape=(jax.ShapeDtypeStruct((2, tile_rows, wide)...  11.5 us
    unnamed x28, local copies, waits for them, and re-layouts  5.59 us
    select_n x3, other arithmetic, pick_side(): return jnp.where(toward_last, last, first)  3.56 us
    sin x1, other arithmetic, per_device(): jnp.sin(phases)  3.23 us
    pallas_call x1, Pallas kernels, per_device(): pl.pallas_call(final_kernel, out_shape=jax.ShapeDtypeStruct(wavefield.sha...  1.88 us
    pallas_call x1, Pallas kernels, fold(): pl.pallas_call(folded_kernel, out_shape=(jax.ShapeDtypeStruct((groups, 2,...  1.58 us
  transfers between devices with their start and end apart: 10, of which 3 were waited for; matrix products, arithmetic and copies ran while one was open for 10% of the time, Pallas kernels for 2%

profile of v1, /device:TPU:9, one launch (start us, length us, event | category | flops | bytes accessed | tf_op | source)
XLA Modules:
  0.0 71.8 jit_solution(18269380425650437683)
XLA Ops:
  0.0 1.2 %broadcast_select_fusion.2 = (bf16[2,240,448]{2,1,0:T(8,128)(2,1)S(1)}, bf16[2,240,448]{2,1,0:T(8,128)(2,1)S(1)}) fusion(pred[]{:T(512)S(6)} %eq.17, bf16[2,448,448]{2,1,0:T(8,128)(2,1)} %bitcast.3, pred[]{:T(512)S(6)} %eq.16), kind=kLoop, calls=%fused_computation.4 | loop fusion | flops 430080 | bytes 1720322 | tf_op jit(solution)/shard_map/jit(_where)/select_n | solution.py:274
  1.2 1.3 %collective-permute-start.2 = (bf16[2,240,448]{2,1,0:T(8,128)(2,1)S(1)}, bf16[2,240,448]{2,1,0:T(8,128)(2,1)S(1)}, u32[]{:S(2)}, u32[]{:S(2)}) collective-permute-start(bf16[2,240,448]{2,1,0:T(8,128)(2,1)S(1)} %get-tuple-element.24), channel_id=1, source_target_pairs={{0,4},{4,0},{8,12},{12,8},{16,20},{20,16},{24,28},{28,24},{1,5},{5... | collective-permute-start | bytes 1290248 | tf_op jit(solution)/shard_map/ppermute | solution.py:45
  2.6 1.9 %collective-permute-start.3 = (bf16[2,240,448]{2,1,0:T(8,128)(2,1)S(1)}, bf16[2,240,448]{2,1,0:T(8,128)(2,1)S(1)}, u32[]{:S(2)}, u32[]{:S(2)}) collective-permute-start(bf16[2,240,448]{2,1,0:T(8,128)(2,1)S(1)} %get-tuple-element.23), channel_id=1, source_target_pairs={{4,8},{8,4},{12,16},{16,12},{20,24},{24,20},{5,9},{9,5},{13,17},{1... | collective-permute-start | bytes 1290248 | tf_op jit(solution)/shard_map/ppermute | solution.py:45
  4.5 0.0 copy-start
  4.5 19.4 %collective-permute-done.2.refs_6_ = bf16[2,240,448]{2,1,0:T(8,128)(2,1)S(1)} collective-permute-done((bf16[2,240,448]{2,1,0:T(8,128)(2,1)S(1)}, bf16[2,240,448]{2,1,0:T(8,128)(2,1)S(1)}, u32[]{:S(2)}, u32[]{:S(2)}) %collective-permute-start.2) | collective-permute-done | bytes 430112 | tf_op jit(solution)/shard_map/ppermute | solution.py:45
  24.0 0.0 collective-permute-done.3.refs_7_
  24.0 0.0 copy-start.9
  24.0 1.2 %broadcast_select_fusion = (bf16[2,480,240]{2,1,0:T(8,128)(2,1)}, bf16[2,480,240]{2,1,0:T(8,128)(2,1)}) fusion(pred[]{:T(512)S(6)} %eq.15, bf16[2,480,448]{2,1,0:T(8,128)(2,1)S(1)} %constant_dynamic-update-slice_fusion, pred[]{:T(512)S(6)} %eq.14), kind=kLoop, calls=%fused_computation.2 | loop fusion | flops 460800 | bytes 1843202 | tf_op jit(solution)/shard_map/jit(_where)/select_n | solution.py:274
  25.2 0.0 copy-start.5
  25.2 0.0 copy-start.7
  25.2 1.6 %collective-permute-start.4 = (bf16[2,480,240]{2,1,0:T(8,128)(2,1)}, bf16[2,480,240]{2,1,0:T(8,128)(2,1)S(1)}, u32[]{:S(2)}, u32[]{:S(2)}) collective-permute-start(bf16[2,480,240]{2,1,0:T(8,128)(2,1)} %get-tuple-element.20), channel_id=1, source_target_pairs={{0,1},{1,0},{2,3},{3,2},{4,5},{5,4},{6,7},{7,6},{8,9},{9,8},{10,11... | collective-permute-start | bytes 1382408 | tf_op jit(solution)/shard_map/ppermute | solution.py:45
  26.8 3.1 %collective-permute-start.5 = (bf16[2,480,240]{2,1,0:T(8,128)(2,1)}, bf16[2,480,240]{2,1,0:T(8,128)(2,1)}, u32[]{:S(2)}, u32[]{:S(2)}) collective-permute-start(bf16[2,480,240]{2,1,0:T(8,128)(2,1)} %get-tuple-element.19), channel_id=1, source_target_pairs={{1,2},{2,1},{5,6},{6,5},{9,10},{10,9},{13,14},{14,13},{17,18},{18,... | collective-permute-start | bytes 1382408 | tf_op jit(solution)/shard_map/ppermute | solution.py:45
  30.0 0.0 copy-done
  30.0 1.2 %broadcast_select_fusion.4 = (bf16[2,448,240]{2,1,0:T(8,128)(2,1)}, bf16[2,448,240]{2,1,0:T(8,128)(2,1)}) fusion(pred[]{:T(512)S(6)} %eq.15, bf16[2,448,448]{2,1,0:T(8,128)(2,1)S(1)} %bitcast.4, pred[]{:T(512)S(6)} %eq.14), kind=kLoop, calls=%fused_computation.6 | loop fusion | flops 430080 | bytes 1720322 | tf_op jit(solution)/shard_map/jit(_where)/select_n | solution.py:274
  31.2 0.0 collective-permute-start
  31.2 2.4 %collective-permute-start.1 = (bf16[2,448,240]{2,1,0:T(8,128)(2,1)}, bf16[2,448,240]{2,1,0:T(8,128)(2,1)}, u32[]{:S(2)}, u32[]{:S(2)}) collective-permute-start(bf16[2,448,240]{2,1,0:T(8,128)(2,1)} %get-tuple-element.25), channel_id=1, source_target_pairs={{1,2},{2,1},{5,6},{6,5},{9,10},{10,9},{13,14},{14,13},{17,18},{18,... | collective-permute-start | bytes 1290248 | tf_op jit(solution)/shard_map/ppermute | solution.py:45
  33.6 0.0 copy-done.9
  33.6 1.3 %copy.14 = f32[16,8,5,2]{3,2,1,0:T(8,128)} copy(f32[16,8,5,2]{0,3,2,1:T(2,128)S(1)} %copy-done.9) | data formatting | bytes 10240 | tf_op args[6]
  34.9 1.2 %reshape.10.refs_1_ = f32[1280]{0:T(1024)S(1)} reshape(f32[16,8,5,2]{3,2,1,0:T(8,128)} %copy.14) | data formatting | bytes 10240 | tf_op jit(solution)/shard_map/reshape | solution.py:323
  36.1 0.0 copy-done.10
  36.1 0.1 copy.13
  36.3 0.2 reshape.9.refs_0_
  36.5 0.0 copy-done.11
  36.5 0.1 copy.15
  36.5 0.1 reshape.11.refs_2_
  36.6 0.0 copy-done.3
  36.7 0.0 copy-start.6
  36.7 0.9 %copy-done.6 = f32[256,1]{1,0:T(8,128)S(1)} copy-done((f32[256,1]{1,0:T(8,128)S(1)}, f32[256,1]{1,0:T(8,128)}, u32[]{:S(2)}) %copy-start.6) | copy-done | bytes 1048
  37.6 1.6 %fold.1 = (f32[3,2,256,256]{3,2,1,0:T(8,128)S(1)}, bf16[3,2,2,256,512]{4,3,2,1,0:T(8,128)(2,1)S(1)}) custom-call(bf16[3,1,2,256,256]{4,3,2,1,0:T(8,128)(2,1)S(1)} %copy-done.3, bf16[256,256]{1,0:T(8,128)(2,1)S(1)} %copy-done.4, bf16[256,256]{1,0:T(8,128)(2,1)S(1)} %copy-done.5, f32[1,256]{1,0:T(1,128)S(1)} %copy-done.7, f32[256,1]{1,0:T(8,128)S(1)} %copy-done.6), custom_call_target="tpu_custom_call" | custom-call | tf_op jit(solution)/shard_map/fold/pallas_call | solution.py:91
  39.2 0.0 copy-start.2
  39.2 1.6 %copy-done.2 = bf16[3,2,2,256,512]{4,3,2,1,0:T(8,128)(2,1)} copy-done((bf16[3,2,2,256,512]{4,3,2,1,0:T(8,128)(2,1)}, bf16[3,2,2,256,512]{4,3,2,1,0:T(8,128)(2,1)S(1)}, u32[]{:S(2)}) %copy-start.2) | copy-done | bytes 3145752
  40.8 0.0 collective-permute-done.refs_4_
  40.8 1.4 %collective-permute-done.1.refs_5_ = bf16[2,448,240]{2,1,0:T(8,128)(2,1)} collective-permute-done((bf16[2,448,240]{2,1,0:T(8,128)(2,1)}, bf16[2,448,240]{2,1,0:T(8,128)(2,1)}, u32[]{:S(2)}, u32[]{:S(2)}) %collective-permute-start.1) | collective-permute-done | bytes 430112 | tf_op jit(solution)/shard_map/ppermute | solution.py:45
  42.2 0.0 collective-permute-done.4.refs_8_
  42.2 0.0 collective-permute-done.5.refs_9_
  42.2 11.5 %mix.1 = (f32[2,448,512]{2,1,0:T(8,128)}, bf16[2,16,512]{2,1,0:T(8,128)(2,1)S(1)}, bf16[2,16,512]{2,1,0:T(8,128)(2,1)S(1)}) custom-call(s32[640]{0:T(1024)S(1)} %reshape.9.refs_0_, f32[1280]{0:T(1024)S(1)} %reshape.10.refs_1_, s32[128]{0:T(128)S(1)} %reshape.11.refs_2_, bf16[2,448,448]{2,1,0:T(8,128)(2,1)S(1)} %bitcast.5, ...), custom_call_target="tpu_custom_call" | custom-call | tf_op jit(solution)/shard_map/mix/pallas_call | solution.py:306
  53.7 0.3 collective-permute-start.6
  54.0 2.7 %collective-permute-start.7 = (bf16[2,16,512]{2,1,0:T(8,128)(2,1)S(1)}, bf16[2,16,512]{2,1,0:T(8,128)(2,1)S(1)}, u32[]{:S(2)}, u32[]{:S(2)}) collective-permute-start(bf16[2,16,512]{2,1,0:T(8,128)(2,1)S(1)} %get-tuple-element.16), channel_id=1, source_target_pairs={{4,8},{8,4},{12,16},{16,12},{20,24},{24,20},{5,9},{9,5},{13,17},{1... | collective-permute-start | bytes 98312 | tf_op jit(solution)/shard_map/ppermute | solution.py:45
  57.4 0.0 collective-permute-done.6.got_e_ref.xe_ref
  57.4 2.2 %collective-permute-done.7.got_o_ref.xo_ref = bf16[2,16,512]{2,1,0:T(8,128)(2,1)S(1)} collective-permute-done((bf16[2,16,512]{2,1,0:T(8,128)(2,1)S(1)}, bf16[2,16,512]{2,1,0:T(8,128)(2,1)S(1)}, u32[]{:S(2)}, u32[]{:S(2)}) %collective-permute-start.7) | collective-permute-done | bytes 32800 | tf_op jit(solution)/shard_map/ppermute | solution.py:45
  59.6 1.5 %copy-done.1 = f32[2,448,512]{2,1,0:T(8,128)S(1)} copy-done((f32[2,448,512]{2,1,0:T(8,128)S(1)}, f32[2,448,512]{2,1,0:T(8,128)}, u32[]{:S(2)}) %copy-start.1) | copy-done | bytes 1835032
  61.1 0.3 border.1
  61.4 0.1 collective-permute-start.8
  61.4 5.2 %collective-permute-start.9 = (bf16[2,16,448]{2,1,0:T(8,128)(2,1)S(1)}, bf16[2,16,448]{2,1,0:T(8,128)(2,1)S(1)}, u32[]{:S(2)}, u32[]{:S(2)}) collective-permute-start(bf16[2,16,448]{2,1,0:T(8,128)(2,1)S(1)} %get-tuple-element.18), channel_id=1, source_target_pairs={{1,2},{2,1},{5,6},{6,5},{9,10},{10,9},{13,14},{14,13},{17,18},{18,... | collective-permute-start | bytes 86024 | tf_op jit(solution)/shard_map/ppermute | solution.py:45
  66.7 3.2 %multiply_sine_fusion = (f32[448,448]{1,0:T(8,128)S(1)}, f32[448,448]{1,0:T(8,128)S(1)}) fusion(f32[448,448]{1,0:T(8,128)S(1)} %copy-done.8, f32[]{:T(128)} %bitcast.2), kind=kLoop, calls=%fused_computation | loop fusion | flops 200704 | bytes 2408452 | tf_op jit(solution)/shard_map/sin | solution.py:363
  69.9 0.0 collective-permute-done.8.ye_ref
  69.9 0.0 collective-permute-done.9.yo_ref
  69.9 1.9 %turn.1 = bf16[2,1,448,448]{3,2,1,0:T(8,128)(2,1)} custom-call(f32[2,448,512]{2,1,0:T(8,128)S(1)} %copy-done.1, bf16[2,16,512]{2,1,0:T(8,128)(2,1)S(1)} %collective-permute-done.6.got_e_ref.xe_ref, bf16[2,16,512]{2,1,0:T(8,128)(2,1)S(1)} %collective-permute-done.7.got_o_ref.xo_ref, bf16[2,16,448]{2,1,0:T(8,128)(2,1)S(1)} %collective-permute-done.8.ye_ref, ...), custom_call_target="tpu_custom_call" | custom-call | tf_op jit(solution)/shard_map/turn/pallas_call | solution.py:355
  (12 shorter events, 0.1 us)
Async XLA Ops:
  1.2 22.7 %collective-permute-start.2 = (bf16[2,240,448]{2,1,0:T(8,128)(2,1)S(1)}, bf16[2,240,448]{2,1,0:T(8,128)(2,1)S(1)}, u32[]{:S(2)}, u32[]{:S(2)}) collective-permute-start(bf16[2,240,448]{2,1,0:T(8,128)(2,1)S(1)} %get-tuple-element.24), channel_id=1, source_target_pairs={{0,4},{4,0},{8,12},{12,8},{16,20},{20,16},{24,28},{28,24},{1,5},{5... | collective-permute-start | bytes 1290248 | tf_op jit(solution)/shard_map/ppermute | solution.py:45
  2.6 21.4 %collective-permute-start.3 = (bf16[2,240,448]{2,1,0:T(8,128)(2,1)S(1)}, bf16[2,240,448]{2,1,0:T(8,128)(2,1)S(1)}, u32[]{:S(2)}, u32[]{:S(2)}) collective-permute-start(bf16[2,240,448]{2,1,0:T(8,128)(2,1)S(1)} %get-tuple-element.23), channel_id=1, source_target_pairs={{4,8},{8,4},{12,16},{16,12},{20,24},{24,20},{5,9},{9,5},{13,17},{1... | collective-permute-start | bytes 1290248 | tf_op jit(solution)/shard_map/ppermute | solution.py:45
  4.5 25.5 %copy-start = (bf16[2,1,448,448]{3,2,1,0:T(8,128)(2,1)S(1)}, bf16[2,1,448,448]{3,2,1,0:T(8,128)(2,1)}, u32[]{:S(2)}) copy-start(bf16[2,1,448,448]{3,2,1,0:T(8,128)(2,1)} %param.11) | copy-start | bytes 2408452
  24.0 9.5 %copy-start.9 = (f32[16,8,5,2]{0,3,2,1:T(2,128)S(1)}, f32[16,8,5,2]{0,3,2,1:T(2,128)}, u32[]{:S(2)}) copy-start(f32[16,8,5,2]{0,3,2,1:T(2,128)} %param.17) | copy-start | bytes 15364
  25.2 10.9 %copy-start.10 = (s32[16,8,5]{0,1,2:T(8,128)S(1)}, s32[16,8,5]{0,1,2:T(8,128)}, u32[]{:S(2)}) copy-start(s32[16,8,5]{0,1,2:T(8,128)} %param.16) | copy-start | bytes 7684
  25.2 11.3 %copy-start.11 = (s32[16,8]{0,1:T(8,128)S(1)}, s32[16,8]{0,1:T(8,128)}, u32[]{:S(2)}) copy-start(s32[16,8]{0,1:T(8,128)} %param.15) | copy-start | bytes 1540
  25.2 11.4 %copy-start.3 = (bf16[3,1,2,256,256]{4,3,2,1,0:T(8,128)(2,1)S(1)}, bf16[3,1,2,256,256]{4,3,2,1,0:T(8,128)(2,1)}, u32[]{:S(2)}) copy-start(bf16[3,1,2,256,256]{4,3,2,1,0:T(8,128)(2,1)} %prop_ref.1) | copy-start | bytes 2359300
  25.2 11.4 %copy-start.4 = (bf16[256,256]{1,0:T(8,128)(2,1)S(1)}, bf16[256,256]{1,0:T(8,128)(2,1)}, u32[]{:S(2)}) copy-start(bf16[256,256]{1,0:T(8,128)(2,1)} %constant.26.clone.cos_ref) | copy-start | bytes 393220
  25.2 11.4 %copy-start.5 = (bf16[256,256]{1,0:T(8,128)(2,1)S(1)}, bf16[256,256]{1,0:T(8,128)(2,1)}, u32[]{:S(2)}) copy-start(bf16[256,256]{1,0:T(8,128)(2,1)} %constant.27.clone.cos_t_ref) | copy-start | bytes 393220
  25.2 11.4 %copy-start.7 = (f32[1,256]{1,0:T(1,128)S(1)}, f32[1,256]{1,0:T(1,128)}, u32[]{:S(2)}) copy-start(f32[1,256]{1,0:T(1,128)} %constant.28.clone.row_ref) | copy-start | bytes 3076
  25.2 17.0 %collective-permute-start.4 = (bf16[2,480,240]{2,1,0:T(8,128)(2,1)}, bf16[2,480,240]{2,1,0:T(8,128)(2,1)S(1)}, u32[]{:S(2)}, u32[]{:S(2)}) collective-permute-start(bf16[2,480,240]{2,1,0:T(8,128)(2,1)} %get-tuple-element.20), channel_id=1, source_target_pairs={{0,1},{1,0},{2,3},{3,2},{4,5},{5,4},{6,7},{7,6},{8,9},{9,8},{10,11... | collective-permute-start | bytes 1382408 | tf_op jit(solution)/shard_map/ppermute | solution.py:45
  26.8 15.4 %collective-permute-start.5 = (bf16[2,480,240]{2,1,0:T(8,128)(2,1)}, bf16[2,480,240]{2,1,0:T(8,128)(2,1)}, u32[]{:S(2)}, u32[]{:S(2)}) collective-permute-start(bf16[2,480,240]{2,1,0:T(8,128)(2,1)} %get-tuple-element.19), channel_id=1, source_target_pairs={{1,2},{2,1},{5,6},{6,5},{9,10},{10,9},{13,14},{14,13},{17,18},{18,... | collective-permute-start | bytes 1382408 | tf_op jit(solution)/shard_map/ppermute | solution.py:45
  31.2 9.6 %collective-permute-start = (bf16[2,448,240]{2,1,0:T(8,128)(2,1)}, bf16[2,448,240]{2,1,0:T(8,128)(2,1)}, u32[]{:S(2)}, u32[]{:S(2)}) collective-permute-start(bf16[2,448,240]{2,1,0:T(8,128)(2,1)} %get-tuple-element.26), channel_id=1, source_target_pairs={{0,1},{1,0},{2,3},{3,2},{4,5},{5,4},{6,7},{7,6},{8,9},{9,8},{10,11... | collective-permute-start | bytes 1290248 | tf_op jit(solution)/shard_map/ppermute | solution.py:45
  31.2 11.0 %collective-permute-start.1 = (bf16[2,448,240]{2,1,0:T(8,128)(2,1)}, bf16[2,448,240]{2,1,0:T(8,128)(2,1)}, u32[]{:S(2)}, u32[]{:S(2)}) collective-permute-start(bf16[2,448,240]{2,1,0:T(8,128)(2,1)} %get-tuple-element.25), channel_id=1, source_target_pairs={{1,2},{2,1},{5,6},{6,5},{9,10},{10,9},{13,14},{14,13},{17,18},{18,... | collective-permute-start | bytes 1290248 | tf_op jit(solution)/shard_map/ppermute | solution.py:45
  36.7 0.9 %copy-start.6 = (f32[256,1]{1,0:T(8,128)S(1)}, f32[256,1]{1,0:T(8,128)}, u32[]{:S(2)}) copy-start(f32[256,1]{1,0:T(8,128)} %constant.29.clone.col_ref) | copy-start | bytes 3076
  39.2 1.6 %copy-start.2 = (bf16[3,2,2,256,512]{4,3,2,1,0:T(8,128)(2,1)}, bf16[3,2,2,256,512]{4,3,2,1,0:T(8,128)(2,1)S(1)}, u32[]{:S(2)}) copy-start(bf16[3,2,2,256,512]{4,3,2,1,0:T(8,128)(2,1)S(1)} %get-tuple-element.13.refs_11_) | copy-start | bytes 9437188
  42.2 24.5 %copy-start.8 = (f32[448,448]{1,0:T(8,128)S(1)}, f32[448,448]{1,0:T(8,128)}, u32[]{:S(2)}) copy-start(f32[448,448]{1,0:T(8,128)} %param.12) | copy-start | bytes 2408452
  53.7 3.7 %collective-permute-start.6 = (bf16[2,16,512]{2,1,0:T(8,128)(2,1)S(1)}, bf16[2,16,512]{2,1,0:T(8,128)(2,1)S(1)}, u32[]{:S(2)}, u32[]{:S(2)}) collective-permute-start(bf16[2,16,512]{2,1,0:T(8,128)(2,1)S(1)} %get-tuple-element.15), channel_id=1, source_target_pairs={{0,4},{4,0},{8,12},{12,8},{16,20},{20,16},{24,28},{28,24},{1,5},{5... | collective-permute-start | bytes 98312 | tf_op jit(solution)/shard_map/ppermute | solution.py:45
  54.0 5.5 %collective-permute-start.7 = (bf16[2,16,512]{2,1,0:T(8,128)(2,1)S(1)}, bf16[2,16,512]{2,1,0:T(8,128)(2,1)S(1)}, u32[]{:S(2)}, u32[]{:S(2)}) collective-permute-start(bf16[2,16,512]{2,1,0:T(8,128)(2,1)S(1)} %get-tuple-element.16), channel_id=1, source_target_pairs={{4,8},{8,4},{12,16},{16,12},{20,24},{24,20},{5,9},{9,5},{13,17},{1... | collective-permute-start | bytes 98312 | tf_op jit(solution)/shard_map/ppermute | solution.py:45
  59.6 1.5 %copy-start.1 = (f32[2,448,512]{2,1,0:T(8,128)S(1)}, f32[2,448,512]{2,1,0:T(8,128)}, u32[]{:S(2)}) copy-start(f32[2,448,512]{2,1,0:T(8,128)} %get-tuple-element.14.mid_ref) | copy-start | bytes 5505028
  61.4 8.6 %collective-permute-start.8 = (bf16[2,16,448]{2,1,0:T(8,128)(2,1)S(1)}, bf16[2,16,448]{2,1,0:T(8,128)(2,1)S(1)}, u32[]{:S(2)}, u32[]{:S(2)}) collective-permute-start(bf16[2,16,448]{2,1,0:T(8,128)(2,1)S(1)} %get-tuple-element.17), channel_id=1, source_target_pairs={{0,1},{1,0},{2,3},{3,2},{4,5},{5,4},{6,7},{7,6},{8,9},{9,8},{10,11... | collective-permute-start | bytes 86024 | tf_op jit(solution)/shard_map/ppermute | solution.py:45
  61.4 8.5 %collective-permute-start.9 = (bf16[2,16,448]{2,1,0:T(8,128)(2,1)S(1)}, bf16[2,16,448]{2,1,0:T(8,128)(2,1)S(1)}, u32[]{:S(2)}, u32[]{:S(2)}) collective-permute-start(bf16[2,16,448]{2,1,0:T(8,128)(2,1)S(1)} %get-tuple-element.18), channel_id=1, source_target_pairs={{1,2},{2,1},{5,6},{6,5},{9,10},{10,9},{13,14},{14,13},{17,18},{18,... | collective-permute-start | bytes 86024 | tf_op jit(solution)/shard_map/ppermute | solution.py:45

commit v2 on v1

v2 whole, which is shorter than its diff:
```python
import functools
import math

import jax
import jax.numpy as jnp
import ml_dtypes
import numpy as np
from jax import lax
from jax.experimental import pallas as pl
from jax.experimental.pallas import tpu as pltpu
from jax.sharding import PartitionSpec as P

OVER = 32
HALF = OVER // 2
F32 = jnp.float32
BF16 = jnp.bfloat16
VMEM = pl.BlockSpec(memory_space=pltpu.VMEM)
SMEM = pl.BlockSpec(memory_space=pltpu.SMEM)
HBM = pl.BlockSpec(memory_space=pltpu.HBM)
PARAMS = pltpu.CompilerParams(vmem_limit_bytes=20 * 2**20)


def cosine_table(length):
    points = np.arange(length, dtype=np.float32) + np.float32(0.5)
    angles = (np.float32(math.pi / length) * points[:, None]) * points[None, :]
    waves = np.cos(angles.astype(np.float64)).astype(np.float32)
    return (np.sqrt(np.float32(2.0 / length)) * waves).astype(ml_dtypes.bfloat16)


def bell_curve(length, margin):
    points = np.arange(length, dtype=np.float64)
    rising = np.sin(0.5 * math.pi * (points + 0.5) / margin)
    falling = np.cos(0.5 * math.pi * (points - (length - margin) + 0.5) / margin)
    bell = np.where(points < margin, rising, np.where(points >= length - margin, falling, 1.0))
    return bell.astype(np.float32)


def dot(left, right):
    return jnp.dot(left, right, preferred_element_type=F32)


def swap(block, axis, odd):
    size = lax.axis_size(axis)
    pairs = []
    for i in range(1 if odd else 0, size - 1, 2):
        pairs += [(i, i + 1), (i + 1, i)]
    return lax.ppermute(block, axis, pairs)


def parity(axis):
    return lax.rem(lax.axis_index(axis), 2)


def cost(micros):
    return pl.CostEstimate(
        flops=int(micros * 1.1e9), bytes_accessed=int(micros * 3.6e6), transcendentals=0
    )


def fetch(pairs, sems):
    copies = [pltpu.make_async_copy(a, b, sems.at[i]) for i, (a, b) in enumerate(pairs)]
    for copy in copies:
        copy.start()
    return copies


def list_tables(all_reach_ref, all_coup_ref, all_group_ref, table_ref):
    slots, total_y, total_x = all_reach_ref.shape
    odd_x = parity("gx")
    base_x = lax.axis_index("gx") * 2
    base_y = lax.axis_index("gy") * 2
    for row in range(4):
        for col in range(4):
            x = jnp.clip(base_x - 1 + row, 0, total_x - 1)
            y = jnp.clip(base_y - 1 + col, 0, total_y - 1)
            table_ref[row * 4 + col] = all_group_ref[y, x].astype(F32)
    for row in range(3):
        for col in range(2):
            x, y = base_x - odd_x + row, base_y + col
            for slot in range(slots):
                reach = all_reach_ref[slot, y, x]
                place = (reach // total_y - base_x + 1) * 4 + reach % total_y - base_y + 1
                at = 16 + ((row * 2 + col) * slots + slot) * 3
                table_ref[at] = jnp.where(reach >= 0, place, -1).astype(F32)
                table_ref[at + 1] = all_coup_ref[y, slot, 0, x]
                table_ref[at + 2] = all_coup_ref[y, slot, 1, x]


def folded_kernel(
    reach_any,
    coup_any,
    group_any,
    prop_ref,
    cos_ref,
    cos_t_ref,
    row_ref,
    left_ref,
    right_ref,
    strip_ref,
    table_ref,
    reach_ref,
    coup_ref,
    group_ref,
    sems,
):
    pairs = ((reach_any, reach_ref), (coup_any, coup_ref), (group_any, group_ref))
    copies = fetch(pairs, sems)
    groups, _, _, length, _ = prop_ref.shape
    wide = right_ref.shape[-1]
    curve = jnp.broadcast_to(row_ref[...], (length, length))
    bell = curve * curve.T
    inner = wide - 2 * OVER
    edge = length - HALF
    for g in range(groups):
        for part in range(2):
            half = dot(prop_ref[g, 0, part], cos_ref[...])
            high = half.astype(BF16)
            low = (half - high.astype(F32)).astype(BF16)
            full = (dot(cos_t_ref[...], high) + dot(cos_t_ref[...], low)) * bell
            left_ref[g, part] = full
            strip_ref[g, part] = jnp.concatenate([full[:, :HALF], full[:, edge:]], axis=1)
            flipped = full.T
            zeros = jnp.zeros((length, wide), F32)
            right_ref[g, 0, part] = jnp.concatenate(
                [
                    flipped[:, HALF:],
                    zeros[:, : inner - edge],
                    flipped[:, :HALF],
                    zeros[:, : wide - inner - HALF],
                ],
                axis=1,
            ).astype(BF16)
            right_ref[g, 1, part] = jnp.concatenate(
                [
                    zeros[:, : inner - edge],
                    flipped[:, :edge],
                    zeros[:, :HALF],
                    flipped[:, edge:],
                    zeros[:, : wide - inner - OVER],
                ],
                axis=1,
            ).astype(BF16)
    for copy in copies:
        copy.wait()
    list_tables(reach_ref, coup_ref, group_ref, table_ref)


def fold(propagator, cosines, bell, reach_list, coupling, window_velocity_group):
    groups, _, _, length, _ = propagator.shape
    slots = reach_list.shape[2]
    return pl.pallas_call(
        folded_kernel,
        out_shape=(
            pltpu.VMEM((groups, 2, length, length), F32),
            pltpu.VMEM((groups, 2, 2, length, 2 * length), BF16),
            pltpu.VMEM((groups, 2, length, OVER), F32),
            jax.ShapeDtypeStruct((16 + 18 * slots,), F32),
        ),
        in_specs=[pl.BlockSpec(memory_space=pl.ANY)] * 3 + [VMEM] * 4,
        out_specs=(VMEM,) * 3 + (SMEM,),
        scratch_shapes=[
            pltpu.SMEM(reach_list.shape[::-1], jnp.int32),
            pltpu.SMEM(coupling.shape[1:] + coupling.shape[:1], F32),
            pltpu.SMEM(window_velocity_group.shape[::-1], jnp.int32),
            pltpu.SemaphoreType.DMA((3,)),
        ],
        compiler_params=PARAMS,
        cost_estimate=cost(2),
        name="fold",
    )(
        jnp.transpose(reach_list, (2, 1, 0)),
        jnp.transpose(coupling, (1, 2, 3, 0)),
        window_velocity_group.T,
        propagator,
        cosines,
        cosines.T,
        bell[None, :],
    )


def spread(west, middle, east, part):
    span = west.shape[2]
    wide = middle.shape[2]
    left, centre, right = west[part], middle[part], east[part]
    return (
        jnp.concatenate([left, centre[:, :HALF]], axis=1),
        jnp.concatenate([left[:, span - HALF :], centre[:, :span]], axis=1),
        jnp.concatenate([centre[:, wide - span :], right[:, :HALF]], axis=1),
        jnp.concatenate([centre[:, wide - HALF :], right], axis=1),
    )


def each_way(odd, even_call, odd_call):
    pl.when(odd == 0)(even_call)
    pl.when(odd == 1)(odd_call)


def start_of(odd, if_even, if_odd):
    return pl.multiple_of(jnp.where(odd == 0, if_even, if_odd), HALF)


def scaled(table, w_real, w_imag):
    real, imag = table[0], table[1]
    return (
        (w_real * real - w_imag * imag).astype(BF16),
        (w_real * imag + w_imag * real).astype(BF16),
    )


def add_product(out, at, weights, real, imag):
    w_real, w_imag = weights
    out[at + (0,)] += dot(w_real, real) - dot(w_imag, imag)
    out[at + (1,)] += dot(w_real, imag) + dot(w_imag, real)


class Lists:
    def __init__(self, table_ref, slots):
        self.table_ref, self.slots = table_ref, slots
        self.odd_x = parity("gx")

    def group_at(self, place):
        return self.table_ref[place].astype(jnp.int32)

    def window(self, row, col):
        return (row + 1) * 4 + col + 1

    def entry(self, row, col, slot):
        at = 16 + (((row + self.odd_x) * 2 + col) * self.slots + slot) * 3
        reach = self.table_ref[at].astype(jnp.int32)
        return reach, self.table_ref[at + 1], self.table_ref[at + 2]

    def weight_of(self, row, col, source):
        real, imag = jnp.float32(0), jnp.float32(0)
        for slot in range(self.slots):
            reach, c_real, c_imag = self.entry(row, col, slot)
            real += jnp.where(reach == source, c_real, 0.0)
            imag += jnp.where(reach == source, c_imag, 0.0)
        return real, imag

    def slot_of(self, row, col, slot):
        reach, c_real, c_imag = self.entry(row, col, slot)
        live = reach >= 0
        source = jnp.where(live, reach, self.window(row, col))
        at_row = source // 4
        at_x = jnp.where(self.odd_x == 0, at_row, 3 - at_row)
        real = jnp.where(live, c_real, 0.0)
        imag = jnp.where(live, c_imag, 0.0)
        return self.group_at(source), at_x, source % 4, real, imag


def pack_sides(blocks, near_ref, far_ref, part):
    width = near_ref.shape[2]
    start = blocks[0].shape[2] - width

    def store(high_ref, low_ref):
        row = 0
        for block in blocks:
            rows = pl.ds(row, block.shape[1])
            high_ref[part, rows] = block[part, :, start:]
            low_ref[part, rows] = block[part, :, :width]
            row += block.shape[1]

    each_way(parity("gy"), lambda: store(near_ref, far_ref), lambda: store(far_ref, near_ref))


def rows_kernel(wave_ref, x_ref, rim_ref):
    odd_x = parity("gx")
    tile, span = wave_ref.shape[2], x_ref.shape[1]
    for part in range(2):
        x_ref[part] = wave_ref[part, 0, pl.ds(start_of(odd_x, 0, tile - span), span)]
        rim_ref[part] = wave_ref[part, 0, pl.ds(start_of(odd_x, tile - HALF, 0), HALF)]


def cols_kernel(wave_ref, rim_ref, near_ref, far_ref):
    for part in range(2):
        pack_sides([wave_ref.at[:, 0]], near_ref, far_ref, part)


def corner_kernel(x_ref, rim_ref, near_ref, far_ref):
    x_ref = x_ref.at[:, pl.ds(start_of(parity("gx"), HALF, 0), x_ref.shape[1] - HALF)]
    for part in range(2):
        pack_sides([x_ref, rim_ref], near_ref, far_ref, part)


def edge_kernel(lists, wave_ref, ye_ref, yo_ref, left_ref, x_ref, part_ref, frame_ref, sum_ref):
    length = left_ref.shape[-1]
    own_ref = wave_ref.at[:, 0]
    tile = own_ref.shape[1]
    span = length - HALF
    odd_x, odd_y = lists.odd_x, parity("gy")

    def fill(west, east):
        for part in range(2):
            for at, block in enumerate(spread(west, own_ref, east, part)):
                frame_ref[at, part] = block

    each_way(odd_y, lambda: fill(yo_ref, ye_ref), lambda: fill(ye_ref, yo_ref))
    far = tile - span
    low_o, low_e = start_of(odd_x, 0, far), start_of(odd_x, far, 0)
    edge_o, edge_e = start_of(odd_x, 0, tile - HALF), start_of(odd_x, tile - HALF, 0)
    at_o, at_e = start_of(odd_x, HALF, 0), start_of(odd_x, 0, HALF)
    hole_o, hole_e = start_of(odd_x, 0, span), start_of(odd_x, span, 0)
    rim = jnp.zeros((HALF, length), BF16)
    empty = jnp.zeros((length, length), BF16)
    for at in range(4):
        for part in range(2):
            rows = frame_ref.at[at, part]
            x_ref[0, at, part] = empty
            x_ref[3, at, part] = empty
            x_ref[0, at, part, pl.ds(hole_e, HALF)] = rows[pl.ds(edge_o, HALF)]
            x_ref[3, at, part, pl.ds(hole_o, HALF)] = rows[pl.ds(edge_e, HALF)]
            x_ref[1, at, part, pl.ds(at_o, span)] = rows[pl.ds(low_o, span)]
            x_ref[2, at, part, pl.ds(at_e, span)] = rows[pl.ds(low_e, span)]
            x_ref[1, at, part, pl.ds(hole_o, HALF)] = rim
            x_ref[2, at, part, pl.ds(hole_e, HALF)] = rim
    beyond = jnp.where(odd_x == 0, 2, -1)
    mine = jnp.where(odd_x == 0, 1, 0)
    for col in range(2):
        for part in range(2):
            sum_ref[part] = jnp.zeros((length, length), F32)
        for step in range(3):
            source = lists.window(mine, col + step - 1)
            w_real, w_imag = lists.weight_of(beyond, col, source)
            weights = scaled(left_ref.at[lists.group_at(source)], w_real, w_imag)
            add_product(sum_ref, (), weights, x_ref[2, col + step, 0], x_ref[2, col + step, 1])
        for part in range(2):
            part_ref[part, :, col * length : (col + 1) * length] = sum_ref[part].astype(BF16)


def early_kernel(lists, x_ref, left_ref, strip_ref, sum_ref, packed_ref, *, c):
    length = left_ref.shape[-1]
    row = lists.odd_x ^ c
    for col in range(2):
        for part in range(2):
            sum_ref[col, part] = jnp.zeros((length, length), F32)
        strips = []
        for slot in range(lists.slots):
            group, at_x, at_y, w_real, w_imag = lists.slot_of(row, col, slot)
            weights = scaled(left_ref.at[group], w_real, w_imag)
            add_product(sum_ref, (col,), weights, x_ref[at_x, at_y, 0], x_ref[at_x, at_y, 1])
            inside = (at_x == 1) | (at_x == 2)
            w_real = jnp.where(inside, w_real, 0.0)
            w_imag = jnp.where(inside, w_imag, 0.0)
            strips.append(scaled(strip_ref.at[group], w_real, w_imag))
        for part in range(2):
            packed_ref[col, part] = jnp.concatenate([s[part] for s in strips], axis=1)


def late_kernel(
    lists,
    xo_ref,
    rim_ref,
    ze_ref,
    zo_ref,
    left_ref,
    early_o_ref,
    packed_o_ref,
    early_e_ref,
    packed_e_ref,
    right_ref,
    mid_ref,
    send_e_ref,
    send_o_ref,
    outer_ref,
    strip_ref,
    sum_ref,
    out_ref,
):
    length = left_ref.shape[-1]
    span = length - HALF
    tile = mid_ref.shape[1]
    odd_x, odd_y = lists.odd_x, parity("gy")
    at_o, hole_o = start_of(odd_x, 0, HALF), start_of(odd_x, span, 0)
    lean_o, lean_e = start_of(odd_x, 0, HALF), start_of(odd_x, HALF, 0)
    touch = start_of(odd_x, span - HALF, 0)
    xo_ref = xo_ref.at[:, pl.ds(start_of(odd_x, HALF, 0), span)]
    strip_ref[...] = jnp.zeros_like(strip_ref)

    def fill(west, east):
        for part in range(2):
            for at, block in enumerate(spread(west.at[:, :span], xo_ref, east.at[:, :span], part)):
                outer_ref[at, part, pl.ds(at_o, span)] = block
                outer_ref[at, part, pl.ds(hole_o, HALF)] = jnp.zeros((HALF, length), BF16)
            for at, block in enumerate(spread(west.at[:, span:], rim_ref, east.at[:, span:], part)):
                strip_ref[1, at, part, pl.ds(lean_e, HALF)] = block

    each_way(odd_y, lambda: fill(zo_ref, ze_ref), lambda: fill(ze_ref, zo_ref))
    shift = start_of(odd_x, span - HALF, HALF)
    for at in range(4):
        for part in range(2):
            strip_ref[0, at, part, pl.ds(lean_o, HALF)] = outer_ref[at, part, pl.ds(shift, HALF)]

    sum_ref[0] = early_o_ref[...]
    sum_ref[1] = early_e_ref[...]
    beyond = jnp.where(odd_x == 0, -1, 2)
    for c in range(2):
        row = odd_x ^ c
        for col in range(2):
            if c == 0:
                for step in range(3):
                    source = lists.window(beyond, col + step - 1)
                    w_real, w_imag = lists.weight_of(row, col, source)
                    weights = scaled(left_ref.at[lists.group_at(source)], w_real, w_imag)
                    add_product(
                        sum_ref, (c, col), weights, outer_ref[col + step, 0], outer_ref[col + step, 1]
                    )
            rows = [[], []]
            for slot in range(lists.slots):
                _, at_x, at_y, _, _ = lists.slot_of(row, col, slot)
                at_x = jnp.clip(at_x - 1, 0, 1)
                for part in range(2):
                    rows[part].append(strip_ref[at_x, at_y, part])
            real, imag = (jnp.concatenate(r, axis=0) for r in rows)
            packed_ref = packed_o_ref if c == 0 else packed_e_ref
            add_product(sum_ref, (c, col), (packed_ref[col, 0], packed_ref[col, 1]), real, imag)
    mid_ref[...] = jnp.zeros_like(mid_ref)
    for c in range(2):
        row = odd_x ^ c
        groups = [lists.group_at(lists.window(row, col)) for col in range(2)]
        blocks = [[sum_ref[c, col, part].astype(BF16) for part in range(2)] for col in range(2)]
        turn(blocks, right_ref, groups, out_ref)
        lower = odd_x if c == 0 else 1 - odd_x
        source = start_of(lower, HALF, 0)
        target = start_of(lower, 0, tile - span)
        border = start_of(lower, 0, span)
        send = send_o_ref if c == 0 else send_e_ref
        for part in range(2):
            mid_ref[part, pl.ds(target, span)] += out_ref[part, pl.ds(source, span)]
            send[part] = out_ref[part, pl.ds(border, HALF)].astype(BF16)


def turn(blocks, right_ref, groups, out_ref):
    real, imag = 0.0, 0.0
    for col in range(2):
        m_real, m_imag = blocks[col]
        r_real, r_imag = right_ref[groups[col], col, 0], right_ref[groups[col], col, 1]
        real += dot(m_real, r_real) - dot(m_imag, r_imag)
        imag += dot(m_real, r_imag) + dot(m_imag, r_real)
    out_ref[0] = real
    out_ref[1] = imag


def join_kernel(
    lists,
    mid_ref,
    got_ref,
    gave_ref,
    right_ref,
    freq_ref,
    slow_hbm,
    full_ref,
    cos_ref,
    sin_ref,
    out_ref,
    echo_ref,
    slow_ref,
    sems,
):
    copies = fetch([(slow_hbm, slow_ref)], sems)
    length = got_ref.shape[1]
    span = length - HALF
    tile = mid_ref.shape[1]
    odd_x = lists.odd_x

    def halves(ref, rows):
        return [
            [ref[part, rows, col * length : (col + 1) * length] for part in range(2)]
            for col in range(2)
        ]

    mine = jnp.where(odd_x == 0, 1, 0)
    beyond = jnp.where(odd_x == 0, 2, -1)
    groups = [lists.group_at(lists.window(mine, col)) for col in range(2)]
    turn(halves(got_ref, slice(None)), right_ref, groups, out_ref)
    groups = [lists.group_at(lists.window(beyond, col)) for col in range(2)]
    turn(halves(gave_ref, pl.ds(start_of(odd_x, 0, span), HALF)), right_ref, groups, echo_ref)
    source = start_of(odd_x, 0, HALF)
    target = start_of(odd_x, tile - span, 0)
    row_e = start_of(odd_x, tile - HALF, 0)
    full_ref[...] = mid_ref[...]
    for part in range(2):
        full_ref[part, pl.ds(target, span)] += out_ref[part, pl.ds(source, span)]
        full_ref[part, pl.ds(row_e, HALF)] += echo_ref[part]
    copies[0].wait()
    phase(freq_ref, slow_ref, cos_ref, sin_ref)


def add_rows(work_ref, rows_e_ref, rows_o_ref):
    tile, lanes = work_ref.shape[1:]
    odd_x = parity("gx")
    row_e, row_o = start_of(odd_x, tile - HALF, 0), start_of(odd_x, 0, tile - HALF)
    for part in range(2):
        work_ref[part, pl.ds(row_e, HALF)] += rows_e_ref[part, :, :lanes].astype(F32)
        work_ref[part, pl.ds(row_o, HALF)] += rows_o_ref[part, :, :lanes].astype(F32)


def border_kernel(full_ref, rows_e_ref, rows_o_ref, send_e_ref, send_o_ref, work_ref):
    tile = full_ref.shape[1]
    work_ref[...] = full_ref[...]
    add_rows(work_ref, rows_e_ref, rows_o_ref)
    at = tile % 128
    for part in range(2):
        turned = work_ref[part].T
        west = turned[at : at + HALF].astype(BF16)
        east = turned[at + HALF : at + OVER].astype(BF16)

        def store(near, away):
            send_e_ref[part] = near
            send_o_ref[part] = away

        each_way(parity("gy"), lambda: store(east, west), lambda: store(west, east))


def final_kernel(
    full_ref,
    rows_e_ref,
    rows_o_ref,
    cols_e_ref,
    cols_o_ref,
    cos_ref,
    sin_ref,
    result_ref,
    work_ref,
):
    tile = full_ref.shape[1]
    odd_y = parity("gy")
    far = tile - HALF
    lane = lax.broadcasted_iota(jnp.int32, (HALF, tile), 1)
    line = lax.broadcasted_iota(jnp.int32, (HALF, tile), 0)
    pick_e = (lane == line + jnp.where(odd_y == 0, far, 0)).astype(F32).astype(BF16)
    pick_o = (lane == line + jnp.where(odd_y == 0, 0, far)).astype(F32).astype(BF16)

    def outer(values, pick):
        return lax.dot_general(values, pick, (((0,), (0,)), ((), ())), preferred_element_type=F32)

    for part in range(2):
        work_ref[part] = (
            full_ref[part, :, :tile]
            + outer(cols_e_ref[part], pick_e)
            + outer(cols_o_ref[part], pick_o)
        )
    add_rows(work_ref, rows_e_ref, rows_o_ref)
    real, imag = work_ref[0], work_ref[1]
    result_ref[0, 0] = (real * cos_ref[...] - imag * sin_ref[...]).astype(BF16)
    result_ref[1, 0] = (real * sin_ref[...] + imag * cos_ref[...]).astype(BF16)


def phase(freq_ref, slow_ref, cos_ref, sin_ref):
    angle = freq_ref[0] * slow_ref[...]
    turns = jnp.round(angle * (2.0 / math.pi))
    rest = angle - turns * 1.5703125
    rest = rest - turns * 4.8375129699707031e-4
    rest = rest - turns * 7.5495138331e-8
    square = rest * rest
    sine = rest + rest * square * (
        -1.6666654611e-1 + square * (8.3321608736e-3 - square * 1.9515295891e-4)
    )
    cosine = 1.0 - 0.5 * square + square * square * (
        4.166664568298827e-2 + square * (-1.388731625493765e-3 + square * 2.443315711809948e-5)
    )
    quarter = turns.astype(jnp.int32) & 3
    crossed = (quarter & 1) == 1
    sin_value = jnp.where(crossed, cosine, sine)
    cos_value = jnp.where(crossed, sine, cosine)
    sin_ref[...] = jnp.where(quarter >= 2, -sin_value, sin_value)
    cos_ref[...] = jnp.where((quarter == 1) | (quarter == 2), -cos_value, cos_value)


def per_device(
    wavefield, slowness, frequencies, propagator, window_velocity_group, reach_list, coupling
):
    length = propagator.shape[-1]
    span = length - HALF
    wide = 2 * length
    tile_rows, tile_cols = wavefield.shape[2:]
    slots = reach_list.shape[2]

    def shape(*dims, kind=BF16):
        return pltpu.VMEM(dims, kind)

    x_send, rim_send = pl.pallas_call(
        rows_kernel,
        out_shape=(shape(2, span + HALF, tile_cols), shape(2, HALF, tile_cols)),
        in_specs=[VMEM],
        out_specs=(VMEM,) * 2,
        compiler_params=PARAMS,
        cost_estimate=cost(0.5),
        name="rows",
    )(wavefield)
    x_odd = swap(x_send, "gx", True)
    near, far = pl.pallas_call(
        cols_kernel,
        out_shape=(shape(2, tile_rows, span),) * 2,
        in_specs=[VMEM] * 2,
        out_specs=(VMEM,) * 2,
        compiler_params=PARAMS,
        cost_estimate=cost(0.5),
        name="cols",
    )(wavefield, rim_send)
    y_far = swap(far, "gy", True)
    y_near = swap(near, "gy", False)
    rim = swap(rim_send, "gx", False)

    left, right, strip, table = fold(
        propagator,
        cosine_table(length),
        bell_curve(length, OVER),
        reach_list,
        coupling,
        window_velocity_group,
    )

    def call(kernel, name, micros, out_shape, inputs, scratch=(), **options):
        def body(*refs):
            kernel(Lists(refs[0], slots), *refs[1:])

        specs = options.pop("in_specs", [VMEM] * len(inputs))
        outs = options.pop("out_specs", jax.tree.map(lambda _: VMEM, out_shape))
        return pl.pallas_call(
            body,
            out_shape=out_shape,
            in_specs=[SMEM] + specs,
            out_specs=outs,
            scratch_shapes=list(scratch),
            compiler_params=PARAMS,
            name=name,
            cost_estimate=cost(micros),
            **options,
        )(table, *inputs)

    blocks, given = call(
        edge_kernel,
        "edge",
        0.001,
        (shape(4, 4, 2, length, length), shape(2, length, wide)),
        (wavefield, y_near, y_far, left),
        (pltpu.VMEM((4, 2, tile_rows, length), BF16), pltpu.VMEM((2, length, length), F32)),
    )
    got = swap(given, "gx", False)

    def early(c):
        return call(
            functools.partial(early_kernel, c=c),
            "early",
            2,
            (
                shape(2, 2, length, length, kind=F32),
                shape(2, 2, length, slots * OVER),
            ),
            (blocks, left, strip),
        )

    early_e = early(1)
    early_o = early(0)
    x_odd, rim, _ = lax.optimization_barrier((x_odd, rim, given))
    near, far = pl.pallas_call(
        corner_kernel,
        out_shape=(shape(2, span + HALF, span),) * 2,
        in_specs=[VMEM, VMEM],
        out_specs=(VMEM, VMEM),
        compiler_params=PARAMS,
        cost_estimate=cost(0.5),
        name="corner",
    )(x_odd, rim)
    z_far = swap(far, "gy", True)
    z_near = swap(near, "gy", False)
    mid, send_e, send_o = call(
        late_kernel,
        "late",
        4,
        (shape(2, tile_rows, wide, kind=F32), shape(2, HALF, wide), shape(2, HALF, wide)),
        (x_odd, rim, z_near, z_far, left, *early_o, *early_e, right),
        (
            pltpu.VMEM((4, 2, length, length), BF16),
            pltpu.VMEM((2, 4, 2, OVER, length), BF16),
            pltpu.VMEM((2, 2, 2, length, length), F32),
            pltpu.VMEM((2, length, wide), F32),
        ),
    )
    rows_o = swap(send_o, "gx", True)
    rows_e = swap(send_e, "gx", False)

    full, cos_phase, sin_phase = call(
        join_kernel,
        "join",
        3,
        (
            shape(2, tile_rows, wide, kind=F32),
            shape(tile_rows, tile_cols, kind=F32),
            shape(tile_rows, tile_cols, kind=F32),
        ),
        (mid, got, given, right, frequencies, slowness),
        (
            pltpu.VMEM((2, length, wide), F32),
            pltpu.VMEM((2, HALF, wide), F32),
            pltpu.VMEM((tile_rows, tile_cols), F32),
            pltpu.SemaphoreType.DMA((1,)),
        ),
        in_specs=[VMEM] * 4 + [SMEM, HBM],
    )
    last = tile_cols // 128
    side = pl.BlockSpec((2, HALF, 128), lambda i: (0, 0, last))
    send_e, send_o = pl.pallas_call(
        border_kernel,
        grid=(1,),
        out_shape=(shape(2, HALF, tile_rows),) * 2,
        in_specs=[pl.BlockSpec((2, tile_rows, 128), lambda i: (0, 0, last)), side, side],
        out_specs=(pl.BlockSpec((2, HALF, tile_rows), lambda i: (0, 0, 0)),) * 2,
        scratch_shapes=[pltpu.VMEM((2, tile_rows, 128), F32)],
        compiler_params=PARAMS,
        cost_estimate=cost(0.5),
        name="border",
    )(full, rows_e, rows_o)
    cols_o = swap(send_o, "gy", True)
    cols_e = swap(send_e, "gy", False)
    return pl.pallas_call(
        final_kernel,
        out_shape=jax.ShapeDtypeStruct(wavefield.shape, BF16),
        in_specs=[VMEM] * 7,
        out_specs=VMEM,
        scratch_shapes=[pltpu.VMEM((2, tile_rows, tile_cols), F32)],
        compiler_params=PARAMS,
        cost_estimate=cost(1.5),
        name="final",
    )(full, rows_e, rows_o, cols_e, cols_o, cos_phase, sin_phase)


def solution(mesh):
    return jax.shard_map(
        per_device,
        mesh=mesh,
        in_specs=(P(None, None, "gx", "gy"), P("gx", "gy"), P(), P(), P(), P(), P()),
        out_specs=P(None, None, "gx", "gy"),
        check_vma=False,
    )
```

time: 72.5 us -> 48 us (0.66)
  waiting for transfers between devices: 23 us -> 3.76 us
  other arithmetic: 6.79 us -> 0 us
  Pallas kernels: 15.2 us -> 21.4 us
  local copies, waits for them, and re-layouts: 7.15 us -> 1.23 us
  starting transfers between devices: 18.7 us -> 20 us
    ppermute x10 -> x11, waiting for transfers between devices: 23 us -> 3.76 us  [swap(): return lax.ppermute(block, axis, pairs)]
    pallas_call x3 -> x10, Pallas kernels: 13.4 us -> 19.5 us  [the longest x5 15.7 us: call(): pl.pallas_call(body, out_shape=out_shape, in_specs=[SMEM] + specs, out_sp...]
    unnamed x28 -> x20, local copies, waits for them, and re-layouts: 5.59 us -> 1.23 us
    select_n x3 -> x0, other arithmetic: 3.56 us -> none  [pick_side(): return jnp.where(toward_last, last, first)]
    sin x1 -> x0, other arithmetic: 3.23 us -> none  [per_device(): jnp.sin(phases)]
    reshape x3 -> x0, local copies, waits for them, and re-layouts: 1.52 us -> none  [the longest x1 1.24 us: per_device(): coupling.reshape(-1)]
    ppermute x10 -> x11, starting transfers between devices: 18.7 us -> 20 us  [swap(): return lax.ppermute(block, axis, pairs)]
  transfers between devices with their start and end apart: 10 -> 11, of which waited for: 3 -> 2; matrix products, arithmetic and copies ran while one was open for 10% -> 0% of each run, Pallas kernels for 2% -> 40%
where the time goes in v2:
time: 48 us; the launch traced here: 47.4 us
  Pallas kernels  21.4 us (45%)
  starting transfers between devices  20 us (42%)
  waiting for transfers between devices  3.76 us (8%)
  local copies, waits for them, and re-layouts  1.23 us (3%)
  between operations  0.91 us (2%)
    ppermute x11, starting transfers between devices, swap(): return lax.ppermute(block, axis, pairs)  20 us
    pallas_call x5, Pallas kernels, call(): pl.pallas_call(body, out_shape=out_shape, in_specs=[SMEM] + specs, out_sp...  15.7 us
    ppermute x11, waiting for transfers between devices, swap(): return lax.ppermute(block, axis, pairs)  3.76 us
    pallas_call x1, Pallas kernels, fold(): pl.pallas_call(folded_kernel, out_shape=(pltpu.VMEM((groups, 2, length, l...  2.81 us
    pallas_call x1, Pallas kernels, per_device(): pl.pallas_call(final_kernel, out_shape=jax.ShapeDtypeStruct(wavefield.sha...  1.95 us
    unnamed x20, local copies, waits for them, and re-layouts  1.23 us
  transfers between devices with their start and end apart: 11, of which 2 were waited for; matrix products, arithmetic and copies ran while one was open for 0% of the time, Pallas kernels for 40%

profile of v2, /device:TPU:9, one launch (start us, length us, event | category | flops | bytes accessed | tf_op | source)
XLA Modules:
  0.0 47.4 jit_solution(17045774218678743636)
XLA Ops:
  0.0 1.2 %copy-done = bf16[2,1,448,448]{3,2,1,0:T(8,128)(2,1)S(1)} copy-done((bf16[2,1,448,448]{3,2,1,0:T(8,128)(2,1)S(1)}, bf16[2,1,448,448]{3,2,1,0:T(8,128)(2,1)}, u32[]{:S(2)}) %copy-start) | copy-done | bytes 802840
  1.2 0.0 copy-start.7
  1.2 0.0 copy-start.8
  1.2 0.0 copy-start.9
  1.2 0.1 rows.1
  1.3 3.2 %collective-permute-start = (bf16[2,256,448]{2,1,0:T(8,128)(2,1)S(1)}, bf16[2,256,448]{2,1,0:T(8,128)(2,1)S(1)}, u32[]{:S(2)}, u32[]{:S(2)}) collective-permute-start(bf16[2,256,448]{2,1,0:T(8,128)(2,1)S(1)} %get-tuple-element.32), channel_id=1, source_target_pairs={{4,8},{8,4},{12,16},{16,12},{20,24},{24,20},{5,9},{9,5},{13,17},{1... | collective-permute-start | bytes 1376264 | tf_op jit(solution)/shard_map/ppermute | solution.py:47
  4.5 0.4 cols.1
  4.9 1.0 %collective-permute-start.2 = (bf16[2,448,240]{2,1,0:T(8,128)(2,1)S(1)}, bf16[2,448,240]{2,1,0:T(8,128)(2,1)S(1)}, u32[]{:S(2)}, u32[]{:S(2)}) collective-permute-start(bf16[2,448,240]{2,1,0:T(8,128)(2,1)S(1)} %get-tuple-element.34), channel_id=1, source_target_pairs={{0,1},{1,0},{2,3},{3,2},{4,5},{5,4},{6,7},{7,6},{8,9},{9,8},{10,11... | collective-permute-start | bytes 1290248 | tf_op jit(solution)/shard_map/ppermute | solution.py:47
  5.9 3.0 %collective-permute-start.3 = (bf16[2,448,240]{2,1,0:T(8,128)(2,1)S(1)}, bf16[2,448,240]{2,1,0:T(8,128)(2,1)S(1)}, u32[]{:S(2)}, u32[]{:S(2)}) collective-permute-start(bf16[2,448,240]{2,1,0:T(8,128)(2,1)S(1)} %get-tuple-element.35), channel_id=1, source_target_pairs={{1,2},{2,1},{5,6},{6,5},{9,10},{10,9},{13,14},{14,13},{17,18},{18,... | collective-permute-start | bytes 1290248 | tf_op jit(solution)/shard_map/ppermute | solution.py:47
  8.9 1.4 %collective-permute-start.1 = (bf16[2,16,448]{2,1,0:T(8,128)(2,1)S(1)}, bf16[2,16,448]{2,1,0:T(8,128)(2,1)S(1)}, u32[]{:S(2)}, u32[]{:S(2)}) collective-permute-start(bf16[2,16,448]{2,1,0:T(8,128)(2,1)S(1)} %get-tuple-element.33.rim_ref), channel_id=1, source_target_pairs={{0,4},{4,0},{8,12},{12,8},{16,20},{20,16},{24,28},{28,24},{1,5},{5... | collective-permute-start | bytes 86024 | tf_op jit(solution)/shard_map/ppermute | solution.py:47
  10.3 0.0 copy-done.3
  10.3 0.0 copy-done.4
  10.3 0.0 copy-done.5
  10.3 0.0 copy-done.6
  10.3 0.0 copy-done.7
  10.3 0.0 copy-done.8
  10.4 0.0 copy-done.9
  10.4 0.0 copy-start.1
  10.4 2.8 %fold.1 = (f32[3,2,256,256]{3,2,1,0:T(8,128)S(1)}, bf16[3,2,2,256,512]{4,3,2,1,0:T(8,128)(2,1)S(1)}, f32[3,2,256,32]{3,2,1,0:T(8,128)S(1)}, f32[106]{0:T(128)S(1)}) custom-call(s32[5,8,16]{2,1,0:T(8,128)S(1)} %bitcast.4, f32[8,5,2,16]{3,2,1,0:T(2,128)S(1)} %bitcast.3, s32[8,16]{1,0:T(8,128)S(1)} %bitcast.5, bf16[3,1,2,256,256]{4,3,2,1,0:T(8,128)(2,1)S(1)} %copy-done.3, ...), custom_call_target="tpu_custom_call" | custom-call | flops 2200000000 | bytes 7200000 | tf_op jit(solution)/shard_map/fold/pallas_call | solution.py:151
  13.8 0.0 collective-permute-done.2.refs_2_
  13.8 2.1 %collective-permute-done.3.refs_3_ = bf16[2,448,240]{2,1,0:T(8,128)(2,1)S(1)} collective-permute-done((bf16[2,448,240]{2,1,0:T(8,128)(2,1)S(1)}, bf16[2,448,240]{2,1,0:T(8,128)(2,1)S(1)}, u32[]{:S(2)}, u32[]{:S(2)}) %collective-permute-start.3) | collective-permute-done | bytes 430112 | tf_op jit(solution)/shard_map/ppermute | solution.py:47
  16.0 0.0 copy-done.1
  16.0 2.6 %edge.1 = (bf16[4,4,2,256,256]{4,3,2,1,0:T(8,128)(2,1)S(1)}, bf16[2,256,512]{2,1,0:T(8,128)(2,1)S(1)}) custom-call(f32[106]{0:T(128)S(1)} %get-tuple-element.31.refs_0_, bf16[2,1,448,448]{3,2,1,0:T(8,128)(2,1)S(1)} %copy-done.1, bf16[2,448,240]{2,1,0:T(8,128)(2,1)S(1)} %collective-permute-done.2.refs_2_, ...), custom_call_target="tpu_custom_call" | custom-call | flops 1100000 | bytes 3600 | tf_op jit(solution)/shard_map/edge/pallas_call | solution.py:619
  18.6 1.4 %collective-permute-start.6 = (bf16[2,256,512]{2,1,0:T(8,128)(2,1)S(1)}, bf16[2,256,512]{2,1,0:T(8,128)(2,1)S(1)}, u32[]{:S(2)}, u32[]{:S(2)}) collective-permute-start(bf16[2,256,512]{2,1,0:T(8,128)(2,1)S(1)} %get-tuple-element.37.refs_3_), channel_id=1, source_target_pairs={{0,4},{4,0},{8,12},{12,8},{16,20},{20,16},{24,28},{28,24},{1,5},{5... | collective-permute-start | bytes 1572872 | tf_op jit(solution)/shard_map/ppermute | solution.py:47
  20.0 0.0 collective-permute-done.1.rim_ref.refs_2_
  20.0 0.0 collective-permute-done.x_ref.refs_1_
  20.0 0.3 corner.1
  20.3 0.1 collective-permute-start.4
  20.4 3.0 %collective-permute-start.5 = (bf16[2,256,240]{2,1,0:T(8,128)(2,1)S(1)}, bf16[2,256,240]{2,1,0:T(8,128)(2,1)S(1)}, u32[]{:S(2)}, u32[]{:S(2)}) collective-permute-start(bf16[2,256,240]{2,1,0:T(8,128)(2,1)S(1)} %get-tuple-element.41), channel_id=1, source_target_pairs={{1,2},{2,1},{5,6},{6,5},{9,10},{10,9},{13,14},{14,13},{17,18},{18,... | collective-permute-start | bytes 737288 | tf_op jit(solution)/shard_map/ppermute | solution.py:47
  23.4 2.5 %early.3 = (f32[2,2,256,256]{3,2,1,0:T(8,128)S(1)}, bf16[2,2,256,160]{3,2,1,0:T(8,128)(2,1)S(1)}) custom-call(f32[106]{0:T(128)S(1)} %get-tuple-element.31.refs_0_, bf16[4,4,2,256,256]{4,3,2,1,0:T(8,128)(2,1)S(1)} %get-tuple-element.42.refs_1_, f32[3,2,256,256]{3,2,1,0:T(8,128)S(1)} %get-tuple-element.36.refs_4_.refs_2_.refs_5_, ...), custom_call_target="tpu_custom_call" | custom-call | flops 2200000000 | bytes 7200000 | tf_op jit(solution)/shard_map/early/pallas_call | solution.py:619
  25.9 2.5 %early.2 = (f32[2,2,256,256]{3,2,1,0:T(8,128)S(1)}, bf16[2,2,256,160]{3,2,1,0:T(8,128)(2,1)S(1)}) custom-call(f32[106]{0:T(128)S(1)} %get-tuple-element.31.refs_0_, bf16[4,4,2,256,256]{4,3,2,1,0:T(8,128)(2,1)S(1)} %get-tuple-element.42.refs_1_, f32[3,2,256,256]{3,2,1,0:T(8,128)S(1)} %get-tuple-element.36.refs_4_.refs_2_.refs_5_, ...), custom_call_target="tpu_custom_call" | custom-call | flops 2200000000 | bytes 7200000 | tf_op jit(solution)/shard_map/early/pallas_call | solution.py:619
  28.4 0.0 collective-permute-done.4.refs_3_
  28.4 0.0 collective-permute-done.5.refs_4_
  28.4 0.0 copy-start.2
  28.4 4.7 %late.1 = (f32[2,448,512]{2,1,0:T(8,128)S(1)}, bf16[2,16,512]{2,1,0:T(8,128)(2,1)S(1)}, bf16[2,16,512]{2,1,0:T(8,128)(2,1)S(1)}) custom-call(f32[106]{0:T(128)S(1)} %get-tuple-element.31.refs_0_, bf16[2,256,448]{2,1,0:T(8,128)(2,1)S(1)} %collective-permute-done.x_ref.refs_1_, bf16[2,16,448]{2,1,0:T(8,128)(2,1)S(1)} %collective-permute-done.1.rim_ref.refs_2_, ...), custom_call_target="tpu_custom_call" | custom-call | flops 4400000000 | bytes 14400000 | tf_op jit(solution)/shard_map/late/pallas_call | solution.py:619
  33.1 0.6 %collective-permute-start.7 = (bf16[2,16,512]{2,1,0:T(8,128)(2,1)S(1)}, bf16[2,16,512]{2,1,0:T(8,128)(2,1)S(1)}, u32[]{:S(2)}, u32[]{:S(2)}) collective-permute-start(bf16[2,16,512]{2,1,0:T(8,128)(2,1)S(1)} %get-tuple-element.51), channel_id=1, source_target_pairs={{0,4},{4,0},{8,12},{12,8},{16,20},{20,16},{24,28},{28,24},{1,5},{5... | collective-permute-start | bytes 98312 | tf_op jit(solution)/shard_map/ppermute | solution.py:47
  33.7 2.7 %collective-permute-start.8 = (bf16[2,16,512]{2,1,0:T(8,128)(2,1)S(1)}, bf16[2,16,512]{2,1,0:T(8,128)(2,1)S(1)}, u32[]{:S(2)}, u32[]{:S(2)}) collective-permute-start(bf16[2,16,512]{2,1,0:T(8,128)(2,1)S(1)} %get-tuple-element.52), channel_id=1, source_target_pairs={{4,8},{8,4},{12,16},{16,12},{20,24},{24,20},{5,9},{9,5},{13,17},{1... | collective-permute-start | bytes 98312 | tf_op jit(solution)/shard_map/ppermute | solution.py:47
  36.4 0.0 collective-permute-done.6.refs_2_
  36.4 0.0 copy-done.2
  36.4 3.4 %join.1 = (f32[2,448,512]{2,1,0:T(8,128)S(1)}, f32[448,448]{1,0:T(8,128)S(1)}, f32[448,448]{1,0:T(8,128)S(1)}) custom-call(f32[106]{0:T(128)S(1)} %get-tuple-element.31.refs_0_, f32[2,448,512]{2,1,0:T(8,128)S(1)} %get-tuple-element.49.refs_1_, bf16[2,256,512]{2,1,0:T(8,128)(2,1)S(1)} %collective-permute-done.6.refs_2_, ...), custom_call_target="tpu_custom_call" | custom-call | flops 3300000000 | bytes 10800000 | tf_op jit(solution)/shard_map/join/pallas_call | solution.py:619
  39.8 0.0 collective-permute-done.7.rows_e_ref
  39.9 0.0 collective-permute-done.8.rows_o_ref
  39.9 0.3 border.1
  40.2 3.5 %collective-permute-start.10 = (bf16[2,16,448]{2,1,0:T(8,128)(2,1)S(1)}, bf16[2,16,448]{2,1,0:T(8,128)(2,1)S(1)}, u32[]{:S(2)}, u32[]{:S(2)}) collective-permute-start(bf16[2,16,448]{2,1,0:T(8,128)(2,1)S(1)} %get-tuple-element.54), channel_id=1, source_target_pairs={{1,2},{2,1},{5,6},{6,5},{9,10},{10,9},{13,14},{14,13},{17,18},{18,... | collective-permute-start | bytes 86024 | tf_op jit(solution)/shard_map/ppermute | solution.py:47
  43.7 0.1 collective-permute-start.9
  43.8 1.6 %collective-permute-done.10.cols_o_ref = bf16[2,16,448]{2,1,0:T(8,128)(2,1)S(1)} collective-permute-done((bf16[2,16,448]{2,1,0:T(8,128)(2,1)S(1)}, bf16[2,16,448]{2,1,0:T(8,128)(2,1)S(1)}, u32[]{:S(2)}, u32[]{:S(2)}) %collective-permute-start.10) | collective-permute-done | bytes 28704 | tf_op jit(solution)/shard_map/ppermute | solution.py:47
  45.4 0.0 collective-permute-done.9.cols_e_ref
  45.4 2.0 %final.1 = bf16[2,1,448,448]{3,2,1,0:T(8,128)(2,1)} custom-call(f32[2,448,512]{2,1,0:T(8,128)S(1)} %get-tuple-element.50.full_ref, bf16[2,16,512]{2,1,0:T(8,128)(2,1)S(1)} %collective-permute-done.7.rows_e_ref, bf16[2,16,512]{2,1,0:T(8,128)(2,1)S(1)} %collective-permute-done.8.rows_o_ref, bf16[2,16,448]{2,1,0:T(8,128)(2,1)S(1)} %collective-permute-done.9.cols_e_ref, ...), custom_call_target="tpu_custom_call" | custom-call | flops 1650000000 | bytes 5400000 | tf_op jit(solution)/shard_map/final/pallas_call | solution.py:716
  (5 shorter events, 0.0 us)
Async XLA Ops:
  0.0 1.2 %copy-start = (bf16[2,1,448,448]{3,2,1,0:T(8,128)(2,1)S(1)}, bf16[2,1,448,448]{3,2,1,0:T(8,128)(2,1)}, u32[]{:S(2)}) copy-start(bf16[2,1,448,448]{3,2,1,0:T(8,128)(2,1)} %refs_1_.1) | copy-start | bytes 2408452
  1.2 9.1 %copy-start.3 = (bf16[3,1,2,256,256]{4,3,2,1,0:T(8,128)(2,1)S(1)}, bf16[3,1,2,256,256]{4,3,2,1,0:T(8,128)(2,1)}, u32[]{:S(2)}) copy-start(bf16[3,1,2,256,256]{4,3,2,1,0:T(8,128)(2,1)} %prop_ref.1) | copy-start | bytes 2359300
  1.2 9.1 %copy-start.4 = (f32[16,8,5,2]{0,3,2,1:T(2,128)S(1)}, f32[16,8,5,2]{0,3,2,1:T(2,128)}, u32[]{:S(2)}) copy-start(f32[16,8,5,2]{0,3,2,1:T(2,128)} %param.16) | copy-start | bytes 15364
  1.2 9.1 %copy-start.5 = (s32[16,8,5]{0,1,2:T(8,128)S(1)}, s32[16,8,5]{0,1,2:T(8,128)}, u32[]{:S(2)}) copy-start(s32[16,8,5]{0,1,2:T(8,128)} %param.15) | copy-start | bytes 7684
  1.2 9.1 %copy-start.6 = (s32[16,8]{0,1:T(8,128)S(1)}, s32[16,8]{0,1:T(8,128)}, u32[]{:S(2)}) copy-start(s32[16,8]{0,1:T(8,128)} %param.14) | copy-start | bytes 1540
  1.2 9.1 %copy-start.7 = (bf16[256,256]{1,0:T(8,128)(2,1)S(1)}, bf16[256,256]{1,0:T(8,128)(2,1)}, u32[]{:S(2)}) copy-start(bf16[256,256]{1,0:T(8,128)(2,1)} %constant.6.clone.cos_ref) | copy-start | bytes 393220
  1.2 9.1 %copy-start.8 = (bf16[256,256]{1,0:T(8,128)(2,1)S(1)}, bf16[256,256]{1,0:T(8,128)(2,1)}, u32[]{:S(2)}) copy-start(bf16[256,256]{1,0:T(8,128)(2,1)} %constant.7.clone.cos_t_ref) | copy-start | bytes 393220
  1.2 9.1 %copy-start.9 = (f32[1,256]{1,0:T(1,128)S(1)}, f32[1,256]{1,0:T(1,128)}, u32[]{:S(2)}) copy-start(f32[1,256]{1,0:T(1,128)} %constant.8.clone.row_ref) | copy-start | bytes 3076
  1.3 18.8 %collective-permute-start = (bf16[2,256,448]{2,1,0:T(8,128)(2,1)S(1)}, bf16[2,256,448]{2,1,0:T(8,128)(2,1)S(1)}, u32[]{:S(2)}, u32[]{:S(2)}) collective-permute-start(bf16[2,256,448]{2,1,0:T(8,128)(2,1)S(1)} %get-tuple-element.32), channel_id=1, source_target_pairs={{4,8},{8,4},{12,16},{16,12},{20,24},{24,20},{5,9},{9,5},{13,17},{1... | collective-permute-start | bytes 1376264 | tf_op jit(solution)/shard_map/ppermute | solution.py:47
  4.9 9.0 %collective-permute-start.2 = (bf16[2,448,240]{2,1,0:T(8,128)(2,1)S(1)}, bf16[2,448,240]{2,1,0:T(8,128)(2,1)S(1)}, u32[]{:S(2)}, u32[]{:S(2)}) collective-permute-start(bf16[2,448,240]{2,1,0:T(8,128)(2,1)S(1)} %get-tuple-element.34), channel_id=1, source_target_pairs={{0,1},{1,0},{2,3},{3,2},{4,5},{5,4},{6,7},{7,6},{8,9},{9,8},{10,11... | collective-permute-start | bytes 1290248 | tf_op jit(solution)/shard_map/ppermute | solution.py:47
  5.9 10.1 %collective-permute-start.3 = (bf16[2,448,240]{2,1,0:T(8,128)(2,1)S(1)}, bf16[2,448,240]{2,1,0:T(8,128)(2,1)S(1)}, u32[]{:S(2)}, u32[]{:S(2)}) collective-permute-start(bf16[2,448,240]{2,1,0:T(8,128)(2,1)S(1)} %get-tuple-element.35), channel_id=1, source_target_pairs={{1,2},{2,1},{5,6},{6,5},{9,10},{10,9},{13,14},{14,13},{17,18},{18,... | collective-permute-start | bytes 1290248 | tf_op jit(solution)/shard_map/ppermute | solution.py:47
  8.9 11.1 %collective-permute-start.1 = (bf16[2,16,448]{2,1,0:T(8,128)(2,1)S(1)}, bf16[2,16,448]{2,1,0:T(8,128)(2,1)S(1)}, u32[]{:S(2)}, u32[]{:S(2)}) collective-permute-start(bf16[2,16,448]{2,1,0:T(8,128)(2,1)S(1)} %get-tuple-element.33.rim_ref), channel_id=1, source_target_pairs={{0,4},{4,0},{8,12},{12,8},{16,20},{20,16},{24,28},{28,24},{1,5},{5... | collective-permute-start | bytes 86024 | tf_op jit(solution)/shard_map/ppermute | solution.py:47
  10.4 5.6 %copy-start.1 = (bf16[2,1,448,448]{3,2,1,0:T(8,128)(2,1)S(1)}, bf16[2,1,448,448]{3,2,1,0:T(8,128)(2,1)}, u32[]{:S(2)}) copy-start(bf16[2,1,448,448]{3,2,1,0:T(8,128)(2,1)} %refs_1_.1) | copy-start | bytes 2408452
  18.6 17.8 %collective-permute-start.6 = (bf16[2,256,512]{2,1,0:T(8,128)(2,1)S(1)}, bf16[2,256,512]{2,1,0:T(8,128)(2,1)S(1)}, u32[]{:S(2)}, u32[]{:S(2)}) collective-permute-start(bf16[2,256,512]{2,1,0:T(8,128)(2,1)S(1)} %get-tuple-element.37.refs_3_), channel_id=1, source_target_pairs={{0,4},{4,0},{8,12},{12,8},{16,20},{20,16},{24,28},{28,24},{1,5},{5... | collective-permute-start | bytes 1572872 | tf_op jit(solution)/shard_map/ppermute | solution.py:47
  20.3 8.1 %collective-permute-start.4 = (bf16[2,256,240]{2,1,0:T(8,128)(2,1)S(1)}, bf16[2,256,240]{2,1,0:T(8,128)(2,1)S(1)}, u32[]{:S(2)}, u32[]{:S(2)}) collective-permute-start(bf16[2,256,240]{2,1,0:T(8,128)(2,1)S(1)} %get-tuple-element.40), channel_id=1, source_target_pairs={{0,1},{1,0},{2,3},{3,2},{4,5},{5,4},{6,7},{7,6},{8,9},{9,8},{10,11... | collective-permute-start | bytes 737288 | tf_op jit(solution)/shard_map/ppermute | solution.py:47
  20.4 8.0 %collective-permute-start.5 = (bf16[2,256,240]{2,1,0:T(8,128)(2,1)S(1)}, bf16[2,256,240]{2,1,0:T(8,128)(2,1)S(1)}, u32[]{:S(2)}, u32[]{:S(2)}) collective-permute-start(bf16[2,256,240]{2,1,0:T(8,128)(2,1)S(1)} %get-tuple-element.41), channel_id=1, source_target_pairs={{1,2},{2,1},{5,6},{6,5},{9,10},{10,9},{13,14},{14,13},{17,18},{18,... | collective-permute-start | bytes 737288 | tf_op jit(solution)/shard_map/ppermute | solution.py:47
  28.4 8.0 %copy-start.2 = (f32[448,448]{1,0:T(8,128)S(1)}, f32[448,448]{1,0:T(8,128)}, u32[]{:S(2)}) copy-start(f32[448,448]{1,0:T(8,128)} %refs_6_.1) | copy-start | bytes 2408452
  33.1 6.7 %collective-permute-start.7 = (bf16[2,16,512]{2,1,0:T(8,128)(2,1)S(1)}, bf16[2,16,512]{2,1,0:T(8,128)(2,1)S(1)}, u32[]{:S(2)}, u32[]{:S(2)}) collective-permute-start(bf16[2,16,512]{2,1,0:T(8,128)(2,1)S(1)} %get-tuple-element.51), channel_id=1, source_target_pairs={{0,4},{4,0},{8,12},{12,8},{16,20},{20,16},{24,28},{28,24},{1,5},{5... | collective-permute-start | bytes 98312 | tf_op jit(solution)/shard_map/ppermute | solution.py:47
  33.7 6.1 %collective-permute-start.8 = (bf16[2,16,512]{2,1,0:T(8,128)(2,1)S(1)}, bf16[2,16,512]{2,1,0:T(8,128)(2,1)S(1)}, u32[]{:S(2)}, u32[]{:S(2)}) collective-permute-start(bf16[2,16,512]{2,1,0:T(8,128)(2,1)S(1)} %get-tuple-element.52), channel_id=1, source_target_pairs={{4,8},{8,4},{12,16},{16,12},{20,24},{24,20},{5,9},{9,5},{13,17},{1... | collective-permute-start | bytes 98312 | tf_op jit(solution)/shard_map/ppermute | solution.py:47
  40.2 5.2 %collective-permute-start.10 = (bf16[2,16,448]{2,1,0:T(8,128)(2,1)S(1)}, bf16[2,16,448]{2,1,0:T(8,128)(2,1)S(1)}, u32[]{:S(2)}, u32[]{:S(2)}) collective-permute-start(bf16[2,16,448]{2,1,0:T(8,128)(2,1)S(1)} %get-tuple-element.54), channel_id=1, source_target_pairs={{1,2},{2,1},{5,6},{6,5},{9,10},{10,9},{13,14},{14,13},{17,18},{18,... | collective-permute-start | bytes 86024 | tf_op jit(solution)/shard_map/ppermute | solution.py:47
  43.7 1.7 %collective-permute-start.9 = (bf16[2,16,448]{2,1,0:T(8,128)(2,1)S(1)}, bf16[2,16,448]{2,1,0:T(8,128)(2,1)S(1)}, u32[]{:S(2)}, u32[]{:S(2)}) collective-permute-start(bf16[2,16,448]{2,1,0:T(8,128)(2,1)S(1)} %get-tuple-element.53), channel_id=1, source_target_pairs={{0,1},{1,0},{2,3},{3,2},{4,5},{5,4},{6,7},{7,6},{8,9},{9,8},{10,11... | collective-permute-start | bytes 86024 | tf_op jit(solution)/shard_map/ppermute | solution.py:47

commit v3 on v2

v3 whole, which is shorter than its diff:
```python
import functools
import math

import jax
import jax.numpy as jnp
import ml_dtypes
import numpy as np
from jax import lax
from jax.experimental import pallas as pl
from jax.experimental.pallas import tpu as pltpu
from jax.sharding import PartitionSpec as P

OVER = 32
HALF = OVER // 2
F32 = jnp.float32
BF16 = jnp.bfloat16
VMEM = pl.BlockSpec(memory_space=pltpu.VMEM)
SMEM = pl.BlockSpec(memory_space=pltpu.SMEM)
ANY = pl.BlockSpec(memory_space=pl.ANY)
PARAMS = pltpu.CompilerParams(vmem_limit_bytes=20 * 2**20)


def cosine_table(length):
    points = np.arange(length, dtype=np.float32) + np.float32(0.5)
    angles = (np.float32(math.pi / length) * points[:, None]) * points[None, :]
    waves = np.cos(angles.astype(np.float64)).astype(np.float32)
    return (np.sqrt(np.float32(2.0 / length)) * waves).astype(ml_dtypes.bfloat16)


def bell_curve(length, margin):
    points = np.arange(length, dtype=np.float64)
    rising = np.sin(0.5 * math.pi * (points + 0.5) / margin)
    falling = np.cos(0.5 * math.pi * (points - (length - margin) + 0.5) / margin)
    bell = np.where(points < margin, rising, np.where(points >= length - margin, falling, 1.0))
    return bell.astype(np.float32)


def dot(left, right):
    return jnp.dot(left, right, preferred_element_type=F32)


def swap(block, axis, odd):
    size = lax.axis_size(axis)
    pairs = []
    for i in range(1 if odd else 0, size - 1, 2):
        pairs += [(i, i + 1), (i + 1, i)]
    return lax.ppermute(block, axis, pairs)


def far_corner(block):
    across, along = (lax.axis_size(axis) for axis in ("gx", "gy"))
    pairs = []
    for x in range(1, across - 1, 2):
        for y in range(1, along - 1, 2):
            first, second = x * along + y, (x + 1) * along + y + 1
            third, fourth = x * along + y + 1, (x + 1) * along + y
            pairs += [(first, second), (second, first), (third, fourth), (fourth, third)]
    return lax.ppermute(block, ("gx", "gy"), pairs)


def parity(axis):
    return lax.rem(lax.axis_index(axis), 2)


def cost(micros):
    return pl.CostEstimate(
        flops=int(micros * 1.1e9), bytes_accessed=int(micros * 3.6e6), transcendentals=0
    )


def fetch(pairs, sems):
    copies = [pltpu.make_async_copy(a, b, sems.at[i]) for i, (a, b) in enumerate(pairs)]
    for copy in copies:
        copy.start()
    return copies


def list_tables(all_reach_ref, all_coup_ref, all_group_ref, table_ref):
    slots, total_y, total_x = all_reach_ref.shape
    odd_x = parity("gx")
    base_x = lax.axis_index("gx") * 2
    base_y = lax.axis_index("gy") * 2
    for row in range(4):
        for col in range(4):
            x = jnp.clip(base_x - 1 + row, 0, total_x - 1)
            y = jnp.clip(base_y - 1 + col, 0, total_y - 1)
            table_ref[row * 4 + col] = all_group_ref[y, x].astype(F32)
    for row in range(3):
        for col in range(2):
            x, y = base_x - odd_x + row, base_y + col
            for slot in range(slots):
                reach = all_reach_ref[slot, y, x]
                place = (lax.div(reach, total_y) - base_x + 1) * 4
                place += lax.rem(reach, total_y) - base_y + 1
                at = 16 + ((row * 2 + col) * slots + slot) * 3
                table_ref[at] = jnp.where(reach >= 0, place, -1).astype(F32)
                table_ref[at + 1] = all_coup_ref[col, slot, 0, x]
                table_ref[at + 2] = all_coup_ref[col, slot, 1, x]


def folded_kernel(
    reach_any,
    coup_any,
    group_any,
    prop_ref,
    cos_ref,
    cos_t_ref,
    row_ref,
    left_ref,
    strip_ref,
    table_any,
    reach_ref,
    coup_ref,
    group_ref,
    table_ref,
    sems,
):
    columns = pl.ds(lax.axis_index("gy") * 2, 2)
    pairs = ((reach_any, reach_ref), (coup_any.at[columns], coup_ref), (group_any, group_ref))
    copies = fetch(pairs, sems)
    out_copy = pltpu.make_async_copy(table_ref, table_any, sems.at[len(copies)])
    groups, _, _, length, _ = prop_ref.shape
    strip_ref[...] = jnp.zeros_like(strip_ref)
    curve = jnp.broadcast_to(row_ref[...], (length, length))
    bell = curve * curve.T
    edge = length - HALF
    for g in range(groups):
        if g == groups - 1:
            for copy in copies:
                copy.wait()
            list_tables(reach_ref, coup_ref, group_ref, table_ref)
            out_copy.start()
        for part in range(2):
            half = dot(prop_ref[g, 0, part], cos_ref[...])
            high = half.astype(BF16)
            low = (half - high.astype(F32)).astype(BF16)
            full = (dot(cos_t_ref[...], high) + dot(cos_t_ref[...], low)) * bell
            left_ref[g, part] = full.astype(BF16)
            strip = jnp.concatenate([full[:, :HALF], full[:, edge:]], axis=1).astype(BF16)
            low = slice(g * OVER, (g + 1) * OVER)
            high = slice(length // 2 + g * OVER, length // 2 + (g + 1) * OVER)
            strip_ref[part, :, low] = strip
            strip_ref[1 - part, :, high] = strip if part == 0 else -strip
    out_copy.wait()

def right_kernel(left_ref, _, right_ref):
    groups, _, length, _ = left_ref.shape
    wide = right_ref.shape[-1]
    inner = wide - 2 * OVER
    edge = length - HALF
    zeros = jnp.zeros((length, wide), BF16)
    for g in range(groups):
        for part in range(2):
            flipped = left_ref[g, part].astype(F32).T.astype(BF16)
            right_ref[g, 0, part] = jnp.concatenate(
                [
                    flipped[:, HALF:],
                    zeros[:, : inner - edge],
                    flipped[:, :HALF],
                    zeros[:, : wide - inner - HALF],
                ],
                axis=1,
            )
            right_ref[g, 1, part] = jnp.concatenate(
                [
                    zeros[:, : inner - edge],
                    flipped[:, :edge],
                    zeros[:, :HALF],
                    flipped[:, edge:],
                    zeros[:, : wide - inner - OVER],
                ],
                axis=1,
            )


def fold(propagator, cosines, bell, reach_list, coupling, window_velocity_group):
    groups, _, _, length, _ = propagator.shape
    slots = reach_list.shape[2]
    entries = 16 + 18 * slots
    return pl.pallas_call(
        folded_kernel,
        out_shape=(
            pltpu.VMEM((groups, 2, length, length), BF16),
            pltpu.VMEM((2, length, length), BF16),
            jax.ShapeDtypeStruct((entries,), F32),
        ),
        in_specs=[ANY] * 3 + [VMEM] * 4,
        out_specs=(VMEM,) * 2 + (ANY,),
        scratch_shapes=[
            pltpu.SMEM(reach_list.shape[::-1], jnp.int32),
            pltpu.SMEM((2, slots, 2, coupling.shape[0]), F32),
            pltpu.SMEM(window_velocity_group.shape[::-1], jnp.int32),
            pltpu.SMEM((entries,), F32),
            pltpu.SemaphoreType.DMA((4,)),
        ],
        compiler_params=PARAMS,
        cost_estimate=cost(0.1),
        name="fold",
    )(
        jnp.transpose(reach_list, (2, 1, 0)),
        jnp.transpose(coupling, (1, 2, 3, 0)),
        window_velocity_group.T,
        propagator,
        cosines,
        cosines.T,
        bell[None, :],
    )


def spread(west, middle, east, part):
    span = west.shape[2]
    wide = middle.shape[2]
    left, centre, right = west[part], middle[part], east[part]
    return (
        jnp.concatenate([left, centre[:, :HALF]], axis=1),
        jnp.concatenate([left[:, span - HALF :], centre[:, :span]], axis=1),
        jnp.concatenate([centre[:, wide - span :], right[:, :HALF]], axis=1),
        jnp.concatenate([centre[:, wide - HALF :], right], axis=1),
    )


def each_way(odd, even_call, odd_call):
    pl.when(odd == 0)(even_call)
    pl.when(odd == 1)(odd_call)


def start_of(odd, if_even, if_odd):
    return pl.multiple_of(jnp.where(odd == 0, if_even, if_odd), HALF)


def sweep(matrix_ref, x_real, x_imag, out_ref):
    t_real, t_imag = matrix_ref[0], matrix_ref[1]
    out_ref[0] = dot(t_real, x_real) - dot(t_imag, x_imag)
    out_ref[1] = dot(t_real, x_imag) + dot(t_imag, x_real)


def mix(base_ref, terms, store):
    length = terms[0][1].shape[1]
    for start in range(0, length, OVER):
        rows = slice(start, start + OVER)
        real, imag = (0.0, 0.0) if base_ref is None else (base_ref[0, rows], base_ref[1, rows])
        for (w_real, w_imag), ref in terms:
            u_real, u_imag = ref[0, rows], ref[1, rows]
            real += w_real * u_real - w_imag * u_imag
            imag += w_real * u_imag + w_imag * u_real
        store(rows, real, imag)


class Lists:
    def __init__(self, table_ref, copy, slots):
        self.table_ref, self.copy, self.slots = table_ref, copy, slots
        self.odd_x = parity("gx")

    def group_at(self, place):
        return self.table_ref[place].astype(jnp.int32)

    def window(self, row, col):
        return (row + 1) * 4 + col + 1

    def entry(self, row, col, slot):
        at = 16 + (((row + self.odd_x) * 2 + col) * self.slots + slot) * 3
        reach = self.table_ref[at].astype(jnp.int32)
        return reach, self.table_ref[at + 1], self.table_ref[at + 2]

    def weight_of(self, row, col, source):
        real, imag = jnp.float32(0), jnp.float32(0)
        for slot in range(self.slots):
            reach, c_real, c_imag = self.entry(row, col, slot)
            real += jnp.where(reach == source, c_real, 0.0)
            imag += jnp.where(reach == source, c_imag, 0.0)
        return real, imag

    def slot_of(self, row, col, slot):
        reach, c_real, c_imag = self.entry(row, col, slot)
        live = reach >= 0
        source = jnp.where(live, reach, self.window(row, col))
        at_row = source // 4
        at_x = jnp.where(self.odd_x == 0, at_row, 3 - at_row)
        real = jnp.where(live, c_real, 0.0)
        imag = jnp.where(live, c_imag, 0.0)
        return self.group_at(source), at_x, source % 4, real, imag


def pack_sides(block, near_ref, far_ref):
    width = near_ref.shape[2]
    start = block.shape[2] - width

    def store(high_ref, low_ref):
        high_ref[...] = block[:, :, start:]
        low_ref[...] = block[:, :, :width]

    each_way(parity("gy"), lambda: store(near_ref, far_ref), lambda: store(far_ref, near_ref))


def rows_kernel(wave_ref, x_ref):
    tile, span = wave_ref.shape[2], x_ref.shape[1]
    for part in range(2):
        x_ref[part] = wave_ref[part, 0, pl.ds(start_of(parity("gx"), 0, tile - span), span)]


def cols_kernel(wave_ref, _, near_ref, far_ref, corner_ref):
    pack_sides(wave_ref.at[:, 0], near_ref, far_ref)
    span = corner_ref.shape[1]
    rows = pl.ds(start_of(parity("gx"), 0, wave_ref.shape[2] - span), span)
    corner_ref[...] = far_ref[:, rows]


def corner_kernel(x_ref, near_ref):
    width = near_ref.shape[2]
    start = x_ref.shape[2] - width
    rows = pl.ds(start_of(parity("gx"), HALF, 0), near_ref.shape[1])

    def store(cols):
        near_ref[...] = x_ref[:, rows, cols]

    each_way(
        parity("gy"), lambda: store(slice(start, start + width)), lambda: store(slice(0, width))
    )


def window_rows(odd_x, at_x, length):
    return pl.multiple_of(jnp.where((at_x == 1) == (odd_x == 0), 0, length - OVER), HALF)


def fill_frame(frame_ref, wave_ref, ye_ref, yo_ref):
    tile = wave_ref.shape[2]
    rim = jnp.zeros((HALF, frame_ref.shape[3]), BF16)

    def fill(west, east):
        for part in range(2):
            for at, block in enumerate(spread(west, wave_ref.at[:, 0], east, part)):
                frame_ref[at, part, HALF : HALF + tile] = block
                frame_ref[at, part, :HALF] = rim
                frame_ref[at, part, HALF + tile :] = rim

    each_way(parity("gy"), lambda: fill(yo_ref, ye_ref), lambda: fill(ye_ref, yo_ref))


def edge_kernel(
    lists, wave_ref, ye_ref, yo_ref, left_ref, frame_ref, part_ref, swept_ref, rim_ref
):
    length = left_ref.shape[-1]
    tile = wave_ref.shape[2]
    fill_frame(frame_ref, wave_ref, ye_ref, yo_ref)
    edge = pl.ds(start_of(lists.odd_x, tile, HALF), HALF)
    for at in range(4):
        for part in range(2):
            rim_ref[at, part] = frame_ref[at, part, edge]
    lists.copy.wait()
    beyond = jnp.where(lists.odd_x == 0, 2, -1)
    mine = jnp.where(lists.odd_x == 0, 1, 0)
    rows = pl.ds(window_rows(lists.odd_x, 2, length), length)
    places = [lists.window(mine, at - 1) for at in range(4)]
    for at, place in enumerate(places):
        matrix_ref = left_ref.at[lists.group_at(place)]
        sweep(matrix_ref, frame_ref[at, 0, rows], frame_ref[at, 1, rows], swept_ref.at[1, at])
    for col in range(2):
        cols = slice(col * length, (col + 1) * length)
        terms = [
            (lists.weight_of(beyond, col, places[at]), swept_ref.at[1, at])
            for at in range(col, col + 3)
        ]

        def store(rows, real, imag):
            part_ref[0, rows, cols] = real.astype(BF16)
            part_ref[1, rows, cols] = imag.astype(BF16)

        mix(None, terms, store)


def early_kernel(
    lists, frame_ref, left_ref, gave_ref, right_ref, _, __, ___, sum_ref, echo_ref, swept_ref
):
    length = left_ref.shape[-1]
    lists.copy.wait()
    beyond = jnp.where(lists.odd_x == 0, 2, -1)
    edge = pl.ds(start_of(lists.odd_x, 0, length - HALF), HALF)
    groups = [lists.group_at(lists.window(beyond, col)) for col in range(2)]
    turn(halves(gave_ref, edge), right_ref, groups, echo_ref)
    rows = pl.ds(window_rows(lists.odd_x, 1, length), length)
    for at in range(4):
        matrix_ref = left_ref.at[lists.group_at(lists.window(lists.odd_x, at - 1))]
        sweep(matrix_ref, frame_ref[at, 0, rows], frame_ref[at, 1, rows], swept_ref.at[0, at])
    for c in range(2):
        for col in range(2):
            terms = []
            for slot in range(lists.slots):
                _, at_x, at_y, w_real, w_imag = lists.slot_of(lists.odd_x ^ c, col, slot)
                inside = (at_x == 1) | (at_x == 2)
                weight = jnp.where(inside, w_real, 0.0), jnp.where(inside, w_imag, 0.0)
                terms.append((weight, swept_ref.at[jnp.clip(at_x - 1, 0, 1), at_y]))

            def store(rows, real, imag):
                sum_ref[c, col, 0, rows] = real
                sum_ref[c, col, 1, rows] = imag

            mix(None, terms, store)


def mix_slots(mixed_ref, groups, weights, pieces):
    half = mixed_ref.shape[0] // 2
    for group, (w_real, w_imag), (real, imag) in zip(groups, weights, pieces):
        real, imag = real.astype(F32), imag.astype(F32)
        at = pl.multiple_of(group * OVER, OVER)
        mixed_ref[pl.ds(at, OVER)] += w_real * real - w_imag * imag
        mixed_ref[pl.ds(half + at, OVER)] += w_real * imag + w_imag * real


def strip_sums(lists, strip_ref, mixed_ref, row, col):
    mixed_ref[...] = jnp.zeros_like(mixed_ref)
    groups, weights, pieces = [], [], []
    for slot in range(lists.slots):
        group, at_x, at_y, w_real, w_imag = lists.slot_of(row, col, slot)
        groups.append(group)
        weights.append((w_real, w_imag))
        pieces.append((strip_ref[at_x, at_y, 0], strip_ref[at_x, at_y, 1]))
    mix_slots(mixed_ref, groups, weights, pieces)
    return mixed_ref[...].astype(BF16)


def late_kernel(
    lists,
    xo_ref,
    rim_ref,
    ze_ref,
    zo_ref,
    left_ref,
    lean_ref,
    frame_ref,
    early_ref,
    right_ref,
    mid_ref,
    rest_ref,
    send_o_ref,
    send_e_ref,
    strip_ref,
    outer_ref,
    swept_ref,
    base_ref,
    mixed_ref,
    sum_ref,
    out_ref,
    border_ref,
):
    length = left_ref.shape[-1]
    span = length - HALF
    tile = mid_ref.shape[1]
    odd_x, odd_y = lists.odd_x, parity("gy")
    at_o, hole_o = start_of(odd_x, 0, HALF), start_of(odd_x, span, 0)
    lean_o, lean_e = start_of(odd_x, 0, HALF), start_of(odd_x, HALF, 0)
    xo_ref = xo_ref.at[:, pl.ds(start_of(odd_x, HALF, 0), span)]
    strip_ref[...] = jnp.zeros_like(strip_ref)

    def fill(west, east):
        for part in range(2):
            for at, block in enumerate(spread(west, xo_ref, east, part)):
                outer_ref[at, part, pl.ds(at_o, span)] = block
                outer_ref[at, part, pl.ds(hole_o, HALF)] = jnp.zeros((HALF, length), BF16)
                strip_ref[2, at, part, pl.ds(lean_e, HALF)] = rim_ref[at, part]

    each_way(odd_y, lambda: fill(zo_ref, ze_ref), lambda: fill(ze_ref, zo_ref))
    shift = start_of(odd_x, span - HALF, HALF)
    near_o, near_e = start_of(odd_x, HALF, tile), start_of(odd_x, tile, HALF)
    for at in range(4):
        for part in range(2):
            strip_ref[1, at, part, pl.ds(lean_o, HALF)] = outer_ref[at, part, pl.ds(shift, HALF)]
            strip_ref[0, at, part, pl.ds(lean_e, HALF)] = frame_ref[at, part, pl.ds(near_o, HALF)]
            strip_ref[3, at, part, pl.ds(lean_o, HALF)] = frame_ref[at, part, pl.ds(near_e, HALF)]

    lists.copy.wait()
    beyond = jnp.where(odd_x == 0, -1, 2)
    places = [lists.window(beyond, at - 1) for at in range(4)]
    for at, place in enumerate(places):
        matrix_ref = left_ref.at[lists.group_at(place)]
        sweep(matrix_ref, outer_ref[at, 0], outer_ref[at, 1], swept_ref.at[at])
    for col in range(2):
        stacked = strip_sums(lists, strip_ref, mixed_ref.at[col], odd_x, col)
        for part in range(2):
            base_ref[part] = early_ref[0, col, part] + dot(lean_ref[part], stacked)
        cols = slice(col * length, (col + 1) * length)
        terms = [
            (lists.weight_of(odd_x, col, places[at]), swept_ref.at[at])
            for at in range(col, col + 3)
        ]

        def store(rows, real, imag):
            sum_ref[0, rows, cols] = real.astype(BF16)
            sum_ref[1, rows, cols] = imag.astype(BF16)

        mix(base_ref, terms, store)
    groups = [lists.group_at(lists.window(odd_x, col)) for col in range(2)]
    turn(halves(sum_ref, slice(None)), right_ref, groups, out_ref)
    source = start_of(odd_x, HALF, 0)
    target = start_of(odd_x, 0, tile - span)
    border = start_of(odd_x, 0, span)
    for part in range(2):
        mid_ref[part, pl.ds(target, span)] = out_ref[part, pl.ds(source, span)]
        send_o_ref[part] = out_ref[part, pl.ds(border, HALF)].astype(BF16)
    row = 1 - odd_x
    for col in range(2):
        stacked = strip_sums(lists, strip_ref, mixed_ref.at[2 + col], row, col)
        for part in range(2):
            rest_ref[part, :, col * length : (col + 1) * length] = early_ref[1, col, part] + dot(
                lean_ref[part], stacked
            )
    groups = [lists.group_at(lists.window(row, col)) for col in range(2)]
    rows = pl.ds(start_of(odd_x, span, 0), HALF)
    turn(halves(rest_ref, rows), right_ref, groups, border_ref)
    for part in range(2):
        send_e_ref[part] = border_ref[part, :, : send_e_ref.shape[2]].astype(BF16)


def halves(ref, rows):
    length = ref.shape[2] // 2
    return [
        [ref[part, rows, col * length : (col + 1) * length].astype(BF16) for part in range(2)]
        for col in range(2)
    ]


def turn(blocks, right_ref, groups, out_ref):
    real, imag = 0.0, 0.0
    for col in range(2):
        m_real, m_imag = blocks[col]
        r_real, r_imag = right_ref[groups[col], col, 0], right_ref[groups[col], col, 1]
        real += dot(m_real, r_real) - dot(m_imag, r_imag)
        imag += dot(m_real, r_imag) + dot(m_imag, r_real)
    out_ref[0] = real
    out_ref[1] = imag


def join_kernel(lists, mid_ref, rest_ref, got_ref, right_ref, full_ref, sum_ref, out_ref):
    length = got_ref.shape[1]
    span = length - HALF
    tile = full_ref.shape[1]
    odd_x = lists.odd_x
    mine = jnp.where(odd_x == 0, 1, 0)
    for part in range(2):
        sum_ref[part] = (rest_ref[part] + got_ref[part].astype(F32)).astype(BF16)
    lists.copy.wait()
    groups = [lists.group_at(lists.window(mine, col)) for col in range(2)]
    turn(halves(sum_ref, slice(None)), right_ref, groups, out_ref)
    alone = tile - span
    both = slice(alone, span)
    source, target = start_of(odd_x, span - alone, HALF), start_of(odd_x, span, 0)
    shared = start_of(odd_x, 0, HALF + alone)
    for part in range(2):
        full_ref[part, pl.ds(target, alone)] = out_ref[part, pl.ds(source, alone)]
        full_ref[part, both] = (
            mid_ref[part, both] + out_ref[part, pl.ds(shared, span - alone)]
        )


def border_kernel(full_ref, echo_ref, rows_e_ref, rows_o_ref, done_ref, send_e_ref, send_o_ref):
    tile = done_ref.shape[1]
    lanes = tile // 128 * 128
    odd_x = parity("gx")
    row_e = pl.ds(start_of(odd_x, tile - HALF, 0), HALF)
    row_o = pl.ds(start_of(odd_x, 0, tile - HALF), HALF)
    width = rows_e_ref.shape[2]
    for part in range(2):
        done_ref[part, row_o] = full_ref[part, row_o] + rows_o_ref[part].astype(F32)
        done_ref[part, row_e, :width] = (
            full_ref[part, row_e, :width]
            + echo_ref[part, :, :width]
            + rows_e_ref[part].astype(F32)
        )
        turned = done_ref[part, :, lanes:].T
        west = turned[tile - lanes : tile - lanes + HALF].astype(BF16)
        east = turned[tile - lanes + HALF : tile - lanes + OVER].astype(BF16)

        def store(near, away):
            send_e_ref[part] = near
            send_o_ref[part] = away

        each_way(parity("gy"), lambda: store(east, west), lambda: store(west, east))


def rotate(real, imag, cos, sin, result_ref):
    result_ref[0, 0] = (real * cos - imag * sin).astype(BF16)
    result_ref[1, 0] = (real * sin + imag * cos).astype(BF16)


def inner_kernel(full_ref, cos_ref, sin_ref, result_ref):
    rotate(full_ref[0], full_ref[1], cos_ref[...], sin_ref[...], result_ref)


def outer_kernel(
    _, full_ref, cols_e_ref, cols_o_ref, cos_ref, sin_ref, result_hbm, west_ref, east_ref, sems
):
    tile = full_ref.shape[1]
    lanes = tile // 128 * 128

    def side(cols_ref, cols, shift, out_ref):
        size = cols.stop - cols.start
        lane = lax.broadcasted_iota(jnp.int32, (HALF, size), 1)
        line = lax.broadcasted_iota(jnp.int32, (HALF, size), 0)
        pick = (lane == line + shift).astype(F32).astype(BF16)
        real, imag = (
            full_ref[part, :, cols]
            + lax.dot_general(
                cols_ref[part], pick, (((0,), (0,)), ((), ())), preferred_element_type=F32
            )
            for part in range(2)
        )
        rotate(real, imag, cos_ref[:, cols], sin_ref[:, cols], out_ref)

    west, east = slice(0, 128), slice(lanes, tile)
    copies = [
        pltpu.make_async_copy(ref, result_hbm.at[:, :, :, cols], sems.at[i])
        for i, (ref, cols) in enumerate(((west_ref, west), (east_ref, east)))
    ]

    def sides(to_west_ref, to_east_ref):
        side(to_west_ref, west, 0, west_ref)
        copies[0].start()
        side(to_east_ref, east, tile - HALF - lanes, east_ref)
        copies[1].start()

    each_way(
        parity("gy"), lambda: sides(cols_o_ref, cols_e_ref), lambda: sides(cols_e_ref, cols_o_ref)
    )
    for copy in copies:
        copy.wait()


def phase_kernel(freq_ref, slow_ref, _, cos_ref, sin_ref):
    angle = freq_ref[...] * slow_ref[...]
    turns = jnp.round(angle * (2.0 / math.pi))
    rest = angle - turns * 1.5703125
    rest = rest - turns * 4.8375129699707031e-4
    rest = rest - turns * 7.5495138331e-8
    square = rest * rest
    sine = rest + rest * square * (
        -1.6666654611e-1 + square * (8.3321608736e-3 - square * 1.9515295891e-4)
    )
    cosine = 1.0 - 0.5 * square + square * square * (
        4.166664568298827e-2 + square * (-1.388731625493765e-3 + square * 2.443315711809948e-5)
    )
    quarter = turns.astype(jnp.int32) & 3
    crossed = (quarter & 1) == 1
    sin_value = jnp.where(crossed, cosine, sine)
    cos_value = jnp.where(crossed, sine, cosine)
    sin_ref[...] = jnp.where(quarter >= 2, -sin_value, sin_value)
    cos_ref[...] = jnp.where((quarter == 1) | (quarter == 2), -cos_value, cos_value)


def per_device(
    wavefield, slowness, frequencies, propagator, window_velocity_group, reach_list, coupling
):
    length = propagator.shape[-1]
    span = length - HALF
    wide = 2 * length
    tile_rows, tile_cols = wavefield.shape[2:]
    slots = reach_list.shape[2]

    def shape(*dims, kind=BF16):
        return pltpu.VMEM(dims, kind)

    x_send = pl.pallas_call(
        rows_kernel,
        out_shape=shape(2, span + HALF, tile_cols),
        in_specs=[VMEM],
        out_specs=VMEM,
        compiler_params=PARAMS,
        cost_estimate=cost(0.5),
        name="rows",
    )(wavefield)
    x_odd = swap(x_send, "gx", True)
    near, far, corner = pl.pallas_call(
        cols_kernel,
        out_shape=(shape(2, tile_rows, span),) * 2 + (shape(2, span, span),),
        in_specs=[VMEM] * 2,
        out_specs=(VMEM,) * 3,
        compiler_params=PARAMS,
        cost_estimate=cost(0.5),
        name="cols",
    )(wavefield, x_send)
    y_near = swap(near, "gy", False)
    y_far = swap(far, "gy", True)
    z_far = far_corner(corner)
    y_near = swap(near, "gy", False)

    left, strip, table = fold(
        propagator,
        cosine_table(length),
        bell_curve(length, OVER),
        reach_list,
        coupling,
        window_velocity_group,
    )
    def call(kernel, name, micros, out_shape, inputs, scratch=(), **options):
        def body(table_any, *refs):
            *refs, table_ref, sem = refs
            copy = pltpu.make_async_copy(table_any, table_ref, sem)
            copy.start()
            kernel(Lists(table_ref, copy, slots), *refs)

        specs = options.pop("in_specs", [VMEM] * len(inputs))
        outs = options.pop("out_specs", jax.tree.map(lambda _: VMEM, out_shape))
        return pl.pallas_call(
            body,
            out_shape=out_shape,
            in_specs=[ANY] + specs,
            out_specs=outs,
            scratch_shapes=list(scratch)
            + [pltpu.SMEM(table.shape, F32), pltpu.SemaphoreType.DMA(())],
            compiler_params=PARAMS,
            name=name,
            cost_estimate=cost(micros),
            **options,
        )(table, *inputs)

    frame, given, swept, rim_send = call(
        edge_kernel,
        "edge",
        0.001,
        (
            shape(4, 2, tile_rows + OVER, length),
            shape(2, length, wide),
            shape(2, 4, 2, length, length, kind=F32),
            shape(4, 2, HALF, length),
        ),
        (wavefield, y_near, y_far, left),
    )
    rim = swap(rim_send, "gx", False)
    got = swap(given, "gx", False)

    right = pl.pallas_call(
        right_kernel,
        out_shape=shape(left.shape[0], 2, 2, length, wide),
        in_specs=[VMEM, ANY],
        out_specs=VMEM,
        compiler_params=PARAMS,
        cost_estimate=cost(0.01),
        name="right",
    )(left, rim_send)
    cos_phase, sin_phase = pl.pallas_call(
        phase_kernel,
        out_shape=(shape(tile_rows, tile_cols, kind=F32),) * 2,
        in_specs=[VMEM] * 2 + [ANY],
        out_specs=(VMEM,) * 2,
        compiler_params=PARAMS,
        cost_estimate=cost(0.01),
        name="phase",
    )(jnp.broadcast_to(frequencies[:, None], (1, tile_cols)), slowness, rim_send)

    early, echo, _ = call(
        early_kernel,
        "early",
        3,
        (
            shape(2, 2, 2, length, length, kind=F32),
            shape(2, HALF, wide, kind=F32),
            shape(2, 4, 2, length, length, kind=F32),
        ),
        (frame, left, given, right, swept, z_far, cos_phase),
        in_specs=[VMEM] * 5 + [ANY] * 2,
        input_output_aliases={5: 2},
    )
    near = pl.pallas_call(
        corner_kernel,
        out_shape=shape(2, span, span),
        in_specs=[VMEM],
        out_specs=VMEM,
        compiler_params=PARAMS,
        cost_estimate=cost(0.2),
        name="corner",
    )(x_odd)
    z_near = swap(near, "gy", False)
    mid, rest, send_o, send_e = call(
        late_kernel,
        "late",
        4,
        (
            shape(2, tile_rows, wide, kind=F32),
            shape(2, length, wide, kind=F32),
            shape(2, HALF, wide),
            shape(2, HALF, tile_cols + OVER),
        ),
        (x_odd, rim, z_near, z_far, left, strip, frame, early, right),
        (
            pltpu.VMEM((4, 4, 2, OVER, length), BF16),
            pltpu.VMEM((4, 2, length, length), BF16),
            pltpu.VMEM((4, 2, length, length), F32),
            pltpu.VMEM((2, length, length), F32),
            pltpu.VMEM((4, length, length), F32),
            pltpu.VMEM((2, length, wide), BF16),
            pltpu.VMEM((2, length, wide), F32),
            pltpu.VMEM((2, HALF, wide), F32),
        ),
    )
    rows_o = swap(send_o, "gx", True)
    rows_e = swap(send_e, "gx", False)
    full = call(
        join_kernel,
        "join",
        0.001,
        shape(2, tile_rows, wide, kind=F32),
        (mid, rest, got, right),
        (
            pltpu.VMEM((2, length, wide), BF16),
            pltpu.VMEM((2, length, wide), F32),
        ),
        input_output_aliases={1: 0},
    )
    full, send_e, send_o = pl.pallas_call(
        border_kernel,
        out_shape=(shape(2, tile_rows, wide, kind=F32),) + (shape(2, HALF, tile_rows),) * 2,
        in_specs=[VMEM] * 4,
        out_specs=(VMEM,) * 3,
        input_output_aliases={0: 0},
        compiler_params=PARAMS,
        cost_estimate=cost(0.5),
        name="border",
    )(full, echo, rows_e, rows_o)
    cols_o = swap(send_o, "gy", True)
    cols_e = swap(send_e, "gy", False)
    result = jax.ShapeDtypeStruct(wavefield.shape, BF16)
    count = -(-tile_cols // 128)

    def blocks(place):
        return (
            pl.BlockSpec((2, tile_rows, 128), lambda i: (0, 0, place(i))),
            pl.BlockSpec((tile_rows, 128), lambda i: (0, place(i))),
            pl.BlockSpec((2, 1, tile_rows, 128), lambda i: (0, 0, 0, place(i))),
        )

    full_spec, phase_spec, out_spec = blocks(lambda i: i + 1)
    partly = pl.pallas_call(
        inner_kernel,
        grid=(count - 2,),
        out_shape=result,
        in_specs=[full_spec, phase_spec, phase_spec],
        out_specs=out_spec,
        compiler_params=PARAMS,
        cost_estimate=cost(1),
        name="inner",
    )(full, cos_phase, sin_phase)
    return pl.pallas_call(
        outer_kernel,
        out_shape=result,
        in_specs=[ANY] + [VMEM] * 5,
        out_specs=ANY,
        scratch_shapes=[
            pltpu.VMEM((2, 1, tile_rows, 128), BF16),
            pltpu.VMEM((2, 1, tile_rows, tile_cols % 128), BF16),
            pltpu.SemaphoreType.DMA((2,)),
        ],
        input_output_aliases={0: 0},
        compiler_params=PARAMS,
        cost_estimate=cost(1),
        name="outer",
    )(partly, full, cols_e, cols_o, cos_phase, sin_phase)


def solution(mesh):
    return jax.shard_map(
        per_device,
        mesh=mesh,
        in_specs=(P(None, None, "gx", "gy"), P("gx", "gy"), P(), P(), P(), P(), P()),
        out_specs=P(None, None, "gx", "gy"),
        check_vma=False,
    )
```

time: 48 us -> 42.9 us (0.89)
  Pallas kernels: 21.4 us -> 17.4 us
  waiting for transfers between devices: 3.76 us -> 1.28 us
  starting transfers between devices: 20 us -> 21.1 us
    pallas_call x10 -> x12, Pallas kernels: 18.6 us -> 14.6 us  [the longest x4 9.5 us: call(): pl.pallas_call(body, out_shape=out_shape, in_specs=[ANY] + specs, out_spe...]
    ppermute x0 -> x1, starting transfers between devices: none -> 3.49 us  [far_corner(): return lax.ppermute(block, ('gx', 'gy'), pairs)]
    ppermute x11 -> x10, waiting for transfers between devices: 3.76 us -> 1.03 us  [swap(): return lax.ppermute(block, axis, pairs)]
    ppermute x11 -> x10, starting transfers between devices: 20 us -> 17.7 us  [swap(): return lax.ppermute(block, axis, pairs)]
  transfers between devices with their start and end apart: 11 -> 11, of which waited for: 2 -> 4; matrix products, arithmetic and copies ran while one was open for 0% -> 0% of each run, Pallas kernels for 40% -> 38%
where the time goes in v3:
time: 42.9 us; the launch traced here: 42.1 us
  starting transfers between devices  21.1 us (49%)
  Pallas kernels  17.4 us (41%)
  waiting for transfers between devices  1.28 us (3%)
  local copies, waits for them, and re-layouts  1.22 us (3%)
  between operations  1.12 us (3%)
    ppermute x10, starting transfers between devices, swap(): return lax.ppermute(block, axis, pairs)  17.7 us
    pallas_call x4, Pallas kernels, call(): pl.pallas_call(body, out_shape=out_shape, in_specs=[ANY] + specs, out_spe...  9.5 us
    ppermute x1, starting transfers between devices, far_corner(): return lax.ppermute(block, ('gx', 'gy'), pairs)  3.49 us
    pallas_call x1, Pallas kernels, fold(): pl.pallas_call(folded_kernel, out_shape=(pltpu.VMEM((groups, 2, length, l...  2.74 us
    pallas_call x1, Pallas kernels, per_device(): pl.pallas_call(phase_kernel, out_shape=(shape(tile_rows, tile_cols, kind=...  1.27 us
    unnamed x20, local copies, waits for them, and re-layouts  1.22 us
    pallas_call x1, Pallas kernels, per_device(): pl.pallas_call(outer_kernel, out_shape=result, in_specs=[ANY] + [VMEM] *...  1.13 us
    pallas_call x1, Pallas kernels, per_device(): pl.pallas_call(inner_kernel, grid=(count - 2,), out_shape=result, in_spec...  1.12 us
  transfers between devices with their start and end apart: 11, of which 4 were waited for; matrix products, arithmetic and copies ran while one was open for 0% of the time, Pallas kernels for 38%

profile of v3, /device:TPU:9, one launch (start us, length us, event | category | flops | bytes accessed | tf_op | source)
XLA Modules:
  0.0 42.1 jit_solution(17088090383373348026)
XLA Ops:
  0.0 1.2 %copy-done = bf16[2,1,448,448]{3,2,1,0:T(8,128)(2,1)S(1)} copy-done((bf16[2,1,448,448]{3,2,1,0:T(8,128)(2,1)S(1)}, bf16[2,1,448,448]{3,2,1,0:T(8,128)(2,1)}, u32[]{:S(2)}) %copy-start) | copy-done | bytes 802840
  1.2 0.0 copy-start.7
  1.2 0.0 copy-start.8
  1.2 0.0 copy-start.9
  1.2 0.0 copy-start.1
  1.2 0.1 rows.1._
  1.3 3.2 %collective-permute-start = (bf16[2,256,448]{2,1,0:T(8,128)(2,1)S(1)}, bf16[2,256,448]{2,1,0:T(8,128)(2,1)S(1)}, u32[]{:S(2)}, u32[]{:S(2)}) collective-permute-start(bf16[2,256,448]{2,1,0:T(8,128)(2,1)S(1)} %rows.1._), channel_id=1, source_target_pairs={{4,8},{8,4},{12,16},{16,12},{20,24},{24,20},{5,9},{9,5},{13,17},{1... | collective-permute-start | bytes 1376264 | tf_op jit(solution)/shard_map/ppermute | solution.py:47
  4.5 0.3 cols.1
  4.8 1.0 %collective-permute-start.1 = (bf16[2,448,240]{2,1,0:T(8,128)(2,1)S(1)}, bf16[2,448,240]{2,1,0:T(8,128)(2,1)S(1)}, u32[]{:S(2)}, u32[]{:S(2)}) collective-permute-start(bf16[2,448,240]{2,1,0:T(8,128)(2,1)S(1)} %get-tuple-element.27), channel_id=1, source_target_pairs={{0,1},{1,0},{2,3},{3,2},{4,5},{5,4},{6,7},{7,6},{8,9},{9,8},{10,11... | collective-permute-start | bytes 1290248 | tf_op jit(solution)/shard_map/ppermute | solution.py:47
  5.8 3.0 %collective-permute-start.2 = (bf16[2,448,240]{2,1,0:T(8,128)(2,1)S(1)}, bf16[2,448,240]{2,1,0:T(8,128)(2,1)S(1)}, u32[]{:S(2)}, u32[]{:S(2)}) collective-permute-start(bf16[2,448,240]{2,1,0:T(8,128)(2,1)S(1)} %get-tuple-element.28), channel_id=1, source_target_pairs={{1,2},{2,1},{5,6},{6,5},{9,10},{10,9},{13,14},{14,13},{17,18},{18,... | collective-permute-start | bytes 1290248 | tf_op jit(solution)/shard_map/ppermute | solution.py:47
  8.9 3.5 %collective-permute-start.5 = (bf16[2,240,240]{2,1,0:T(8,128)(2,1)S(1)}, bf16[2,240,240]{2,1,0:T(8,128)(2,1)S(1)}, u32[]{:S(2)}, u32[]{:S(2)}) collective-permute-start(bf16[2,240,240]{2,1,0:T(8,128)(2,1)S(1)} %get-tuple-element.31), channel_id=1, source_target_pairs={{5,10},{10,5},{6,9},{9,6},{13,18},{18,13},{14,17},{17,14},{21,26},... | collective-permute-start | bytes 691208 | tf_op jit(solution)/shard_map/ppermute | solution.py:58
  13.0 0.0 copy-done.3
  13.0 0.0 copy-done.4
  13.0 0.0 copy-done.5
  13.0 0.0 copy-done.6
  13.0 0.0 copy-done.7
  13.1 0.0 copy-done.8
  13.1 0.0 copy-done.9
  13.1 2.7 %fold.1 = (bf16[3,2,256,256]{3,2,1,0:T(8,128)(2,1)S(1)}, bf16[2,256,256]{2,1,0:T(8,128)(2,1)S(1)}, f32[106]{0:T(128)S(1)}) custom-call(s32[5,8,16]{2,1,0:T(8,128)S(1)} %bitcast.6, f32[8,5,2,16]{3,2,1,0:T(2,128)S(1)} %bitcast.5, s32[8,16]{1,0:T(8,128)S(1)} %bitcast.7, bf16[3,1,2,256,256]{4,3,2,1,0:T(8,128)(2,1)S(1)} %copy-done.3, ...), custom_call_target="tpu_custom_call" | custom-call | flops 110000000 | bytes 360000 | tf_op jit(solution)/shard_map/fold/pallas_call | solution.py:180
  15.8 0.0 collective-permute-done.1.refs_1_
  15.8 0.1 collective-permute-done.2.refs_2_
  15.9 0.0 copy-done.1
  15.9 1.6 %edge.1 = (bf16[4,2,480,256]{3,2,1,0:T(8,128)(2,1)S(1)}, bf16[2,256,512]{2,1,0:T(8,128)(2,1)S(1)}, f32[2,4,2,256,256]{4,3,2,1,0:T(8,128)S(1)}, bf16[4,2,16,256]{3,2,1,0:T(8,128)(2,1)S(1)}) custom-call(f32[106]{0:T(128)S(1)} %get-tuple-element.26.table_any, bf16[2,1,448,448]{3,2,1,0:T(8,128)(2,1)S(1)} %copy-done.1, ...), custom_call_target="tpu_custom_call" | custom-call | flops 1100000 | bytes 3600 | tf_op jit(solution)/shard_map/edge/pallas_call | solution.py:701
  17.5 0.0 copy-start.2
  17.5 1.4 %collective-permute-start.3 = (bf16[4,2,16,256]{3,2,1,0:T(8,128)(2,1)S(1)}, bf16[4,2,16,256]{3,2,1,0:T(8,128)(2,1)S(1)}, u32[]{:S(2)}, u32[]{:S(2)}) collective-permute-start(bf16[4,2,16,256]{3,2,1,0:T(8,128)(2,1)S(1)} %get-tuple-element.30._), channel_id=1, source_target_pairs={{0,4},{4,0},{8,12},{12,8},{16,20},{20,16},{24,28},{28,24},{1,5},{5... | collective-permute-start | bytes 196616 | tf_op jit(solution)/shard_map/ppermute | solution.py:47
  19.0 0.1 collective-permute-start.6
  19.1 0.9 %right.1.refs_3_.refs_8_ = bf16[3,2,2,256,512]{4,3,2,1,0:T(8,128)(2,1)S(1)} custom-call(bf16[3,2,256,256]{3,2,1,0:T(8,128)(2,1)S(1)} %get-tuple-element.29.refs_3_.left_ref.refs_1_.refs_4_, bf16[4,2,16,256]{3,2,1,0:T(8,128)(2,1)S(1)} %get-tuple-element.30._), custom_call_target="tpu_custom_call" | custom-call | flops 11000000 | bytes 36000 | tf_op jit(solution)/shard_map/right/pallas_call | solution.py:729
  20.0 1.3 %phase.1 = (f32[448,448]{1,0:T(8,128)S(1)}, f32[448,448]{1,0:T(8,128)S(1)}) custom-call(f32[1,448]{1,0:T(1,128)S(1)} %broadcast_in_dim.9.freq_ref, f32[448,448]{1,0:T(8,128)S(1)} %copy-done.2, bf16[4,2,16,256]{3,2,1,0:T(8,128)(2,1)S(1)} %get-tuple-element.30._), custom_call_target="tpu_custom_call" | custom-call | flops 11000000 | bytes 36000 | tf_op jit(solution)/shard_map/phase/pallas_call | solution.py:738
  21.3 0.0 collective-permute-done.x_ref.refs_0_
  21.3 0.1 collective-permute-start.4
  21.4 0.2 collective-permute-done.5.refs_5_.refs_3_
  21.7 3.0 %early.1 = (f32[2,2,2,256,256]{4,3,2,1,0:T(8,128)S(1)}, f32[2,16,512]{2,1,0:T(8,128)S(1)}, f32[2,4,2,256,256]{4,3,2,1,0:T(8,128)S(1)}) custom-call(f32[106]{0:T(128)S(1)} %get-tuple-element.26.table_any, bf16[4,2,480,256]{3,2,1,0:T(8,128)(2,1)S(1)} %get-tuple-element.33.refs_0_.refs_6_, ...), custom_call_target="tpu_custom_call", output_to_operand_aliasing={{2}: (5, {})} | custom-call | flops 3300000000 | bytes 10800000 | tf_op jit(solution)/shard_map/early/pallas_call | solution.py:701
  24.6 0.0 collective-permute-done.3.refs_1_
  24.7 0.0 collective-permute-done.4.refs_2_
  24.7 3.5 %late.1 = (f32[2,448,512]{2,1,0:T(8,128)S(1)}, f32[2,256,512]{2,1,0:T(8,128)S(1)}, bf16[2,16,512]{2,1,0:T(8,128)(2,1)S(1)}, bf16[2,16,480]{2,1,0:T(8,128)(2,1)S(1)}) custom-call(f32[106]{0:T(128)S(1)} %get-tuple-element.26.table_any, bf16[2,256,448]{2,1,0:T(8,128)(2,1)S(1)} %collective-permute-done.x_ref.refs_0_, ...), custom_call_target="tpu_custom_call" | custom-call | flops 4400000000 | bytes 14400000 | tf_op jit(solution)/shard_map/late/pallas_call | solution.py:701
  28.1 3.0 %collective-permute-start.8 = (bf16[2,16,512]{2,1,0:T(8,128)(2,1)S(1)}, bf16[2,16,512]{2,1,0:T(8,128)(2,1)S(1)}, u32[]{:S(2)}, u32[]{:S(2)}) collective-permute-start(bf16[2,16,512]{2,1,0:T(8,128)(2,1)S(1)} %get-tuple-element.42), channel_id=1, source_target_pairs={{4,8},{8,4},{12,16},{16,12},{20,24},{24,20},{5,9},{9,5},{13,17},{1... | collective-permute-start | bytes 98312 | tf_op jit(solution)/shard_map/ppermute | solution.py:47
  31.2 1.4 %collective-permute-start.7 = (bf16[2,16,480]{2,1,0:T(8,128)(2,1)S(1)}, bf16[2,16,480]{2,1,0:T(8,128)(2,1)S(1)}, u32[]{:S(2)}, u32[]{:S(2)}) collective-permute-start(bf16[2,16,480]{2,1,0:T(8,128)(2,1)S(1)} %get-tuple-element.41), channel_id=1, source_target_pairs={{0,4},{4,0},{8,12},{12,8},{16,20},{20,16},{24,28},{28,24},{1,5},{5... | collective-permute-start | bytes 92168 | tf_op jit(solution)/shard_map/ppermute | solution.py:47
  32.6 0.5 %collective-permute-done.6.refs_2_ = bf16[2,256,512]{2,1,0:T(8,128)(2,1)S(1)} collective-permute-done((bf16[2,256,512]{2,1,0:T(8,128)(2,1)S(1)}, bf16[2,256,512]{2,1,0:T(8,128)(2,1)S(1)}, u32[]{:S(2)}, u32[]{:S(2)}) %collective-permute-start.6) | collective-permute-done | bytes 524320 | tf_op jit(solution)/shard_map/ppermute | solution.py:47
  33.1 1.5 %join.1.full_ref = f32[2,448,512]{2,1,0:T(8,128)S(1)} custom-call(f32[106]{0:T(128)S(1)} %get-tuple-element.26.table_any, f32[2,448,512]{2,1,0:T(8,128)S(1)} %get-tuple-element.38.refs_0_, f32[2,256,512]{2,1,0:T(8,128)S(1)} %get-tuple-element.39.refs_1_, bf16[2,256,512]{2,1,0:T(8,128)(2,1)S(1)} %collective-permute-done.6.refs_2_, ...), custom_call_target="tpu_custom_call", output_to_operand_aliasing={{}: (1, {})} | custom-call | flops 1100000 | bytes 3600 | tf_op jit(solution)/shard_map/join/pallas_call | solution.py:701
  34.6 0.0 collective-permute-done.7.rows_e_ref
  34.6 0.0 collective-permute-done.8.rows_o_ref
  34.6 0.3 border.1
  34.9 4.3 %collective-permute-start.10 = (bf16[2,16,448]{2,1,0:T(8,128)(2,1)S(1)}, bf16[2,16,448]{2,1,0:T(8,128)(2,1)S(1)}, u32[]{:S(2)}, u32[]{:S(2)}) collective-permute-start(bf16[2,16,448]{2,1,0:T(8,128)(2,1)S(1)} %get-tuple-element.46), channel_id=1, source_target_pairs={{1,2},{2,1},{5,6},{6,5},{9,10},{10,9},{13,14},{14,13},{17,18},{18,... | collective-permute-start | bytes 86024 | tf_op jit(solution)/shard_map/ppermute | solution.py:47
  39.2 0.1 collective-permute-start.9
  39.3 1.1 %inner.1._ = bf16[2,1,448,448]{3,2,1,0:T(8,128)(2,1)} custom-call(f32[2,448,512]{2,1,0:T(8,128)S(1)} %get-tuple-element.43.full_ref, f32[448,448]{1,0:T(8,128)S(1)} %get-tuple-element.36.refs_6_.cos_ref, f32[448,448]{1,0:T(8,128)S(1)} %get-tuple-element.44.sin_ref), custom_call_target="tpu_custom_call" | custom-call | flops 1100000000 | bytes 3600000 | tf_op jit(solution)/shard_map/inner/pallas_call | solution.py:830
  40.4 0.4 collective-permute-done.10.cols_o_ref
  40.8 0.0 collective-permute-done.9.cols_e_ref
  40.8 1.1 %outer.1 = bf16[2,1,448,448]{3,2,1,0:T(8,128)(2,1)} custom-call(bf16[2,1,448,448]{3,2,1,0:T(8,128)(2,1)} %inner.1._, f32[2,448,512]{2,1,0:T(8,128)S(1)} %get-tuple-element.43.full_ref, bf16[2,16,448]{2,1,0:T(8,128)(2,1)S(1)} %collective-permute-done.9.cols_e_ref, ...), custom_call_target="tpu_custom_call", output_to_operand_aliasing={{}: (0, {})} | custom-call | flops 1100000000 | bytes 3600000 | tf_op jit(solution)/shard_map/outer/pallas_call | solution.py:840
  (8 shorter events, 0.1 us)
Async XLA Ops:
  0.0 1.2 %copy-start = (bf16[2,1,448,448]{3,2,1,0:T(8,128)(2,1)S(1)}, bf16[2,1,448,448]{3,2,1,0:T(8,128)(2,1)}, u32[]{:S(2)}) copy-start(bf16[2,1,448,448]{3,2,1,0:T(8,128)(2,1)} %refs_0_.1) | copy-start | bytes 2408452
  1.2 11.8 %copy-start.3 = (bf16[3,1,2,256,256]{4,3,2,1,0:T(8,128)(2,1)S(1)}, bf16[3,1,2,256,256]{4,3,2,1,0:T(8,128)(2,1)}, u32[]{:S(2)}) copy-start(bf16[3,1,2,256,256]{4,3,2,1,0:T(8,128)(2,1)} %prop_ref.1) | copy-start | bytes 2359300
  1.2 11.8 %copy-start.4 = (bf16[256,256]{1,0:T(8,128)(2,1)S(1)}, bf16[256,256]{1,0:T(8,128)(2,1)}, u32[]{:S(2)}) copy-start(bf16[256,256]{1,0:T(8,128)(2,1)} %constant.6.clone.cos_ref) | copy-start | bytes 393220
  1.2 11.8 %copy-start.5 = (bf16[256,256]{1,0:T(8,128)(2,1)S(1)}, bf16[256,256]{1,0:T(8,128)(2,1)}, u32[]{:S(2)}) copy-start(bf16[256,256]{1,0:T(8,128)(2,1)} %constant.7.clone.cos_t_ref) | copy-start | bytes 393220
  1.2 11.9 %copy-start.6 = (f32[16,8,5,2]{0,3,2,1:T(2,128)S(1)}, f32[16,8,5,2]{0,3,2,1:T(2,128)}, u32[]{:S(2)}) copy-start(f32[16,8,5,2]{0,3,2,1:T(2,128)} %param.16) | copy-start | bytes 15364
  1.2 11.9 %copy-start.7 = (s32[16,8,5]{0,1,2:T(8,128)S(1)}, s32[16,8,5]{0,1,2:T(8,128)}, u32[]{:S(2)}) copy-start(s32[16,8,5]{0,1,2:T(8,128)} %param.15) | copy-start | bytes 7684
  1.2 11.9 %copy-start.8 = (s32[16,8]{0,1:T(8,128)S(1)}, s32[16,8]{0,1:T(8,128)}, u32[]{:S(2)}) copy-start(s32[16,8]{0,1:T(8,128)} %param.14) | copy-start | bytes 1540
  1.2 11.9 %copy-start.9 = (f32[1,256]{1,0:T(1,128)S(1)}, f32[1,256]{1,0:T(1,128)}, u32[]{:S(2)}) copy-start(f32[1,256]{1,0:T(1,128)} %constant.8.clone.row_ref) | copy-start | bytes 3076
  1.2 14.7 %copy-start.1 = (bf16[2,1,448,448]{3,2,1,0:T(8,128)(2,1)S(1)}, bf16[2,1,448,448]{3,2,1,0:T(8,128)(2,1)}, u32[]{:S(2)}) copy-start(bf16[2,1,448,448]{3,2,1,0:T(8,128)(2,1)} %refs_0_.1) | copy-start | bytes 2408452
  1.3 20.0 %collective-permute-start = (bf16[2,256,448]{2,1,0:T(8,128)(2,1)S(1)}, bf16[2,256,448]{2,1,0:T(8,128)(2,1)S(1)}, u32[]{:S(2)}, u32[]{:S(2)}) collective-permute-start(bf16[2,256,448]{2,1,0:T(8,128)(2,1)S(1)} %rows.1._), channel_id=1, source_target_pairs={{4,8},{8,4},{12,16},{16,12},{20,24},{24,20},{5,9},{9,5},{13,17},{1... | collective-permute-start | bytes 1376264 | tf_op jit(solution)/shard_map/ppermute | solution.py:47
  4.8 11.0 %collective-permute-start.1 = (bf16[2,448,240]{2,1,0:T(8,128)(2,1)S(1)}, bf16[2,448,240]{2,1,0:T(8,128)(2,1)S(1)}, u32[]{:S(2)}, u32[]{:S(2)}) collective-permute-start(bf16[2,448,240]{2,1,0:T(8,128)(2,1)S(1)} %get-tuple-element.27), channel_id=1, source_target_pairs={{0,1},{1,0},{2,3},{3,2},{4,5},{5,4},{6,7},{7,6},{8,9},{9,8},{10,11... | collective-permute-start | bytes 1290248 | tf_op jit(solution)/shard_map/ppermute | solution.py:47
  5.8 10.1 %collective-permute-start.2 = (bf16[2,448,240]{2,1,0:T(8,128)(2,1)S(1)}, bf16[2,448,240]{2,1,0:T(8,128)(2,1)S(1)}, u32[]{:S(2)}, u32[]{:S(2)}) collective-permute-start(bf16[2,448,240]{2,1,0:T(8,128)(2,1)S(1)} %get-tuple-element.28), channel_id=1, source_target_pairs={{1,2},{2,1},{5,6},{6,5},{9,10},{10,9},{13,14},{14,13},{17,18},{18,... | collective-permute-start | bytes 1290248 | tf_op jit(solution)/shard_map/ppermute | solution.py:47
  8.9 12.8 %collective-permute-start.5 = (bf16[2,240,240]{2,1,0:T(8,128)(2,1)S(1)}, bf16[2,240,240]{2,1,0:T(8,128)(2,1)S(1)}, u32[]{:S(2)}, u32[]{:S(2)}) collective-permute-start(bf16[2,240,240]{2,1,0:T(8,128)(2,1)S(1)} %get-tuple-element.31), channel_id=1, source_target_pairs={{5,10},{10,5},{6,9},{9,6},{13,18},{18,13},{14,17},{17,14},{21,26},... | collective-permute-start | bytes 691208 | tf_op jit(solution)/shard_map/ppermute | solution.py:58
  17.5 2.5 %copy-start.2 = (f32[448,448]{1,0:T(8,128)S(1)}, f32[448,448]{1,0:T(8,128)}, u32[]{:S(2)}) copy-start(f32[448,448]{1,0:T(8,128)} %slow_ref.1) | copy-start | bytes 2408452
  17.5 7.1 %collective-permute-start.3 = (bf16[4,2,16,256]{3,2,1,0:T(8,128)(2,1)S(1)}, bf16[4,2,16,256]{3,2,1,0:T(8,128)(2,1)S(1)}, u32[]{:S(2)}, u32[]{:S(2)}) collective-permute-start(bf16[4,2,16,256]{3,2,1,0:T(8,128)(2,1)S(1)} %get-tuple-element.30._), channel_id=1, source_target_pairs={{0,4},{4,0},{8,12},{12,8},{16,20},{20,16},{24,28},{28,24},{1,5},{5... | collective-permute-start | bytes 196616 | tf_op jit(solution)/shard_map/ppermute | solution.py:47
  19.0 14.2 %collective-permute-start.6 = (bf16[2,256,512]{2,1,0:T(8,128)(2,1)S(1)}, bf16[2,256,512]{2,1,0:T(8,128)(2,1)S(1)}, u32[]{:S(2)}, u32[]{:S(2)}) collective-permute-start(bf16[2,256,512]{2,1,0:T(8,128)(2,1)S(1)} %get-tuple-element.34.refs_2_), channel_id=1, source_target_pairs={{0,4},{4,0},{8,12},{12,8},{16,20},{20,16},{24,28},{28,24},{1,5},{5... | collective-permute-start | bytes 1572872 | tf_op jit(solution)/shard_map/ppermute | solution.py:47
  21.3 3.3 %collective-permute-start.4 = (bf16[2,240,240]{2,1,0:T(8,128)(2,1)S(1)}, bf16[2,240,240]{2,1,0:T(8,128)(2,1)S(1)}, u32[]{:S(2)}, u32[]{:S(2)}) collective-permute-start(bf16[2,240,240]{2,1,0:T(8,128)(2,1)S(1)} %corner.1), channel_id=1, source_target_pairs={{0,1},{1,0},{2,3},{3,2},{4,5},{5,4},{6,7},{7,6},{8,9},{9,8},{10,11... | collective-permute-start | bytes 691208 | tf_op jit(solution)/shard_map/ppermute | solution.py:47
  28.1 6.5 %collective-permute-start.8 = (bf16[2,16,512]{2,1,0:T(8,128)(2,1)S(1)}, bf16[2,16,512]{2,1,0:T(8,128)(2,1)S(1)}, u32[]{:S(2)}, u32[]{:S(2)}) collective-permute-start(bf16[2,16,512]{2,1,0:T(8,128)(2,1)S(1)} %get-tuple-element.42), channel_id=1, source_target_pairs={{4,8},{8,4},{12,16},{16,12},{20,24},{24,20},{5,9},{9,5},{13,17},{1... | collective-permute-start | bytes 98312 | tf_op jit(solution)/shard_map/ppermute | solution.py:47
  31.2 3.4 %collective-permute-start.7 = (bf16[2,16,480]{2,1,0:T(8,128)(2,1)S(1)}, bf16[2,16,480]{2,1,0:T(8,128)(2,1)S(1)}, u32[]{:S(2)}, u32[]{:S(2)}) collective-permute-start(bf16[2,16,480]{2,1,0:T(8,128)(2,1)S(1)} %get-tuple-element.41), channel_id=1, source_target_pairs={{0,4},{4,0},{8,12},{12,8},{16,20},{20,16},{24,28},{28,24},{1,5},{5... | collective-permute-start | bytes 92168 | tf_op jit(solution)/shard_map/ppermute | solution.py:47
  34.9 5.9 %collective-permute-start.10 = (bf16[2,16,448]{2,1,0:T(8,128)(2,1)S(1)}, bf16[2,16,448]{2,1,0:T(8,128)(2,1)S(1)}, u32[]{:S(2)}, u32[]{:S(2)}) collective-permute-start(bf16[2,16,448]{2,1,0:T(8,128)(2,1)S(1)} %get-tuple-element.46), channel_id=1, source_target_pairs={{1,2},{2,1},{5,6},{6,5},{9,10},{10,9},{13,14},{14,13},{17,18},{18,... | collective-permute-start | bytes 86024 | tf_op jit(solution)/shard_map/ppermute | solution.py:47
  39.2 1.6 %collective-permute-start.9 = (bf16[2,16,448]{2,1,0:T(8,128)(2,1)S(1)}, bf16[2,16,448]{2,1,0:T(8,128)(2,1)S(1)}, u32[]{:S(2)}, u32[]{:S(2)}) collective-permute-start(bf16[2,16,448]{2,1,0:T(8,128)(2,1)S(1)} %get-tuple-element.45), channel_id=1, source_target_pairs={{0,1},{1,0},{2,3},{3,2},{4,5},{5,4},{6,7},{7,6},{8,9},{9,8},{10,11... | collective-permute-start | bytes 86024 | tf_op jit(solution)/shard_map/ppermute | solution.py:47

commit v4 on v3

--- a/solution.py
+++ b/solution.py
@@ -75,7 +75,7 @@
     return copies
 
 
-def list_tables(all_reach_ref, all_coup_ref, all_group_ref, table_ref):
+def list_tables(all_reach_ref, all_coup_ref, all_group_ref, place_ref, weight_ref):
     slots, total_y, total_x = all_reach_ref.shape
     odd_x = parity("gx")
     base_x = lax.axis_index("gx") * 2
@@ -84,18 +84,20 @@
         for col in range(4):
             x = jnp.clip(base_x - 1 + row, 0, total_x - 1)
             y = jnp.clip(base_y - 1 + col, 0, total_y - 1)
-            table_ref[row * 4 + col] = all_group_ref[y, x].astype(F32)
+            place_ref[row * 4 + col] = all_group_ref[y, x]
     for row in range(3):
         for col in range(2):
             x, y = base_x - odd_x + row, base_y + col
+            here = (row - odd_x + 1) * 4 + col + 1
             for slot in range(slots):
                 reach = all_reach_ref[slot, y, x]
-                place = (lax.div(reach, total_y) - base_x + 1) * 4
-                place += lax.rem(reach, total_y) - base_y + 1
-                at = 16 + ((row * 2 + col) * slots + slot) * 3
-                table_ref[at] = jnp.where(reach >= 0, place, -1).astype(F32)
-                table_ref[at + 1] = all_coup_ref[col, slot, 0, x]
-                table_ref[at + 2] = all_coup_ref[col, slot, 1, x]
+                step = reach - (x * total_y + y)
+                down = jnp.where(step > 1, 1, jnp.where(step < -1, -1, 0))
+                place = here + step + down * (4 - total_y)
+                at = (row * 2 + col) * slots + slot
+                place_ref[16 + at] = jnp.where(reach >= 0, place, -1)
+                weight_ref[at * 2] = all_coup_ref[col, slot, 0, x]
+                weight_ref[at * 2 + 1] = all_coup_ref[col, slot, 1, x]
 
 
 def folded_kernel(
@@ -108,17 +110,18 @@
     row_ref,
     left_ref,
     strip_ref,
-    table_any,
+    place_any,
+    weight_any,
     reach_ref,
     coup_ref,
     group_ref,
-    table_ref,
+    place_ref,
+    weight_ref,
     sems,
 ):
     columns = pl.ds(lax.axis_index("gy") * 2, 2)
     pairs = ((reach_any, reach_ref), (coup_any.at[columns], coup_ref), (group_any, group_ref))
     copies = fetch(pairs, sems)
-    out_copy = pltpu.make_async_copy(table_ref, table_any, sems.at[len(copies)])
     groups, _, _, length, _ = prop_ref.shape
     strip_ref[...] = jnp.zeros_like(strip_ref)
     curve = jnp.broadcast_to(row_ref[...], (length, length))
@@ -128,8 +131,8 @@
         if g == groups - 1:
             for copy in copies:
                 copy.wait()
-            list_tables(reach_ref, coup_ref, group_ref, table_ref)
-            out_copy.start()
+            list_tables(reach_ref, coup_ref, group_ref, place_ref, weight_ref)
+            outward = fetch(((place_ref, place_any), (weight_ref, weight_any)), sems.at[3:])
         for part in range(2):
             half = dot(prop_ref[g, 0, part], cos_ref[...])
             high = half.astype(BF16)
@@ -141,9 +144,10 @@
             high = slice(length // 2 + g * OVER, length // 2 + (g + 1) * OVER)
             strip_ref[part, :, low] = strip
             strip_ref[1 - part, :, high] = strip if part == 0 else -strip
-    out_copy.wait()
-
-def right_kernel(left_ref, _, right_ref):
+    for copy in outward:
+        copy.wait()
+
+def right_kernel(left_ref, right_ref):
     groups, _, length, _ = left_ref.shape
     wide = right_ref.shape[-1]
     inner = wide - 2 * OVER
@@ -176,22 +180,24 @@
 def fold(propagator, cosines, bell, reach_list, coupling, window_velocity_group):
     groups, _, _, length, _ = propagator.shape
     slots = reach_list.shape[2]
-    entries = 16 + 18 * slots
+    entries = 6 * slots
     return pl.pallas_call(
         folded_kernel,
         out_shape=(
             pltpu.VMEM((groups, 2, length, length), BF16),
             pltpu.VMEM((2, length, length), BF16),
-            jax.ShapeDtypeStruct((entries,), F32),
+            jax.ShapeDtypeStruct((16 + entries,), jnp.int32),
+            jax.ShapeDtypeStruct((2 * entries,), F32),
         ),
         in_specs=[ANY] * 3 + [VMEM] * 4,
-        out_specs=(VMEM,) * 2 + (ANY,),
+        out_specs=(VMEM,) * 2 + (ANY,) * 2,
         scratch_shapes=[
             pltpu.SMEM(reach_list.shape[::-1], jnp.int32),
             pltpu.SMEM((2, slots, 2, coupling.shape[0]), F32),
             pltpu.SMEM(window_velocity_group.shape[::-1], jnp.int32),
-            pltpu.SMEM((entries,), F32),
-            pltpu.SemaphoreType.DMA((4,)),
+            pltpu.SMEM((16 + entries,), jnp.int32),
+            pltpu.SMEM((2 * entries,), F32),
+            pltpu.SemaphoreType.DMA((5,)),
         ],
         compiler_params=PARAMS,
         cost_estimate=cost(0.1),
@@ -209,13 +215,13 @@
 
 def spread(west, middle, east, part):
     span = west.shape[2]
-    wide = middle.shape[2]
+    wide = 2 * (span - HALF)
     left, centre, right = west[part], middle[part], east[part]
     return (
         jnp.concatenate([left, centre[:, :HALF]], axis=1),
         jnp.concatenate([left[:, span - HALF :], centre[:, :span]], axis=1),
-        jnp.concatenate([centre[:, wide - span :], right[:, :HALF]], axis=1),
-        jnp.concatenate([centre[:, wide - HALF :], right], axis=1),
+        jnp.concatenate([centre[:, wide - span : wide], right[:, :HALF]], axis=1),
+        jnp.concatenate([centre[:, wide - HALF : wide], right], axis=1),
     )
 
 
@@ -247,20 +253,24 @@
 
 
 class Lists:
-    def __init__(self, table_ref, copy, slots):
-        self.table_ref, self.copy, self.slots = table_ref, copy, slots
+    def __init__(self, place_ref, weight_ref, copies, slots):
+        self.place_ref, self.weight_ref = place_ref, weight_ref
+        self.copies, self.slots = copies, slots
         self.odd_x = parity("gx")
 
+    def wait(self):
+        for copy in self.copies:
+            copy.wait()
+
     def group_at(self, place):
-        return self.table_ref[place].astype(jnp.int32)
+        return self.place_ref[place]
 
     def window(self, row, col):
         return (row + 1) * 4 + col + 1
 
     def entry(self, row, col, slot):
-        at = 16 + (((row + self.odd_x) * 2 + col) * self.slots + slot) * 3
-        reach = self.table_ref[at].astype(jnp.int32)
-        return reach, self.table_ref[at + 1], self.table_ref[at + 2]
+        at = ((row + self.odd_x) * 2 + col) * self.slots + slot
+        return self.place_ref[16 + at], self.weight_ref[at * 2], self.weight_ref[at * 2 + 1]
 
     def weight_of(self, row, col, source):
         real, imag = jnp.float32(0), jnp.float32(0)
@@ -274,11 +284,11 @@
         reach, c_real, c_imag = self.entry(row, col, slot)
         live = reach >= 0
         source = jnp.where(live, reach, self.window(row, col))
-        at_row = source // 4
+        at_row = source >> 2
         at_x = jnp.where(self.odd_x == 0, at_row, 3 - at_row)
         real = jnp.where(live, c_real, 0.0)
         imag = jnp.where(live, c_imag, 0.0)
-        return self.group_at(source), at_x, source % 4, real, imag
+        return self.group_at(source), at_x, source & 3, real, imag
 
 
 def pack_sides(block, near_ref, far_ref):
@@ -295,7 +305,9 @@
 def rows_kernel(wave_ref, x_ref):
     tile, span = wave_ref.shape[2], x_ref.shape[1]
     for part in range(2):
-        x_ref[part] = wave_ref[part, 0, pl.ds(start_of(parity("gx"), 0, tile - span), span)]
+        rows = pl.ds(start_of(parity("gx"), 0, tile - span), span)
+        x_ref[part, :, :tile] = wave_ref[part, 0, rows]
+        x_ref[part, :, tile:] = jnp.zeros((span, x_ref.shape[2] - tile), BF16)
 
 
 def cols_kernel(wave_ref, _, near_ref, far_ref, corner_ref):
@@ -305,13 +317,12 @@
     corner_ref[...] = far_ref[:, rows]
 
 
-def corner_kernel(x_ref, near_ref):
+def corner_kernel(x_ref, _, near_ref):
     width = near_ref.shape[2]
-    start = x_ref.shape[2] - width
-    rows = pl.ds(start_of(parity("gx"), HALF, 0), near_ref.shape[1])
+    start = 2 * (width - HALF) - width
 
     def store(cols):
-        near_ref[...] = x_ref[:, rows, cols]
+        near_ref[...] = x_ref[:, :, cols]
 
     each_way(
         parity("gy"), lambda: store(slice(start, start + width)), lambda: store(slice(0, width))
@@ -337,7 +348,18 @@
 
 
 def edge_kernel(
-    lists, wave_ref, ye_ref, yo_ref, left_ref, frame_ref, part_ref, swept_ref, rim_ref
+    lists,
+    wave_ref,
+    ye_ref,
+    yo_ref,
+    left_ref,
+    _,
+    frame_ref,
+    send_ref,
+    border_ref,
+    swept_ref,
+    rim_ref,
+    part_ref,
 ):
     length = left_ref.shape[-1]
     tile = wave_ref.shape[2]
@@ -346,7 +368,7 @@
     for at in range(4):
         for part in range(2):
             rim_ref[at, part] = frame_ref[at, part, edge]
-    lists.copy.wait()
+    lists.wait()
     beyond = jnp.where(lists.odd_x == 0, 2, -1)
     mine = jnp.where(lists.odd_x == 0, 1, 0)
     rows = pl.ds(window_rows(lists.odd_x, 2, length), length)
@@ -366,17 +388,21 @@
             part_ref[1, rows, cols] = imag.astype(BF16)
 
         mix(None, terms, store)
+    span = length - HALF
+    inner, outer = start_of(lists.odd_x, HALF, 0), start_of(lists.odd_x, 0, span)
+    for part in range(2):
+        send_ref[part] = part_ref[part, pl.ds(inner, span)]
+        border_ref[part] = part_ref[part, pl.ds(outer, HALF)]
 
 
 def early_kernel(
-    lists, frame_ref, left_ref, gave_ref, right_ref, _, __, ___, sum_ref, echo_ref, swept_ref
+    lists, frame_ref, left_ref, gave_ref, right_ref, _, sum_ref, echo_ref, swept_ref
 ):
     length = left_ref.shape[-1]
-    lists.copy.wait()
+    lists.wait()
     beyond = jnp.where(lists.odd_x == 0, 2, -1)
-    edge = pl.ds(start_of(lists.odd_x, 0, length - HALF), HALF)
     groups = [lists.group_at(lists.window(beyond, col)) for col in range(2)]
-    turn(halves(gave_ref, edge), right_ref, groups, echo_ref)
+    turn(halves(gave_ref, slice(None)), right_ref, groups, echo_ref)
     rows = pl.ds(window_rows(lists.odd_x, 1, length), length)
     for at in range(4):
         matrix_ref = left_ref.at[lists.group_at(lists.window(lists.odd_x, at - 1))]
@@ -448,7 +474,6 @@
     odd_x, odd_y = lists.odd_x, parity("gy")
     at_o, hole_o = start_of(odd_x, 0, HALF), start_of(odd_x, span, 0)
     lean_o, lean_e = start_of(odd_x, 0, HALF), start_of(odd_x, HALF, 0)
-    xo_ref = xo_ref.at[:, pl.ds(start_of(odd_x, HALF, 0), span)]
     strip_ref[...] = jnp.zeros_like(strip_ref)
 
     def fill(west, east):
@@ -467,7 +492,7 @@
             strip_ref[0, at, part, pl.ds(lean_e, HALF)] = frame_ref[at, part, pl.ds(near_o, HALF)]
             strip_ref[3, at, part, pl.ds(lean_o, HALF)] = frame_ref[at, part, pl.ds(near_e, HALF)]
 
-    lists.copy.wait()
+    lists.wait()
     beyond = jnp.where(odd_x == 0, -1, 2)
     places = [lists.window(beyond, at - 1) for at in range(4)]
     for at, place in enumerate(places):
@@ -530,20 +555,19 @@
 
 
 def join_kernel(lists, mid_ref, rest_ref, got_ref, right_ref, full_ref, sum_ref, out_ref):
-    length = got_ref.shape[1]
-    span = length - HALF
+    span = got_ref.shape[1]
     tile = full_ref.shape[1]
     odd_x = lists.odd_x
-    mine = jnp.where(odd_x == 0, 1, 0)
+    rows = pl.ds(start_of(odd_x, 0, HALF), span)
     for part in range(2):
-        sum_ref[part] = (rest_ref[part] + got_ref[part].astype(F32)).astype(BF16)
-    lists.copy.wait()
-    groups = [lists.group_at(lists.window(mine, col)) for col in range(2)]
+        sum_ref[part] = (rest_ref[part, rows] + got_ref[part].astype(F32)).astype(BF16)
+    lists.wait()
+    groups = [lists.group_at(lists.window(1 - odd_x, col)) for col in range(2)]
     turn(halves(sum_ref, slice(None)), right_ref, groups, out_ref)
     alone = tile - span
     both = slice(alone, span)
-    source, target = start_of(odd_x, span - alone, HALF), start_of(odd_x, span, 0)
-    shared = start_of(odd_x, 0, HALF + alone)
+    source, target = start_of(odd_x, span - alone, 0), start_of(odd_x, span, 0)
+    shared = start_of(odd_x, 0, alone)
     for part in range(2):
         full_ref[part, pl.ds(target, alone)] = out_ref[part, pl.ds(source, alone)]
         full_ref[part, both] = (
@@ -625,11 +649,10 @@
 
 
 def phase_kernel(freq_ref, slow_ref, _, cos_ref, sin_ref):
-    angle = freq_ref[...] * slow_ref[...]
+    angle = freq_ref[0] * slow_ref[...]
     turns = jnp.round(angle * (2.0 / math.pi))
-    rest = angle - turns * 1.5703125
-    rest = rest - turns * 4.8375129699707031e-4
-    rest = rest - turns * 7.5495138331e-8
+    rest = angle - turns * 1.57080078125
+    rest = rest + turns * 4.45445510338e-6
     square = rest * rest
     sine = rest + rest * square * (
         -1.6666654611e-1 + square * (8.3321608736e-3 - square * 1.9515295891e-4)
@@ -659,7 +682,7 @@
 
     x_send = pl.pallas_call(
         rows_kernel,
-        out_shape=shape(2, span + HALF, tile_cols),
+        out_shape=shape(2, span, tile_cols + 8),
         in_specs=[VMEM],
         out_specs=VMEM,
         compiler_params=PARAMS,
@@ -681,7 +704,7 @@
     z_far = far_corner(corner)
     y_near = swap(near, "gy", False)
 
-    left, strip, table = fold(
+    left, strip, *tables = fold(
         propagator,
         cosine_table(length),
         bell_curve(length, OVER),
@@ -690,61 +713,74 @@
         window_velocity_group,
     )
     def call(kernel, name, micros, out_shape, inputs, scratch=(), **options):
-        def body(table_any, *refs):
-            *refs, table_ref, sem = refs
-            copy = pltpu.make_async_copy(table_any, table_ref, sem)
-            copy.start()
-            kernel(Lists(table_ref, copy, slots), *refs)
+        def body(*refs):
+            *refs, place_ref, weight_ref, sems = refs
+            copies = fetch(((refs[0], place_ref), (refs[1], weight_ref)), sems)
+            kernel(Lists(place_ref, weight_ref, copies, slots), *refs[2:])
 
         specs = options.pop("in_specs", [VMEM] * len(inputs))
         outs = options.pop("out_specs", jax.tree.map(lambda _: VMEM, out_shape))
         return pl.pallas_call(
             body,
             out_shape=out_shape,
-            in_specs=[ANY] + specs,
+            in_specs=[ANY] * 2 + specs,
             out_specs=outs,
             scratch_shapes=list(scratch)
-            + [pltpu.SMEM(table.shape, F32), pltpu.SemaphoreType.DMA(())],
+            + [pltpu.SMEM(table.shape, table.dtype) for table in tables]
+            + [pltpu.SemaphoreType.DMA((2,))],
             compiler_params=PARAMS,
             name=name,
             cost_estimate=cost(micros),
             **options,
-        )(table, *inputs)
-
-    frame, given, swept, rim_send = call(
+        )(*tables, *inputs)
+
+    right = pl.pallas_call(
+        right_kernel,
+        out_shape=shape(left.shape[0], 2, 2, length, wide),
+        in_specs=[VMEM],
+        out_specs=VMEM,
+        compiler_params=PARAMS,
+        cost_estimate=cost(0.01),
+        name="right",
+    )(left)
+    frame, given, gave, swept, rim_send = call(
         edge_kernel,
         "edge",
         0.001,
         (
             shape(4, 2, tile_rows + OVER, length),
-            shape(2, length, wide),
+            shape(2, span, wide),
+            shape(2, HALF, wide),
             shape(2, 4, 2, length, length, kind=F32),
             shape(4, 2, HALF, length),
         ),
-        (wavefield, y_near, y_far, left),
+        (wavefield, y_near, y_far, left, right),
+        (pltpu.VMEM((2, length, wide), BF16),),
+        in_specs=[VMEM] * 4 + [ANY],
     )
     rim = swap(rim_send, "gx", False)
     got = swap(given, "gx", False)
 
-    right = pl.pallas_call(
-        right_kernel,
-        out_shape=shape(left.shape[0], 2, 2, length, wide),
-        in_specs=[VMEM, ANY],
-        out_specs=VMEM,
-        compiler_params=PARAMS,
-        cost_estimate=cost(0.01),
-        name="right",
-    )(left, rim_send)
     cos_phase, sin_phase = pl.pallas_call(
         phase_kernel,
         out_shape=(shape(tile_rows, tile_cols, kind=F32),) * 2,
-        in_specs=[VMEM] * 2 + [ANY],
+        in_specs=[SMEM, VMEM, ANY],
         out_specs=(VMEM,) * 2,
         compiler_params=PARAMS,
         cost_estimate=cost(0.01),
         name="phase",
-    )(jnp.broadcast_to(frequencies[:, None], (1, tile_cols)), slowness, rim_send)
-
+    )(frequencies, slowness, rim_send)
+
+    corner_near = pl.pallas_call(
+        corner_kernel,
+        out_shape=shape(2, span, span),
+        in_specs=[VMEM, ANY],
+        out_specs=VMEM,
+        compiler_params=PARAMS,
+        cost_estimate=cost(0.2),
+        name="corner",
+    )(x_odd, rim_send)
+    z_near = swap(corner_near, "gy", False)
     early, echo, _ = call(
         early_kernel,
         "early",
@@ -754,20 +790,9 @@
             shape(2, HALF, wide, kind=F32),
             shape(2, 4, 2, length, length, kind=F32),
         ),
-        (frame, left, given, right, swept, z_far, cos_phase),
-        in_specs=[VMEM] * 5 + [ANY] * 2,
-        input_output_aliases={5: 2},
-    )
-    near = pl.pallas_call(
-        corner_kernel,
-        out_shape=shape(2, span, span),
-        in_specs=[VMEM],
-        out_specs=VMEM,
-        compiler_params=PARAMS,
-        cost_estimate=cost(0.2),
-        name="corner",
-    )(x_odd)
-    z_near = swap(near, "gy", False)
+        (frame, left, gave, right, swept),
+        input_output_aliases={6: 2},
+    )
     mid, rest, send_o, send_e = call(
         late_kernel,
         "late",
@@ -799,10 +824,10 @@
         shape(2, tile_rows, wide, kind=F32),
         (mid, rest, got, right),
         (
-            pltpu.VMEM((2, length, wide), BF16),
-            pltpu.VMEM((2, length, wide), F32),
+            pltpu.VMEM((2, span, wide), BF16),
+            pltpu.VMEM((2, span, wide), F32),
         ),
-        input_output_aliases={1: 0},
+        input_output_aliases={2: 0},
     )
     full, send_e, send_o = pl.pallas_call(
         border_kernel,

time: 42.9 us -> 42.5 us (level)
  the two profiles are of different devices: /device:TPU:9 before, /device:TPU:0 now
where the time goes in v4:
time: 42.5 us; the launch traced here: 42.2 us
  starting transfers between devices  22.4 us (53%)
  Pallas kernels  17.2 us (40%)
  local copies, waits for them, and re-layouts  1.47 us (3%)
  between operations  1.12 us (3%)
    ppermute x10, starting transfers between devices, swap(): return lax.ppermute(block, axis, pairs)  21.7 us
    pallas_call x4, Pallas kernels, call(): pl.pallas_call(body, out_shape=out_shape, in_specs=[ANY] * 2 + specs, out...  9.39 us
    pallas_call x1, Pallas kernels, fold(): pl.pallas_call(folded_kernel, out_shape=(pltpu.VMEM((groups, 2, length, l...  2.57 us
    unnamed x20, local copies, waits for them, and re-layouts  1.47 us
    pallas_call x1, Pallas kernels, per_device(): pl.pallas_call(phase_kernel, out_shape=(shape(tile_rows, tile_cols, kind=...  1.21 us
    pallas_call x1, Pallas kernels, per_device(): pl.pallas_call(outer_kernel, out_shape=result, in_specs=[ANY] + [VMEM] *...  1.12 us
    pallas_call x1, Pallas kernels, per_device(): pl.pallas_call(inner_kernel, grid=(count - 2,), out_shape=result, in_spec...  1.11 us
    pallas_call x1, Pallas kernels, per_device(): pl.pallas_call(right_kernel, out_shape=shape(left.shape[0], 2, 2, length,...  0.89 us
  transfers between devices with their start and end apart: 11, of which 0 were waited for; matrix products, arithmetic and copies ran while one was open for 0% of the time, Pallas kernels for 37%

profile of v4, /device:TPU:0, one launch (start us, length us, event | category | flops | bytes accessed | tf_op | source)
XLA Modules:
  0.0 42.2 jit_solution(8594448852265107235)
XLA Ops:
  0.0 1.2 %copy-done = bf16[2,1,448,448]{3,2,1,0:T(8,128)(2,1)S(1)} copy-done((bf16[2,1,448,448]{3,2,1,0:T(8,128)(2,1)S(1)}, bf16[2,1,448,448]{3,2,1,0:T(8,128)(2,1)}, u32[]{:S(2)}) %copy-start) | copy-done | bytes 802840
  1.2 0.0 copy-start.7
  1.2 0.0 copy-start.8
  1.2 0.0 copy-start.9
  1.2 0.1 rows.1._
  1.3 0.8 %collective-permute-start = (bf16[2,240,456]{2,1,0:T(8,128)(2,1)S(1)}, bf16[2,240,456]{2,1,0:T(8,128)(2,1)S(1)}, u32[]{:S(2)}, u32[]{:S(2)}) collective-permute-start(bf16[2,240,456]{2,1,0:T(8,128)(2,1)S(1)} %rows.1._), channel_id=1, source_target_pairs={{4,8},{8,4},{12,16},{16,12},{20,24},{24,20},{5,9},{9,5},{13,17},{1... | collective-permute-start | bytes 1313288 | tf_op jit(solution)/shard_map/ppermute | solution.py:47
  2.1 0.3 cols.1
  2.5 0.5 %collective-permute-start.1 = (bf16[2,448,240]{2,1,0:T(8,128)(2,1)S(1)}, bf16[2,448,240]{2,1,0:T(8,128)(2,1)S(1)}, u32[]{:S(2)}, u32[]{:S(2)}) collective-permute-start(bf16[2,448,240]{2,1,0:T(8,128)(2,1)S(1)} %get-tuple-element.30), channel_id=1, source_target_pairs={{0,1},{1,0},{2,3},{3,2},{4,5},{5,4},{6,7},{7,6},{8,9},{9,8},{10,11... | collective-permute-start | bytes 1290248 | tf_op jit(solution)/shard_map/ppermute | solution.py:47
  3.0 0.7 %collective-permute-start.2 = (bf16[2,448,240]{2,1,0:T(8,128)(2,1)S(1)}, bf16[2,448,240]{2,1,0:T(8,128)(2,1)S(1)}, u32[]{:S(2)}, u32[]{:S(2)}) collective-permute-start(bf16[2,448,240]{2,1,0:T(8,128)(2,1)S(1)} %get-tuple-element.31), channel_id=1, source_target_pairs={{1,2},{2,1},{5,6},{6,5},{9,10},{10,9},{13,14},{14,13},{17,18},{18,... | collective-permute-start | bytes 1290248 | tf_op jit(solution)/shard_map/ppermute | solution.py:47
  3.7 0.7 %collective-permute-start.5 = (bf16[2,240,240]{2,1,0:T(8,128)(2,1)S(1)}, bf16[2,240,240]{2,1,0:T(8,128)(2,1)S(1)}, u32[]{:S(2)}, u32[]{:S(2)}) collective-permute-start(bf16[2,240,240]{2,1,0:T(8,128)(2,1)S(1)} %get-tuple-element.34), channel_id=1, source_target_pairs={{5,10},{10,5},{6,9},{9,6},{13,18},{18,13},{14,17},{17,14},{21,26},... | collective-permute-start | bytes 691208 | tf_op jit(solution)/shard_map/ppermute | solution.py:58
  4.4 0.0 copy-done.3
  4.4 0.0 copy-done.4
  4.4 0.0 copy-done.5
  4.4 0.0 copy-done.6
  4.4 0.0 copy-done.7
  4.4 0.0 copy-done.8
  4.4 2.6 %fold.1 = (bf16[3,2,256,256]{3,2,1,0:T(8,128)(2,1)S(1)}, bf16[2,256,256]{2,1,0:T(8,128)(2,1)S(1)}, s32[46]{0:T(128)S(1)}, f32[60]{0:T(128)S(1)}) custom-call(s32[5,8,16]{2,1,0:T(8,128)S(1)} %bitcast.4, f32[8,5,2,16]{3,2,1,0:T(2,128)S(1)} %bitcast.3, s32[8,16]{1,0:T(8,128)S(1)} %bitcast.5, bf16[3,1,2,256,256]{4,3,2,1,0:T(8,128)(2,1)S(1)} %copy-done.3, ...), custom_call_target="tpu_custom_call" | custom-call | flops 110000000 | bytes 360000 | tf_op jit(solution)/shard_map/fold/pallas_call | solution.py:184
  7.0 0.0 copy-start.1
  7.0 0.9 %right.1.refs_6_.refs_5_.refs_10_ = bf16[3,2,2,256,512]{4,3,2,1,0:T(8,128)(2,1)S(1)} custom-call(bf16[3,2,256,256]{3,2,1,0:T(8,128)(2,1)S(1)} %get-tuple-element.32.left_ref.refs_5_.refs_3_.refs_6_), custom_call_target="tpu_custom_call" | custom-call | flops 11000000 | bytes 36000 | tf_op jit(solution)/shard_map/right/pallas_call | solution.py:737
  7.9 0.0 collective-permute-done.1.refs_3_
  7.9 0.0 collective-permute-done.2.refs_4_
  7.9 0.2 copy-done.1
  8.2 1.8 %edge.1 = (bf16[4,2,480,256]{3,2,1,0:T(8,128)(2,1)S(1)}, bf16[2,240,512]{2,1,0:T(8,128)(2,1)S(1)}, bf16[2,16,512]{2,1,0:T(8,128)(2,1)S(1)}, f32[2,4,2,256,256]{4...) custom-call(s32[46]{0:T(128)S(1)} %get-tuple-element.28.refs_0_, f32[60]{0:T(128)S(1)} %get-tuple-element.29.refs_1_, ...), custom_call_target="tpu_custom_call" | custom-call | flops 1100000 | bytes 3600 | tf_op jit(solution)/shard_map/edge/pallas_call | solution.py:723
  10.0 5.3 %collective-permute-start.3 = (bf16[4,2,16,256]{3,2,1,0:T(8,128)(2,1)S(1)}, bf16[4,2,16,256]{3,2,1,0:T(8,128)(2,1)S(1)}, u32[]{:S(2)}, u32[]{:S(2)}) collective-permute-start(bf16[4,2,16,256]{3,2,1,0:T(8,128)(2,1)S(1)} %get-tuple-element.33._), channel_id=1, source_target_pairs={{0,4},{4,0},{8,12},{12,8},{16,20},{20,16},{24,28},{28,24},{1,5},{5... | collective-permute-start | bytes 196616 | tf_op jit(solution)/shard_map/ppermute | solution.py:47
  15.3 0.1 collective-permute-start.6
  15.3 0.0 collective-permute-done.x_ref.refs_2_
  15.3 0.2 corner.1
  15.5 5.1 %collective-permute-start.4 = (bf16[2,240,240]{2,1,0:T(8,128)(2,1)S(1)}, bf16[2,240,240]{2,1,0:T(8,128)(2,1)S(1)}, u32[]{:S(2)}, u32[]{:S(2)}) collective-permute-start(bf16[2,240,240]{2,1,0:T(8,128)(2,1)S(1)} %corner.1), channel_id=1, source_target_pairs={{0,1},{1,0},{2,3},{3,2},{4,5},{5,4},{6,7},{7,6},{8,9},{9,8},{10,11... | collective-permute-start | bytes 691208 | tf_op jit(solution)/shard_map/ppermute | solution.py:47
  20.7 3.0 %early.1 = (f32[2,2,2,256,256]{4,3,2,1,0:T(8,128)S(1)}, f32[2,16,512]{2,1,0:T(8,128)S(1)}, f32[2,4,2,256,256]{4,3,2,1,0:T(8,128)S(1)}) custom-call(s32[46]{0:T(128)S(1)} %get-tuple-element.28.refs_0_, f32[60]{0:T(128)S(1)} %get-tuple-element.29.refs_1_, ...), custom_call_target="tpu_custom_call", output_to_operand_aliasing={{2}: (6, {})} | custom-call | flops 3300000000 | bytes 10800000 | tf_op jit(solution)/shard_map/early/pallas_call | solution.py:723
  23.7 0.0 collective-permute-done.5.refs_5_
  23.7 0.0 collective-permute-done.3.refs_3_
  23.7 0.0 collective-permute-done.4.refs_4_
  23.7 0.0 copy-start.2
  23.7 3.2 %late.1 = (f32[2,448,512]{2,1,0:T(8,128)S(1)}, f32[2,256,512]{2,1,0:T(8,128)S(1)}, bf16[2,16,512]{2,1,0:T(8,128)(2,1)S(1)}, bf16[2,16,480]{2,1,0:T(8,128)(2,1)S(1)}) custom-call(s32[46]{0:T(128)S(1)} %get-tuple-element.28.refs_0_, f32[60]{0:T(128)S(1)} %get-tuple-element.29.refs_1_, bf16[2,240,456]{2,1,0:T(8,128)(2,1)S(1)} %collective-permute-done.x_ref.refs_2_, ...), custom_call_target="tpu_custom_call" | custom-call | flops 4400000000 | bytes 14400000 | tf_op jit(solution)/shard_map/late/pallas_call | solution.py:723
  27.0 0.8 %collective-permute-start.8 = (bf16[2,16,512]{2,1,0:T(8,128)(2,1)S(1)}, bf16[2,16,512]{2,1,0:T(8,128)(2,1)S(1)}, u32[]{:S(2)}, u32[]{:S(2)}) collective-permute-start(bf16[2,16,512]{2,1,0:T(8,128)(2,1)S(1)} %get-tuple-element.45), channel_id=1, source_target_pairs={{4,8},{8,4},{12,16},{16,12},{20,24},{24,20},{5,9},{9,5},{13,17},{1... | collective-permute-start | bytes 98312 | tf_op jit(solution)/shard_map/ppermute | solution.py:47
  27.8 4.5 %collective-permute-start.7 = (bf16[2,16,480]{2,1,0:T(8,128)(2,1)S(1)}, bf16[2,16,480]{2,1,0:T(8,128)(2,1)S(1)}, u32[]{:S(2)}, u32[]{:S(2)}) collective-permute-start(bf16[2,16,480]{2,1,0:T(8,128)(2,1)S(1)} %get-tuple-element.44), channel_id=1, source_target_pairs={{0,4},{4,0},{8,12},{12,8},{16,20},{20,16},{24,28},{28,24},{1,5},{5... | collective-permute-start | bytes 92168 | tf_op jit(solution)/shard_map/ppermute | solution.py:47
  33.0 1.2 %phase.1 = (f32[448,448]{1,0:T(8,128)S(1)}, f32[448,448]{1,0:T(8,128)S(1)}) custom-call(f32[1]{0:T(128)S(6)} %copy.19.freq_ref, f32[448,448]{1,0:T(8,128)S(1)} %copy-done.2, bf16[4,2,16,256]{3,2,1,0:T(8,128)(2,1)S(1)} %get-tuple-element.33._), custom_call_target="tpu_custom_call" | custom-call | flops 11000000 | bytes 36000 | tf_op jit(solution)/shard_map/phase/pallas_call | solution.py:764
  34.2 0.0 collective-permute-done.6.refs_4_
  34.2 1.4 %join.1.full_ref = f32[2,448,512]{2,1,0:T(8,128)S(1)} custom-call(s32[46]{0:T(128)S(1)} %get-tuple-element.28.refs_0_, f32[60]{0:T(128)S(1)} %get-tuple-element.29.refs_1_, f32[2,448,512]{2,1,0:T(8,128)S(1)} %get-tuple-element.40.refs_2_, f32[2,256,512]{2,1,0:T(8,128)S(1)} %get-tuple-element.41.refs_3_, ...), custom_call_target="tpu_custom_call", output_to_operand_aliasing={{}: (2, {})} | custom-call | flops 1100000 | bytes 3600 | tf_op jit(solution)/shard_map/join/pallas_call | solution.py:723
  35.7 0.0 collective-permute-done.7.rows_e_ref
  35.7 0.0 collective-permute-done.8.rows_o_ref
  35.7 0.3 border.1
  36.0 0.7 %collective-permute-start.10 = (bf16[2,16,448]{2,1,0:T(8,128)(2,1)S(1)}, bf16[2,16,448]{2,1,0:T(8,128)(2,1)S(1)}, u32[]{:S(2)}, u32[]{:S(2)}) collective-permute-start(bf16[2,16,448]{2,1,0:T(8,128)(2,1)S(1)} %get-tuple-element.50), channel_id=1, source_target_pairs={{1,2},{2,1},{5,6},{6,5},{9,10},{10,9},{13,14},{14,13},{17,18},{18,... | collective-permute-start | bytes 86024 | tf_op jit(solution)/shard_map/ppermute | solution.py:47
  36.6 3.2 %collective-permute-start.9 = (bf16[2,16,448]{2,1,0:T(8,128)(2,1)S(1)}, bf16[2,16,448]{2,1,0:T(8,128)(2,1)S(1)}, u32[]{:S(2)}, u32[]{:S(2)}) collective-permute-start(bf16[2,16,448]{2,1,0:T(8,128)(2,1)S(1)} %get-tuple-element.49), channel_id=1, source_target_pairs={{0,1},{1,0},{2,3},{3,2},{4,5},{5,4},{6,7},{7,6},{8,9},{9,8},{10,11... | collective-permute-start | bytes 86024 | tf_op jit(solution)/shard_map/ppermute | solution.py:47
  39.8 1.1 %inner.1._ = bf16[2,1,448,448]{3,2,1,0:T(8,128)(2,1)} custom-call(f32[2,448,512]{2,1,0:T(8,128)S(1)} %get-tuple-element.46.full_ref, f32[448,448]{1,0:T(8,128)S(1)} %get-tuple-element.47.cos_ref, f32[448,448]{1,0:T(8,128)S(1)} %get-tuple-element.48.sin_ref), custom_call_target="tpu_custom_call" | custom-call | flops 1100000000 | bytes 3600000 | tf_op jit(solution)/shard_map/inner/pallas_call | solution.py:855
  40.9 0.0 collective-permute-done.10.cols_o_ref
  40.9 0.0 collective-permute-done.9.cols_e_ref
  40.9 1.1 %outer.1 = bf16[2,1,448,448]{3,2,1,0:T(8,128)(2,1)} custom-call(bf16[2,1,448,448]{3,2,1,0:T(8,128)(2,1)} %inner.1._, f32[2,448,512]{2,1,0:T(8,128)S(1)} %get-tuple-element.46.full_ref, bf16[2,16,448]{2,1,0:T(8,128)(2,1)S(1)} %collective-permute-done.9.cols_e_ref, ...), custom_call_target="tpu_custom_call", output_to_operand_aliasing={{}: (0, {})} | custom-call | flops 1100000000 | bytes 3600000 | tf_op jit(solution)/shard_map/outer/pallas_call | solution.py:865
  (7 shorter events, 0.0 us)
Async XLA Ops:
  0.0 1.2 %copy-start = (bf16[2,1,448,448]{3,2,1,0:T(8,128)(2,1)S(1)}, bf16[2,1,448,448]{3,2,1,0:T(8,128)(2,1)}, u32[]{:S(2)}) copy-start(bf16[2,1,448,448]{3,2,1,0:T(8,128)(2,1)} %refs_2_.1) | copy-start | bytes 2408452
  1.2 3.2 %copy-start.3 = (bf16[3,1,2,256,256]{4,3,2,1,0:T(8,128)(2,1)S(1)}, bf16[3,1,2,256,256]{4,3,2,1,0:T(8,128)(2,1)}, u32[]{:S(2)}) copy-start(bf16[3,1,2,256,256]{4,3,2,1,0:T(8,128)(2,1)} %prop_ref.1) | copy-start | bytes 2359300
  1.2 3.2 %copy-start.4 = (bf16[256,256]{1,0:T(8,128)(2,1)S(1)}, bf16[256,256]{1,0:T(8,128)(2,1)}, u32[]{:S(2)}) copy-start(bf16[256,256]{1,0:T(8,128)(2,1)} %constant.6.clone.cos_ref) | copy-start | bytes 393220
  1.2 3.2 %copy-start.5 = (bf16[256,256]{1,0:T(8,128)(2,1)S(1)}, bf16[256,256]{1,0:T(8,128)(2,1)}, u32[]{:S(2)}) copy-start(bf16[256,256]{1,0:T(8,128)(2,1)} %constant.7.clone.cos_t_ref) | copy-start | bytes 393220
  1.2 3.2 %copy-start.6 = (f32[16,8,5,2]{0,3,2,1:T(2,128)S(1)}, f32[16,8,5,2]{0,3,2,1:T(2,128)}, u32[]{:S(2)}) copy-start(f32[16,8,5,2]{0,3,2,1:T(2,128)} %param.16) | copy-start | bytes 15364
  1.2 3.2 %copy-start.7 = (s32[16,8,5]{0,1,2:T(8,128)S(1)}, s32[16,8,5]{0,1,2:T(8,128)}, u32[]{:S(2)}) copy-start(s32[16,8,5]{0,1,2:T(8,128)} %param.15) | copy-start | bytes 7684
  1.2 3.2 %copy-start.8 = (s32[16,8]{0,1:T(8,128)S(1)}, s32[16,8]{0,1:T(8,128)}, u32[]{:S(2)}) copy-start(s32[16,8]{0,1:T(8,128)} %param.14) | copy-start | bytes 1540
  1.2 3.2 %copy-start.9 = (f32[1,256]{1,0:T(1,128)S(1)}, f32[1,256]{1,0:T(1,128)}, u32[]{:S(2)}) copy-start(f32[1,256]{1,0:T(1,128)} %constant.8.clone.row_ref) | copy-start | bytes 3076
  1.3 14.0 %collective-permute-start = (bf16[2,240,456]{2,1,0:T(8,128)(2,1)S(1)}, bf16[2,240,456]{2,1,0:T(8,128)(2,1)S(1)}, u32[]{:S(2)}, u32[]{:S(2)}) collective-permute-start(bf16[2,240,456]{2,1,0:T(8,128)(2,1)S(1)} %rows.1._), channel_id=1, source_target_pairs={{4,8},{8,4},{12,16},{16,12},{20,24},{24,20},{5,9},{9,5},{13,17},{1... | collective-permute-start | bytes 1313288 | tf_op jit(solution)/shard_map/ppermute | solution.py:47
  2.5 5.5 %collective-permute-start.1 = (bf16[2,448,240]{2,1,0:T(8,128)(2,1)S(1)}, bf16[2,448,240]{2,1,0:T(8,128)(2,1)S(1)}, u32[]{:S(2)}, u32[]{:S(2)}) collective-permute-start(bf16[2,448,240]{2,1,0:T(8,128)(2,1)S(1)} %get-tuple-element.30), channel_id=1, source_target_pairs={{0,1},{1,0},{2,3},{3,2},{4,5},{5,4},{6,7},{7,6},{8,9},{9,8},{10,11... | collective-permute-start | bytes 1290248 | tf_op jit(solution)/shard_map/ppermute | solution.py:47
  3.0 4.9 %collective-permute-start.2 = (bf16[2,448,240]{2,1,0:T(8,128)(2,1)S(1)}, bf16[2,448,240]{2,1,0:T(8,128)(2,1)S(1)}, u32[]{:S(2)}, u32[]{:S(2)}) collective-permute-start(bf16[2,448,240]{2,1,0:T(8,128)(2,1)S(1)} %get-tuple-element.31), channel_id=1, source_target_pairs={{1,2},{2,1},{5,6},{6,5},{9,10},{10,9},{13,14},{14,13},{17,18},{18,... | collective-permute-start | bytes 1290248 | tf_op jit(solution)/shard_map/ppermute | solution.py:47
  3.7 20.0 %collective-permute-start.5 = (bf16[2,240,240]{2,1,0:T(8,128)(2,1)S(1)}, bf16[2,240,240]{2,1,0:T(8,128)(2,1)S(1)}, u32[]{:S(2)}, u32[]{:S(2)}) collective-permute-start(bf16[2,240,240]{2,1,0:T(8,128)(2,1)S(1)} %get-tuple-element.34), channel_id=1, source_target_pairs={{5,10},{10,5},{6,9},{9,6},{13,18},{18,13},{14,17},{17,14},{21,26},... | collective-permute-start | bytes 691208 | tf_op jit(solution)/shard_map/ppermute | solution.py:58
  7.0 1.2 %copy-start.1 = (bf16[2,1,448,448]{3,2,1,0:T(8,128)(2,1)S(1)}, bf16[2,1,448,448]{3,2,1,0:T(8,128)(2,1)}, u32[]{:S(2)}) copy-start(bf16[2,1,448,448]{3,2,1,0:T(8,128)(2,1)} %refs_2_.1) | copy-start | bytes 2408452
  10.0 13.7 %collective-permute-start.3 = (bf16[4,2,16,256]{3,2,1,0:T(8,128)(2,1)S(1)}, bf16[4,2,16,256]{3,2,1,0:T(8,128)(2,1)S(1)}, u32[]{:S(2)}, u32[]{:S(2)}) collective-permute-start(bf16[4,2,16,256]{3,2,1,0:T(8,128)(2,1)S(1)} %get-tuple-element.33._), channel_id=1, source_target_pairs={{0,4},{4,0},{8,12},{12,8},{16,20},{20,16},{24,28},{28,24},{1,5},{5... | collective-permute-start | bytes 196616 | tf_op jit(solution)/shard_map/ppermute | solution.py:47
  15.3 19.0 %collective-permute-start.6 = (bf16[2,240,512]{2,1,0:T(8,128)(2,1)S(1)}, bf16[2,240,512]{2,1,0:T(8,128)(2,1)S(1)}, u32[]{:S(2)}, u32[]{:S(2)}) collective-permute-start(bf16[2,240,512]{2,1,0:T(8,128)(2,1)S(1)} %get-tuple-element.42), channel_id=1, source_target_pairs={{0,4},{4,0},{8,12},{12,8},{16,20},{20,16},{24,28},{28,24},{1,5},{5... | collective-permute-start | bytes 1474568 | tf_op jit(solution)/shard_map/ppermute | solution.py:47
  15.5 8.2 %collective-permute-start.4 = (bf16[2,240,240]{2,1,0:T(8,128)(2,1)S(1)}, bf16[2,240,240]{2,1,0:T(8,128)(2,1)S(1)}, u32[]{:S(2)}, u32[]{:S(2)}) collective-permute-start(bf16[2,240,240]{2,1,0:T(8,128)(2,1)S(1)} %corner.1), channel_id=1, source_target_pairs={{0,1},{1,0},{2,3},{3,2},{4,5},{5,4},{6,7},{7,6},{8,9},{9,8},{10,11... | collective-permute-start | bytes 691208 | tf_op jit(solution)/shard_map/ppermute | solution.py:47
  23.7 9.3 %copy-start.2 = (f32[448,448]{1,0:T(8,128)S(1)}, f32[448,448]{1,0:T(8,128)}, u32[]{:S(2)}) copy-start(f32[448,448]{1,0:T(8,128)} %slow_ref.1) | copy-start | bytes 2408452
  27.0 8.7 %collective-permute-start.8 = (bf16[2,16,512]{2,1,0:T(8,128)(2,1)S(1)}, bf16[2,16,512]{2,1,0:T(8,128)(2,1)S(1)}, u32[]{:S(2)}, u32[]{:S(2)}) collective-permute-start(bf16[2,16,512]{2,1,0:T(8,128)(2,1)S(1)} %get-tuple-element.45), channel_id=1, source_target_pairs={{4,8},{8,4},{12,16},{16,12},{20,24},{24,20},{5,9},{9,5},{13,17},{1... | collective-permute-start | bytes 98312 | tf_op jit(solution)/shard_map/ppermute | solution.py:47
  27.8 7.8 %collective-permute-start.7 = (bf16[2,16,480]{2,1,0:T(8,128)(2,1)S(1)}, bf16[2,16,480]{2,1,0:T(8,128)(2,1)S(1)}, u32[]{:S(2)}, u32[]{:S(2)}) collective-permute-start(bf16[2,16,480]{2,1,0:T(8,128)(2,1)S(1)} %get-tuple-element.44), channel_id=1, source_target_pairs={{0,4},{4,0},{8,12},{12,8},{16,20},{20,16},{24,28},{28,24},{1,5},{5... | collective-permute-start | bytes 92168 | tf_op jit(solution)/shard_map/ppermute | solution.py:47
  36.0 5.0 %collective-permute-start.10 = (bf16[2,16,448]{2,1,0:T(8,128)(2,1)S(1)}, bf16[2,16,448]{2,1,0:T(8,128)(2,1)S(1)}, u32[]{:S(2)}, u32[]{:S(2)}) collective-permute-start(bf16[2,16,448]{2,1,0:T(8,128)(2,1)S(1)} %get-tuple-element.50), channel_id=1, source_target_pairs={{1,2},{2,1},{5,6},{6,5},{9,10},{10,9},{13,14},{14,13},{17,18},{18,... | collective-permute-start | bytes 86024 | tf_op jit(solution)/shard_map/ppermute | solution.py:47
  36.6 4.3 %collective-permute-start.9 = (bf16[2,16,448]{2,1,0:T(8,128)(2,1)S(1)}, bf16[2,16,448]{2,1,0:T(8,128)(2,1)S(1)}, u32[]{:S(2)}, u32[]{:S(2)}) collective-permute-start(bf16[2,16,448]{2,1,0:T(8,128)(2,1)S(1)} %get-tuple-element.49), channel_id=1, source_target_pairs={{0,1},{1,0},{2,3},{3,2},{4,5},{5,4},{6,7},{7,6},{8,9},{9,8},{10,11... | collective-permute-start | bytes 86024 | tf_op jit(solution)/shard_map/ppermute | solution.py:47

commit v5 on v4

--- a/solution.py
+++ b/solution.py
@@ -353,13 +353,14 @@
     ye_ref,
     yo_ref,
     left_ref,
-    _,
+    right_ref,
     frame_ref,
     send_ref,
-    border_ref,
+    echo_ref,
     swept_ref,
     rim_ref,
     part_ref,
+    out_ref,
 ):
     length = left_ref.shape[-1]
     tile = wave_ref.shape[2]
@@ -388,21 +389,18 @@
             part_ref[1, rows, cols] = imag.astype(BF16)
 
         mix(None, terms, store)
+    groups = [lists.group_at(lists.window(beyond, col)) for col in range(2)]
+    turn(halves(part_ref, slice(None)), right_ref, groups, out_ref)
     span = length - HALF
     inner, outer = start_of(lists.odd_x, HALF, 0), start_of(lists.odd_x, 0, span)
     for part in range(2):
-        send_ref[part] = part_ref[part, pl.ds(inner, span)]
-        border_ref[part] = part_ref[part, pl.ds(outer, HALF)]
-
-
-def early_kernel(
-    lists, frame_ref, left_ref, gave_ref, right_ref, _, sum_ref, echo_ref, swept_ref
-):
+        send_ref[part] = out_ref[part, pl.ds(inner, span), : send_ref.shape[2]].astype(BF16)
+        echo_ref[part] = out_ref[part, pl.ds(outer, HALF)]
+
+
+def early_kernel(lists, frame_ref, left_ref, _, sum_ref, swept_ref):
     length = left_ref.shape[-1]
     lists.wait()
-    beyond = jnp.where(lists.odd_x == 0, 2, -1)
-    groups = [lists.group_at(lists.window(beyond, col)) for col in range(2)]
-    turn(halves(gave_ref, slice(None)), right_ref, groups, echo_ref)
     rows = pl.ds(window_rows(lists.odd_x, 1, length), length)
     for at in range(4):
         matrix_ref = left_ref.at[lists.group_at(lists.window(lists.odd_x, at - 1))]
@@ -456,7 +454,6 @@
     early_ref,
     right_ref,
     mid_ref,
-    rest_ref,
     send_o_ref,
     send_e_ref,
     strip_ref,
@@ -466,7 +463,8 @@
     mixed_ref,
     sum_ref,
     out_ref,
-    border_ref,
+    rest_ref,
+    even_ref,
 ):
     length = left_ref.shape[-1]
     span = length - HALF
@@ -525,14 +523,20 @@
     for col in range(2):
         stacked = strip_sums(lists, strip_ref, mixed_ref.at[2 + col], row, col)
         for part in range(2):
-            rest_ref[part, :, col * length : (col + 1) * length] = early_ref[1, col, part] + dot(
-                lean_ref[part], stacked
-            )
+            rest_ref[part, :, col * length : (col + 1) * length] = (
+                early_ref[1, col, part] + dot(lean_ref[part], stacked)
+            ).astype(BF16)
     groups = [lists.group_at(lists.window(row, col)) for col in range(2)]
-    rows = pl.ds(start_of(odd_x, span, 0), HALF)
-    turn(halves(rest_ref, rows), right_ref, groups, border_ref)
+    turn(halves(rest_ref, slice(None)), right_ref, groups, even_ref)
+    border = start_of(odd_x, span, 0)
+    alone = tile - span
+    both = slice(alone, span)
+    source, target = start_of(odd_x, span - alone, HALF), start_of(odd_x, span, 0)
+    shared = start_of(odd_x, 0, HALF + alone)
     for part in range(2):
-        send_e_ref[part] = border_ref[part, :, : send_e_ref.shape[2]].astype(BF16)
+        mid_ref[part, pl.ds(target, alone)] = even_ref[part, pl.ds(source, alone)]
+        mid_ref[part, both] += even_ref[part, pl.ds(shared, span - alone)]
+        send_e_ref[part] = even_ref[part, pl.ds(border, HALF), : send_e_ref.shape[2]].astype(BF16)
 
 
 def halves(ref, rows):
@@ -554,42 +558,21 @@
     out_ref[1] = imag
 
 
-def join_kernel(lists, mid_ref, rest_ref, got_ref, right_ref, full_ref, sum_ref, out_ref):
-    span = got_ref.shape[1]
+def join_kernel(
+    mid_ref, got_ref, echo_ref, rows_e_ref, rows_o_ref, full_ref, send_e_ref, send_o_ref
+):
+    span, width = got_ref.shape[1:]
     tile = full_ref.shape[1]
-    odd_x = lists.odd_x
-    rows = pl.ds(start_of(odd_x, 0, HALF), span)
-    for part in range(2):
-        sum_ref[part] = (rest_ref[part, rows] + got_ref[part].astype(F32)).astype(BF16)
-    lists.wait()
-    groups = [lists.group_at(lists.window(1 - odd_x, col)) for col in range(2)]
-    turn(halves(sum_ref, slice(None)), right_ref, groups, out_ref)
-    alone = tile - span
-    both = slice(alone, span)
-    source, target = start_of(odd_x, span - alone, 0), start_of(odd_x, span, 0)
-    shared = start_of(odd_x, 0, alone)
-    for part in range(2):
-        full_ref[part, pl.ds(target, alone)] = out_ref[part, pl.ds(source, alone)]
-        full_ref[part, both] = (
-            mid_ref[part, both] + out_ref[part, pl.ds(shared, span - alone)]
-        )
-
-
-def border_kernel(full_ref, echo_ref, rows_e_ref, rows_o_ref, done_ref, send_e_ref, send_o_ref):
-    tile = done_ref.shape[1]
-    lanes = tile // 128 * 128
     odd_x = parity("gx")
+    rows = pl.ds(start_of(odd_x, tile - span, 0), span)
     row_e = pl.ds(start_of(odd_x, tile - HALF, 0), HALF)
     row_o = pl.ds(start_of(odd_x, 0, tile - HALF), HALF)
-    width = rows_e_ref.shape[2]
+    lanes = tile // 128 * 128
     for part in range(2):
-        done_ref[part, row_o] = full_ref[part, row_o] + rows_o_ref[part].astype(F32)
-        done_ref[part, row_e, :width] = (
-            full_ref[part, row_e, :width]
-            + echo_ref[part, :, :width]
-            + rows_e_ref[part].astype(F32)
-        )
-        turned = done_ref[part, :, lanes:].T
+        full_ref[part, rows, :width] = mid_ref[part, rows, :width] + got_ref[part].astype(F32)
+        full_ref[part, row_o] = mid_ref[part, row_o] + rows_o_ref[part].astype(F32)
+        full_ref[part, row_e, :width] += echo_ref[part, :, :width] + rows_e_ref[part].astype(F32)
+        turned = full_ref[part, :, lanes:].T
         west = turned[tile - lanes : tile - lanes + HALF].astype(BF16)
         east = turned[tile - lanes + HALF : tile - lanes + OVER].astype(BF16)
 
@@ -743,20 +726,19 @@
         cost_estimate=cost(0.01),
         name="right",
     )(left)
-    frame, given, gave, swept, rim_send = call(
+    frame, given, echo, swept, rim_send = call(
         edge_kernel,
         "edge",
         0.001,
         (
             shape(4, 2, tile_rows + OVER, length),
-            shape(2, span, wide),
-            shape(2, HALF, wide),
+            shape(2, span, tile_cols + OVER),
+            shape(2, HALF, wide, kind=F32),
             shape(2, 4, 2, length, length, kind=F32),
             shape(4, 2, HALF, length),
         ),
         (wavefield, y_near, y_far, left, right),
-        (pltpu.VMEM((2, length, wide), BF16),),
-        in_specs=[VMEM] * 4 + [ANY],
+        (pltpu.VMEM((2, length, wide), BF16), pltpu.VMEM((2, length, wide), F32)),
     )
     rim = swap(rim_send, "gx", False)
     got = swap(given, "gx", False)
@@ -781,25 +763,23 @@
         name="corner",
     )(x_odd, rim_send)
     z_near = swap(corner_near, "gy", False)
-    early, echo, _ = call(
+    early, _ = call(
         early_kernel,
         "early",
         3,
         (
             shape(2, 2, 2, length, length, kind=F32),
-            shape(2, HALF, wide, kind=F32),
             shape(2, 4, 2, length, length, kind=F32),
         ),
-        (frame, left, gave, right, swept),
-        input_output_aliases={6: 2},
-    )
-    mid, rest, send_o, send_e = call(
+        (frame, left, swept),
+        input_output_aliases={4: 1},
+    )
+    mid, send_o, send_e = call(
         late_kernel,
         "late",
         4,
         (
             shape(2, tile_rows, wide, kind=F32),
-            shape(2, length, wide, kind=F32),
             shape(2, HALF, wide),
             shape(2, HALF, tile_cols + OVER),
         ),
@@ -812,33 +792,26 @@
             pltpu.VMEM((4, length, length), F32),
             pltpu.VMEM((2, length, wide), BF16),
             pltpu.VMEM((2, length, wide), F32),
-            pltpu.VMEM((2, HALF, wide), F32),
+            pltpu.VMEM((2, length, wide), BF16),
+            pltpu.VMEM((2, length, wide), F32),
         ),
     )
     rows_o = swap(send_o, "gx", True)
     rows_e = swap(send_e, "gx", False)
-    full = call(
+    full, send_e, send_o = pl.pallas_call(
         join_kernel,
-        "join",
-        0.001,
-        shape(2, tile_rows, wide, kind=F32),
-        (mid, rest, got, right),
-        (
-            pltpu.VMEM((2, span, wide), BF16),
-            pltpu.VMEM((2, span, wide), F32),
+        out_shape=(
+            shape(2, tile_rows, wide, kind=F32),
+            shape(2, HALF, tile_rows),
+            shape(2, HALF, tile_rows),
         ),
-        input_output_aliases={2: 0},
-    )
-    full, send_e, send_o = pl.pallas_call(
-        border_kernel,
-        out_shape=(shape(2, tile_rows, wide, kind=F32),) + (shape(2, HALF, tile_rows),) * 2,
-        in_specs=[VMEM] * 4,
+        in_specs=[VMEM] * 5,
         out_specs=(VMEM,) * 3,
         input_output_aliases={0: 0},
         compiler_params=PARAMS,
-        cost_estimate=cost(0.5),
-        name="border",
-    )(full, echo, rows_e, rows_o)
+        cost_estimate=cost(0.001),
+        name="join",
+    )(mid, got, echo, rows_e, rows_o)
     cols_o = swap(send_o, "gy", True)
     cols_e = swap(send_e, "gy", False)
     result = jax.ShapeDtypeStruct(wavefield.shape, BF16)

time: 42.5 us -> 42.3 us (level)
  the two profiles are of different devices: /device:TPU:0 before, /device:TPU:9 now
where the time goes in v5:
time: 42.3 us; the launch traced here: 41.5 us
  starting transfers between devices  21.5 us (51%)
  Pallas kernels  17 us (40%)
  local copies, waits for them, and re-layouts  1.47 us (3%)
  between operations  1.12 us (3%)
    ppermute x10, starting transfers between devices, swap(): return lax.ppermute(block, axis, pairs)  18 us
    pallas_call x3, Pallas kernels, call(): pl.pallas_call(body, out_shape=out_shape, in_specs=[ANY] * 2 + specs, out...  9.3 us
    ppermute x1, starting transfers between devices, far_corner(): return lax.ppermute(block, ('gx', 'gy'), pairs)  3.49 us
    pallas_call x1, Pallas kernels, fold(): pl.pallas_call(folded_kernel, out_shape=(pltpu.VMEM((groups, 2, length, l...  2.57 us
    unnamed x20, local copies, waits for them, and re-layouts  1.47 us
    pallas_call x1, Pallas kernels, per_device(): pl.pallas_call(phase_kernel, out_shape=(shape(tile_rows, tile_cols, kind=...  1.21 us
    pallas_call x1, Pallas kernels, per_device(): pl.pallas_call(outer_kernel, out_shape=result, in_specs=[ANY] + [VMEM] *...  1.12 us
    pallas_call x1, Pallas kernels, per_device(): pl.pallas_call(inner_kernel, grid=(count - 2,), out_shape=result, in_spec...  1.12 us
  transfers between devices with their start and end apart: 11, of which 1 were waited for; matrix products, arithmetic and copies ran while one was open for 0% of the time, Pallas kernels for 37%

profile of v5, /device:TPU:9, one launch (start us, length us, event | category | flops | bytes accessed | tf_op | source)
XLA Modules:
  0.0 41.5 jit_solution(2432024932158617661)
XLA Ops:
  0.0 1.2 %copy-done = bf16[2,1,448,448]{3,2,1,0:T(8,128)(2,1)S(1)} copy-done((bf16[2,1,448,448]{3,2,1,0:T(8,128)(2,1)S(1)}, bf16[2,1,448,448]{3,2,1,0:T(8,128)(2,1)}, u32[]{:S(2)}) %copy-start) | copy-done | bytes 802840
  1.2 0.0 copy-start.7
  1.2 0.0 copy-start.8
  1.2 0.0 copy-start.9
  1.2 0.1 rows.1._
  1.3 3.2 %collective-permute-start = (bf16[2,240,456]{2,1,0:T(8,128)(2,1)S(1)}, bf16[2,240,456]{2,1,0:T(8,128)(2,1)S(1)}, u32[]{:S(2)}, u32[]{:S(2)}) collective-permute-start(bf16[2,240,456]{2,1,0:T(8,128)(2,1)S(1)} %rows.1._), channel_id=1, source_target_pairs={{4,8},{8,4},{12,16},{16,12},{20,24},{24,20},{5,9},{9,5},{13,17},{1... | collective-permute-start | bytes 1313288 | tf_op jit(solution)/shard_map/ppermute | solution.py:47
  4.5 0.3 cols.1
  4.8 1.0 %collective-permute-start.1 = (bf16[2,448,240]{2,1,0:T(8,128)(2,1)S(1)}, bf16[2,448,240]{2,1,0:T(8,128)(2,1)S(1)}, u32[]{:S(2)}, u32[]{:S(2)}) collective-permute-start(bf16[2,448,240]{2,1,0:T(8,128)(2,1)S(1)} %get-tuple-element.28), channel_id=1, source_target_pairs={{0,1},{1,0},{2,3},{3,2},{4,5},{5,4},{6,7},{7,6},{8,9},{9,8},{10,11... | collective-permute-start | bytes 1290248 | tf_op jit(solution)/shard_map/ppermute | solution.py:47
  5.8 3.0 %collective-permute-start.2 = (bf16[2,448,240]{2,1,0:T(8,128)(2,1)S(1)}, bf16[2,448,240]{2,1,0:T(8,128)(2,1)S(1)}, u32[]{:S(2)}, u32[]{:S(2)}) collective-permute-start(bf16[2,448,240]{2,1,0:T(8,128)(2,1)S(1)} %get-tuple-element.29), channel_id=1, source_target_pairs={{1,2},{2,1},{5,6},{6,5},{9,10},{10,9},{13,14},{14,13},{17,18},{18,... | collective-permute-start | bytes 1290248 | tf_op jit(solution)/shard_map/ppermute | solution.py:47
  8.9 3.5 %collective-permute-start.5 = (bf16[2,240,240]{2,1,0:T(8,128)(2,1)S(1)}, bf16[2,240,240]{2,1,0:T(8,128)(2,1)S(1)}, u32[]{:S(2)}, u32[]{:S(2)}) collective-permute-start(bf16[2,240,240]{2,1,0:T(8,128)(2,1)S(1)} %get-tuple-element.32), channel_id=1, source_target_pairs={{5,10},{10,5},{6,9},{9,6},{13,18},{18,13},{14,17},{17,14},{21,26},... | collective-permute-start | bytes 691208 | tf_op jit(solution)/shard_map/ppermute | solution.py:58
  12.4 0.0 copy-done.3
  12.4 0.0 copy-done.4
  12.4 0.0 copy-done.5
  12.4 0.0 copy-done.6
  12.4 0.0 copy-done.7
  12.4 0.0 copy-done.8
  12.4 0.0 copy-done.9
  12.4 2.6 %fold.1 = (bf16[3,2,256,256]{3,2,1,0:T(8,128)(2,1)S(1)}, bf16[2,256,256]{2,1,0:T(8,128)(2,1)S(1)}, s32[46]{0:T(128)S(1)}, f32[60]{0:T(128)S(1)}) custom-call(s32[5,8,16]{2,1,0:T(8,128)S(1)} %bitcast.4, f32[8,5,2,16]{3,2,1,0:T(2,128)S(1)} %bitcast.3, s32[8,16]{1,0:T(8,128)S(1)} %bitcast.5, bf16[3,1,2,256,256]{4,3,2,1,0:T(8,128)(2,1)S(1)} %copy-done.3, ...), custom_call_target="tpu_custom_call" | custom-call | flops 110000000 | bytes 360000 | tf_op jit(solution)/shard_map/fold/pallas_call | solution.py:184
  15.0 0.0 copy-start.1
  15.0 0.9 %right.1.refs_6_.refs_10_ = bf16[3,2,2,256,512]{4,3,2,1,0:T(8,128)(2,1)S(1)} custom-call(bf16[3,2,256,256]{3,2,1,0:T(8,128)(2,1)S(1)} %get-tuple-element.30.left_ref.refs_5_.refs_3_.refs_6_), custom_call_target="tpu_custom_call" | custom-call | flops 11000000 | bytes 36000 | tf_op jit(solution)/shard_map/right/pallas_call | solution.py:720
  15.9 0.0 collective-permute-done.1.refs_3_
  15.9 0.0 collective-permute-done.2.refs_4_
  15.9 0.2 copy-done.1
  16.2 2.7 %edge.1 = (bf16[4,2,480,256]{3,2,1,0:T(8,128)(2,1)S(1)}, bf16[2,240,480]{2,1,0:T(8,128)(2,1)S(1)}, f32[2,16,512]{2,1,0:T(8,128)S(1)}, f32[2,4,2,256,256]{4,3,2,1,0:T(8,128)S(1)}, bf16[4,2,16,256]{3,2,1,0:T(8,128)(2,1)S(1)}) custom-call(s32[46]{0:T(128)S(1)} %get-tuple-element.26.refs_0_, f32[60]{0:T(128)S(1)} %get-tuple-element.27.refs_1_, ...), custom_call_target="tpu_custom_call" | custom-call | flops 1100000 | bytes 3600 | tf_op jit(solution)/shard_map/edge/pallas_call | solution.py:706
  18.9 1.2 %collective-permute-start.3 = (bf16[4,2,16,256]{3,2,1,0:T(8,128)(2,1)S(1)}, bf16[4,2,16,256]{3,2,1,0:T(8,128)(2,1)S(1)}, u32[]{:S(2)}, u32[]{:S(2)}) collective-permute-start(bf16[4,2,16,256]{3,2,1,0:T(8,128)(2,1)S(1)} %get-tuple-element.31._), channel_id=1, source_target_pairs={{0,4},{4,0},{8,12},{12,8},{16,20},{20,16},{24,28},{28,24},{1,5},{5... | collective-permute-start | bytes 196616 | tf_op jit(solution)/shard_map/ppermute | solution.py:47
  20.1 0.3 collective-permute-start.6
  20.4 0.0 collective-permute-done.x_ref.refs_2_
  20.4 0.1 collective-permute-start.4
  20.5 2.7 %early.1 = (f32[2,2,2,256,256]{4,3,2,1,0:T(8,128)S(1)}, f32[2,4,2,256,256]{4,3,2,1,0:T(8,128)S(1)}) custom-call(s32[46]{0:T(128)S(1)} %get-tuple-element.26.refs_0_, f32[60]{0:T(128)S(1)} %get-tuple-element.27.refs_1_, bf16[4,2,480,256]{3,2,1,0:T(8,128)(2,1)S(1)} %get-tuple-element.34.refs_2_.refs_8_, ...), custom_call_target="tpu_custom_call", output_to_operand_aliasing={{1}: (4, {})} | custom-call | flops 3300000000 | bytes 10800000 | tf_op jit(solution)/shard_map/early/pallas_call | solution.py:706
  23.2 0.0 collective-permute-done.5.refs_5_
  23.2 0.0 collective-permute-done.3.refs_3_
  23.3 0.0 collective-permute-done.4.refs_4_
  23.3 0.0 copy-start.2
  23.3 3.9 %late.1 = (f32[2,448,512]{2,1,0:T(8,128)S(1)}, bf16[2,16,512]{2,1,0:T(8,128)(2,1)S(1)}, bf16[2,16,480]{2,1,0:T(8,128)(2,1)S(1)}) custom-call(s32[46]{0:T(128)S(1)} %get-tuple-element.26.refs_0_, f32[60]{0:T(128)S(1)} %get-tuple-element.27.refs_1_, bf16[2,240,456]{2,1,0:T(8,128)(2,1)S(1)} %collective-permute-done.x_ref.refs_2_, ...), custom_call_target="tpu_custom_call" | custom-call | flops 4400000000 | bytes 14400000 | tf_op jit(solution)/shard_map/late/pallas_call | solution.py:706
  27.2 3.0 %collective-permute-start.8 = (bf16[2,16,512]{2,1,0:T(8,128)(2,1)S(1)}, bf16[2,16,512]{2,1,0:T(8,128)(2,1)S(1)}, u32[]{:S(2)}, u32[]{:S(2)}) collective-permute-start(bf16[2,16,512]{2,1,0:T(8,128)(2,1)S(1)} %get-tuple-element.41), channel_id=1, source_target_pairs={{4,8},{8,4},{12,16},{16,12},{20,24},{24,20},{5,9},{9,5},{13,17},{1... | collective-permute-start | bytes 98312 | tf_op jit(solution)/shard_map/ppermute | solution.py:47
  30.2 1.5 %collective-permute-start.7 = (bf16[2,16,480]{2,1,0:T(8,128)(2,1)S(1)}, bf16[2,16,480]{2,1,0:T(8,128)(2,1)S(1)}, u32[]{:S(2)}, u32[]{:S(2)}) collective-permute-start(bf16[2,16,480]{2,1,0:T(8,128)(2,1)S(1)} %get-tuple-element.40), channel_id=1, source_target_pairs={{0,4},{4,0},{8,12},{12,8},{16,20},{20,16},{24,28},{28,24},{1,5},{5... | collective-permute-start | bytes 92168 | tf_op jit(solution)/shard_map/ppermute | solution.py:47
  32.3 0.0 copy-done.2
  32.3 1.2 %phase.1 = (f32[448,448]{1,0:T(8,128)S(1)}, f32[448,448]{1,0:T(8,128)S(1)}) custom-call(f32[1]{0:T(128)S(6)} %copy.17.freq_ref, f32[448,448]{1,0:T(8,128)S(1)} %copy-done.2, bf16[4,2,16,256]{3,2,1,0:T(8,128)(2,1)S(1)} %get-tuple-element.31._), custom_call_target="tpu_custom_call" | custom-call | flops 11000000 | bytes 36000 | tf_op jit(solution)/shard_map/phase/pallas_call | solution.py:746
  33.5 0.0 collective-permute-done.7.rows_e_ref
  33.6 0.0 collective-permute-done.8.rows_o_ref
  33.6 0.0 collective-permute-done.6.got_ref
  33.6 0.4 join.1
  34.0 4.7 %collective-permute-start.10 = (bf16[2,16,448]{2,1,0:T(8,128)(2,1)S(1)}, bf16[2,16,448]{2,1,0:T(8,128)(2,1)S(1)}, u32[]{:S(2)}, u32[]{:S(2)}) collective-permute-start(bf16[2,16,448]{2,1,0:T(8,128)(2,1)S(1)} %get-tuple-element.46), channel_id=1, source_target_pairs={{1,2},{2,1},{5,6},{6,5},{9,10},{10,9},{13,14},{14,13},{17,18},{18,... | collective-permute-start | bytes 86024 | tf_op jit(solution)/shard_map/ppermute | solution.py:47
  38.7 0.1 collective-permute-start.9
  38.7 1.1 %inner.1._ = bf16[2,1,448,448]{3,2,1,0:T(8,128)(2,1)} custom-call(f32[2,448,512]{2,1,0:T(8,128)S(1)} %get-tuple-element.42.full_ref, f32[448,448]{1,0:T(8,128)S(1)} %get-tuple-element.43.cos_ref, f32[448,448]{1,0:T(8,128)S(1)} %get-tuple-element.44.sin_ref), custom_call_target="tpu_custom_call" | custom-call | flops 1100000000 | bytes 3600000 | tf_op jit(solution)/shard_map/inner/pallas_call | solution.py:828
  39.9 0.4 collective-permute-done.10.cols_o_ref
  40.2 0.0 collective-permute-done.9.cols_e_ref
  40.2 1.1 %outer.1 = bf16[2,1,448,448]{3,2,1,0:T(8,128)(2,1)} custom-call(bf16[2,1,448,448]{3,2,1,0:T(8,128)(2,1)} %inner.1._, f32[2,448,512]{2,1,0:T(8,128)S(1)} %get-tuple-element.42.full_ref, bf16[2,16,448]{2,1,0:T(8,128)(2,1)S(1)} %collective-permute-done.9.cols_e_ref, ...), custom_call_target="tpu_custom_call", output_to_operand_aliasing={{}: (0, {})} | custom-call | flops 1100000000 | bytes 3600000 | tf_op jit(solution)/shard_map/outer/pallas_call | solution.py:838
  (6 shorter events, 0.0 us)
Async XLA Ops:
  0.0 1.2 %copy-start = (bf16[2,1,448,448]{3,2,1,0:T(8,128)(2,1)S(1)}, bf16[2,1,448,448]{3,2,1,0:T(8,128)(2,1)}, u32[]{:S(2)}) copy-start(bf16[2,1,448,448]{3,2,1,0:T(8,128)(2,1)} %refs_2_.1) | copy-start | bytes 2408452
  1.2 11.2 %copy-start.3 = (bf16[3,1,2,256,256]{4,3,2,1,0:T(8,128)(2,1)S(1)}, bf16[3,1,2,256,256]{4,3,2,1,0:T(8,128)(2,1)}, u32[]{:S(2)}) copy-start(bf16[3,1,2,256,256]{4,3,2,1,0:T(8,128)(2,1)} %prop_ref.1) | copy-start | bytes 2359300
  1.2 11.2 %copy-start.4 = (bf16[256,256]{1,0:T(8,128)(2,1)S(1)}, bf16[256,256]{1,0:T(8,128)(2,1)}, u32[]{:S(2)}) copy-start(bf16[256,256]{1,0:T(8,128)(2,1)} %constant.6.clone.cos_ref) | copy-start | bytes 393220
  1.2 11.2 %copy-start.5 = (bf16[256,256]{1,0:T(8,128)(2,1)S(1)}, bf16[256,256]{1,0:T(8,128)(2,1)}, u32[]{:S(2)}) copy-start(bf16[256,256]{1,0:T(8,128)(2,1)} %constant.7.clone.cos_t_ref) | copy-start | bytes 393220
  1.2 11.2 %copy-start.6 = (f32[16,8,5,2]{0,3,2,1:T(2,128)S(1)}, f32[16,8,5,2]{0,3,2,1:T(2,128)}, u32[]{:S(2)}) copy-start(f32[16,8,5,2]{0,3,2,1:T(2,128)} %param.16) | copy-start | bytes 15364
  1.2 11.2 %copy-start.7 = (s32[16,8,5]{0,1,2:T(8,128)S(1)}, s32[16,8,5]{0,1,2:T(8,128)}, u32[]{:S(2)}) copy-start(s32[16,8,5]{0,1,2:T(8,128)} %param.15) | copy-start | bytes 7684
  1.2 11.2 %copy-start.8 = (s32[16,8]{0,1:T(8,128)S(1)}, s32[16,8]{0,1:T(8,128)}, u32[]{:S(2)}) copy-start(s32[16,8]{0,1:T(8,128)} %param.14) | copy-start | bytes 1540
  1.2 11.2 %copy-start.9 = (f32[1,256]{1,0:T(1,128)S(1)}, f32[1,256]{1,0:T(1,128)}, u32[]{:S(2)}) copy-start(f32[1,256]{1,0:T(1,128)} %constant.8.clone.row_ref) | copy-start | bytes 3076
  1.3 19.1 %collective-permute-start = (bf16[2,240,456]{2,1,0:T(8,128)(2,1)S(1)}, bf16[2,240,456]{2,1,0:T(8,128)(2,1)S(1)}, u32[]{:S(2)}, u32[]{:S(2)}) collective-permute-start(bf16[2,240,456]{2,1,0:T(8,128)(2,1)S(1)} %rows.1._), channel_id=1, source_target_pairs={{4,8},{8,4},{12,16},{16,12},{20,24},{24,20},{5,9},{9,5},{13,17},{1... | collective-permute-start | bytes 1313288 | tf_op jit(solution)/shard_map/ppermute | solution.py:47
  4.8 11.1 %collective-permute-start.1 = (bf16[2,448,240]{2,1,0:T(8,128)(2,1)S(1)}, bf16[2,448,240]{2,1,0:T(8,128)(2,1)S(1)}, u32[]{:S(2)}, u32[]{:S(2)}) collective-permute-start(bf16[2,448,240]{2,1,0:T(8,128)(2,1)S(1)} %get-tuple-element.28), channel_id=1, source_target_pairs={{0,1},{1,0},{2,3},{3,2},{4,5},{5,4},{6,7},{7,6},{8,9},{9,8},{10,11... | collective-permute-start | bytes 1290248 | tf_op jit(solution)/shard_map/ppermute | solution.py:47
  5.8 10.1 %collective-permute-start.2 = (bf16[2,448,240]{2,1,0:T(8,128)(2,1)S(1)}, bf16[2,448,240]{2,1,0:T(8,128)(2,1)S(1)}, u32[]{:S(2)}, u32[]{:S(2)}) collective-permute-start(bf16[2,448,240]{2,1,0:T(8,128)(2,1)S(1)} %get-tuple-element.29), channel_id=1, source_target_pairs={{1,2},{2,1},{5,6},{6,5},{9,10},{10,9},{13,14},{14,13},{17,18},{18,... | collective-permute-start | bytes 1290248 | tf_op jit(solution)/shard_map/ppermute | solution.py:47
  8.9 14.4 %collective-permute-start.5 = (bf16[2,240,240]{2,1,0:T(8,128)(2,1)S(1)}, bf16[2,240,240]{2,1,0:T(8,128)(2,1)S(1)}, u32[]{:S(2)}, u32[]{:S(2)}) collective-permute-start(bf16[2,240,240]{2,1,0:T(8,128)(2,1)S(1)} %get-tuple-element.32), channel_id=1, source_target_pairs={{5,10},{10,5},{6,9},{9,6},{13,18},{18,13},{14,17},{17,14},{21,26},... | collective-permute-start | bytes 691208 | tf_op jit(solution)/shard_map/ppermute | solution.py:58
  15.0 1.2 %copy-start.1 = (bf16[2,1,448,448]{3,2,1,0:T(8,128)(2,1)S(1)}, bf16[2,1,448,448]{3,2,1,0:T(8,128)(2,1)}, u32[]{:S(2)}) copy-start(bf16[2,1,448,448]{3,2,1,0:T(8,128)(2,1)} %refs_2_.1) | copy-start | bytes 2408452
  18.9 4.4 %collective-permute-start.3 = (bf16[4,2,16,256]{3,2,1,0:T(8,128)(2,1)S(1)}, bf16[4,2,16,256]{3,2,1,0:T(8,128)(2,1)S(1)}, u32[]{:S(2)}, u32[]{:S(2)}) collective-permute-start(bf16[4,2,16,256]{3,2,1,0:T(8,128)(2,1)S(1)} %get-tuple-element.31._), channel_id=1, source_target_pairs={{0,4},{4,0},{8,12},{12,8},{16,20},{20,16},{24,28},{28,24},{1,5},{5... | collective-permute-start | bytes 196616 | tf_op jit(solution)/shard_map/ppermute | solution.py:47
  20.1 13.5 %collective-permute-start.6 = (bf16[2,240,480]{2,1,0:T(8,128)(2,1)S(1)}, bf16[2,240,480]{2,1,0:T(8,128)(2,1)S(1)}, u32[]{:S(2)}, u32[]{:S(2)}) collective-permute-start(bf16[2,240,480]{2,1,0:T(8,128)(2,1)S(1)} %get-tuple-element.38), channel_id=1, source_target_pairs={{0,4},{4,0},{8,12},{12,8},{16,20},{20,16},{24,28},{28,24},{1,5},{5... | collective-permute-start | bytes 1382408 | tf_op jit(solution)/shard_map/ppermute | solution.py:47
  20.4 2.8 %collective-permute-start.4 = (bf16[2,240,240]{2,1,0:T(8,128)(2,1)S(1)}, bf16[2,240,240]{2,1,0:T(8,128)(2,1)S(1)}, u32[]{:S(2)}, u32[]{:S(2)}) collective-permute-start(bf16[2,240,240]{2,1,0:T(8,128)(2,1)S(1)} %corner.1), channel_id=1, source_target_pairs={{0,1},{1,0},{2,3},{3,2},{4,5},{5,4},{6,7},{7,6},{8,9},{9,8},{10,11... | collective-permute-start | bytes 691208 | tf_op jit(solution)/shard_map/ppermute | solution.py:47
  23.3 9.0 %copy-start.2 = (f32[448,448]{1,0:T(8,128)S(1)}, f32[448,448]{1,0:T(8,128)}, u32[]{:S(2)}) copy-start(f32[448,448]{1,0:T(8,128)} %slow_ref.1) | copy-start | bytes 2408452
  27.2 6.4 %collective-permute-start.8 = (bf16[2,16,512]{2,1,0:T(8,128)(2,1)S(1)}, bf16[2,16,512]{2,1,0:T(8,128)(2,1)S(1)}, u32[]{:S(2)}, u32[]{:S(2)}) collective-permute-start(bf16[2,16,512]{2,1,0:T(8,128)(2,1)S(1)} %get-tuple-element.41), channel_id=1, source_target_pairs={{4,8},{8,4},{12,16},{16,12},{20,24},{24,20},{5,9},{9,5},{13,17},{1... | collective-permute-start | bytes 98312 | tf_op jit(solution)/shard_map/ppermute | solution.py:47
  30.2 3.4 %collective-permute-start.7 = (bf16[2,16,480]{2,1,0:T(8,128)(2,1)S(1)}, bf16[2,16,480]{2,1,0:T(8,128)(2,1)S(1)}, u32[]{:S(2)}, u32[]{:S(2)}) collective-permute-start(bf16[2,16,480]{2,1,0:T(8,128)(2,1)S(1)} %get-tuple-element.40), channel_id=1, source_target_pairs={{0,4},{4,0},{8,12},{12,8},{16,20},{20,16},{24,28},{28,24},{1,5},{5... | collective-permute-start | bytes 92168 | tf_op jit(solution)/shard_map/ppermute | solution.py:47
  34.0 6.3 %collective-permute-start.10 = (bf16[2,16,448]{2,1,0:T(8,128)(2,1)S(1)}, bf16[2,16,448]{2,1,0:T(8,128)(2,1)S(1)}, u32[]{:S(2)}, u32[]{:S(2)}) collective-permute-start(bf16[2,16,448]{2,1,0:T(8,128)(2,1)S(1)} %get-tuple-element.46), channel_id=1, source_target_pairs={{1,2},{2,1},{5,6},{6,5},{9,10},{10,9},{13,14},{14,13},{17,18},{18,... | collective-permute-start | bytes 86024 | tf_op jit(solution)/shard_map/ppermute | solution.py:47
  38.7 1.6 %collective-permute-start.9 = (bf16[2,16,448]{2,1,0:T(8,128)(2,1)S(1)}, bf16[2,16,448]{2,1,0:T(8,128)(2,1)S(1)}, u32[]{:S(2)}, u32[]{:S(2)}) collective-permute-start(bf16[2,16,448]{2,1,0:T(8,128)(2,1)S(1)} %get-tuple-element.45), channel_id=1, source_target_pairs={{0,1},{1,0},{2,3},{3,2},{4,5},{5,4},{6,7},{7,6},{8,9},{9,8},{10,11... | collective-permute-start | bytes 86024 | tf_op jit(solution)/shard_map/ppermute | solution.py:47
